TPU v7x, 32 devices: a whole 2x2x4 slice. The times are simulated.
32 devices in a mesh: gx: 8 (over z, core), gy: 4 (over y, x).
Axes of the slice: x: 2, y: 2, z: 4, core: 2. Of those that a mesh axis runs over, the one named last changes fastest.
Arguments:
- forcing: float32 [9, 1024, 1024], P(None, 'gx', 'gy')
- start_potential: float32 [9, 1024, 1024], P(None, 'gx', 'gy'), may hold values from -3 to 3
- horiz_coef: float32 [1024, 1024], P('gx', 'gy'), may hold values from 0.5 to 2
- vert_coef: float32 [1024, 1024], P('gx', 'gy'), may hold values from 0.5 to 8
- vert_mix: float32 [9, 9], replicated, may hold values from -1.5 to 1.5
- mode_shapes: float32 [6, 1024, 1024], P(None, 'gx', 'gy'), may hold values from -6 to 6
- block_body: int32 [1024, 8], P('gx', 'gy'), may hold values from 0 to 127
- response: float32 [6, 6, 64], P(None, None, ('gx', 'gy')), may hold values from -2.5 to 2.5
- velocity_old: float32 [6, 64], P(None, ('gx', 'gy')), may hold values from -6 to 6
Outputs:
- potential: float32 [9, 1024, 1024], P(None, 'gx', 'gy')
- velocity: float32 [6, 64], P(None, ('gx', 'gy'))
- normal_flux: float32 [1024, 1024], P('gx', 'gy')
Inputs may be any that keep to these rules, and one draw needn't show every extreme that they name: `block_body`: values of 64 or more mark blocks outside every footprint.
All inputs are finite; a program needn't handle non-finite values.
Results may differ from a plain program's by a relative error of at most 0.00023.
Values sent between devices are 32-bit elements; how exact they have to be, the bound alone decides.
No kernel may reach another device: no remote copies, remote signals or barrier semaphores. Data moves between devices by JAX's collectives and lax.ppermute only.
A program may use at most 64 MiB of HBM per device.

v0:
```python
import math

import jax
import jax.numpy as jnp
from jax import lax
from jax.sharding import PartitionSpec as P

BLOCK = 128
FOOT = 8192


def extended(value, sides, width):
    for axis, dim in sides:
        size, length = (lax.axis_size(axis), value.shape[dim])
        up = [(i, (i + 1) % size) for i in range(size - 1)]
        down = [(j, i) for i, j in up]
        last = lax.slice_in_dim(value, length - width, length, axis=dim)
        leading = lax.slice_in_dim(value, 0, width, axis=dim)
        before = lax.ppermute(last, axis, up)
        after = lax.ppermute(leading, axis, down)
        value = jnp.concatenate([before, value, after], axis=dim)
    return value


def horizontal(padded):
    central = padded[:, 2:-2, 2:-2]
    nearest = (
        padded[:, 1:-3, 2:-2]
        + padded[:, 3:-1, 2:-2]
        + padded[:, 2:-2, 1:-3]
        + padded[:, 2:-2, 3:-1]
    )
    farther = (
        padded[:, :-4, 2:-2] + padded[:, 4:, 2:-2] + padded[:, 2:-2, :-4] + padded[:, 2:-2, 4:]
    )
    return (60.0 * central - 16.0 * nearest + farther) / 12.0


def vertical(values_in):
    upper_level = jnp.concatenate([jnp.zeros_like(values_in[:1]), values_in[:-1]], axis=0)
    lower_level = jnp.concatenate([values_in[1:], values_in[-1:]], axis=0)
    return 2.0 * values_in - upper_level - lower_level


def apply_operator(padded, horiz_coef, vert_coef):
    interior = padded[:, 2:-2, 2:-2]
    return horiz_coef * horizontal(padded) + vert_coef * vertical(interior)


def precondition(residual, line_scale, vert_mix):
    weighted = residual * line_scale
    return weighted + jnp.einsum("lm,mxy->lxy", vert_mix, weighted, precision=lax.Precision.HIGHEST)


def joint_steps(start_potential, residual, first_dir, first_img, second_part, second_img):
    totals = lax.psum(
        (
            jnp.sum(residual * first_img),
            jnp.sum(first_img * first_img),
            jnp.sum(residual * second_img),
            jnp.sum(first_img * second_img),
            jnp.sum(second_img * second_img),
        ),
        ("gx", "gy"),
    )
    cross_first, square_first, cross_mixed, square_mixed, square_second = totals
    first_step = cross_first / square_first
    next_top = (
        cross_first
        - first_step * cross_mixed
        - first_step * square_first
        + first_step * first_step * square_mixed
    )
    next_bottom = (
        square_first - 2.0 * first_step * square_mixed + first_step * first_step * square_second
    )
    second_step = next_top / next_bottom
    potential = start_potential + first_step * first_dir
    second_dir = first_dir - first_step * second_part
    return potential + second_step * second_dir


def per_device(
    forcing,
    start_potential,
    horiz_coef,
    vert_coef,
    vert_mix,
    mode_shapes,
    block_body,
    response,
    velocity_old,
):
    levels = forcing.shape[0]
    row_count = forcing.shape[1]
    col_count = forcing.shape[2]
    stacked = jnp.concatenate([start_potential, forcing, horiz_coef[None], vert_coef[None]], axis=0)
    wide = extended(stacked, (("gx", 1), ("gy", 2)), 6)
    phi_wide = wide[:levels]
    forcing_wide = wide[levels : 2 * levels, 2:-2, 2:-2]
    horiz_wide = wide[2 * levels, 2:-2, 2:-2]
    vert_wide = wide[2 * levels + 1, 2:-2, 2:-2]
    total_rows = row_count * lax.axis_size("gx")
    total_cols = col_count * lax.axis_size("gy")
    row_ids = lax.axis_index("gx") * row_count - 4 + jnp.arange(row_count + 8, dtype=jnp.int32)
    col_ids = lax.axis_index("gy") * col_count - 4 + jnp.arange(col_count + 8, dtype=jnp.int32)
    inside = ((row_ids >= 0) & (row_ids < total_rows))[:, None] & (
        (col_ids >= 0) & (col_ids < total_cols)
    )[None, :]
    inside_mask = inside.astype(jnp.float32)
    resid_wide = inside_mask * (forcing_wide - apply_operator(phi_wide, horiz_wide, vert_wide))
    scale_wide = inside_mask / (5.0 * horiz_wide + 2.0 * vert_wide + (1.0 - inside_mask))
    dir_wide = precondition(resid_wide, scale_wide, vert_mix)
    img_wide = apply_operator(dir_wide, horiz_wide[2:-2, 2:-2], vert_wide[2:-2, 2:-2])
    part_wide = precondition(img_wide, scale_wide[2:-2, 2:-2], vert_mix)
    second_img = apply_operator(part_wide, horiz_coef, vert_coef)
    potential = joint_steps(
        start_potential,
        resid_wide[:, 4:-4, 4:-4],
        dir_wide[:, 4:-4, 4:-4],
        img_wide[:, 2:-2, 2:-2],
        part_wide[:, 2:-2, 2:-2],
        second_img,
    )
    pressure = start_potential[0] - potential[0]
    mode_count = mode_shapes.shape[0]
    block_count = col_count // BLOCK
    owned = velocity_old.shape[1]
    body_total = owned * lax.axis_size(("gx", "gy"))
    block_sums = jnp.sum(
        (mode_shapes * pressure).reshape(mode_count, row_count, block_count, BLOCK), axis=3
    ).reshape(mode_count, row_count * block_count)
    one_hot = (
        block_body.reshape(-1)[:, None] == jnp.arange(body_total, dtype=jnp.int32)[None, :]
    ).astype(jnp.float32)
    partial_forces = jnp.dot(
        block_sums, one_hot, precision=lax.Precision.HIGHEST, preferred_element_type=jnp.float32
    )
    foot_scale = 1.0 / math.sqrt(FOOT)
    forces = (
        lax.psum_scatter(partial_forces, ("gx", "gy"), scatter_dimension=1, tiled=True) * foot_scale
    )
    velocity = velocity_old + jnp.einsum(
        "kmb,mb->kb", response, forces, precision=lax.Precision.HIGHEST
    )
    all_velocity = lax.all_gather(velocity, ("gx", "gy"), axis=1, tiled=True)
    block_vel = jnp.dot(
        all_velocity, one_hot.T, precision=lax.Precision.HIGHEST, preferred_element_type=jnp.float32
    )
    normal_flux = jnp.sum(
        mode_shapes.reshape(mode_count, row_count, block_count, BLOCK)
        * block_vel.reshape(mode_count, row_count, block_count)[..., None],
        axis=0,
    ).reshape(row_count, col_count)
    return (potential, velocity, normal_flux)


def solution(mesh):
    return jax.shard_map(
        per_device,
        mesh=mesh,
        in_specs=(
            P(None, "gx", "gy"),
            P(None, "gx", "gy"),
            P("gx", "gy"),
            P("gx", "gy"),
            P(),
            P(None, "gx", "gy"),
            P("gx", "gy"),
            P(None, None, ("gx", "gy")),
            P(None, ("gx", "gy")),
        ),
        out_specs=(P(None, "gx", "gy"), P(None, ("gx", "gy")), P("gx", "gy")),
        check_vma=False,
    )
```

profile of v0, /device:TPU:0, one launch (start us, length us, event | category | flops | bytes accessed | tf_op | source)
XLA Modules:
  0.0 254.2 jit_solution(10362364851152660197)
XLA Ops:
  0.7 2.1 copy.26
  5.7 3.0 %collective-permute-start = (f32[20,6,256]{2,0,1:T(8,128)}, f32[20,6,256]{2,0,1:T(8,128)}, u32[]{:S(2)}, u32[]{:S(2)}) collective-permute-start(f32[20,6,256]{2,0,1:T(8,128)} %get-tuple-element.28), channel_id=1, source_target_pairs={{0,4},{4,8},{8,12},{12,16},{16,20},{20,24},{24,28},{1,5},{5,9},{9,... | collective-permute-start | bytes 368648 | tf_op jit(solution)/shard_map/ppermute | solution.py:19
  8.7 1.3 collective-permute-start.1
  10.7 3.2 %collective-permute-done.1 = f32[20,6,256]{2,0,1:T(8,128)} collective-permute-done((f32[20,6,256]{2,0,1:T(8,128)}, f32[20,6,256]{2,0,1:T(8,128)}, u32[]{:S(2)}, u32[]{:S(2)}) %collective-permute-start.1) | collective-permute-done | bytes 122912 | tf_op jit(solution)/shard_map/ppermute | solution.py:20
  13.8 2.4 pad_maximum_fusion.1
  16.3 2.3 fusion.41
  18.6 3.1 %copy.27 = f32[20,140,6]{1,0,2:T(8,128)} copy(f32[20,140,6]{2,0,1:T(8,128)} %get-tuple-element.30) | data formatting | bytes 134400 | tf_op jit(solution)/shard_map/slice | solution.py:17
  21.7 4.1 %collective-permute-start.2 = (f32[20,140,6]{1,0,2:T(8,128)}, f32[20,140,6]{1,0,2:T(8,128)}, u32[]{:S(2)}, u32[]{:S(2)}) collective-permute-start(f32[20,140,6]{1,0,2:T(8,128)} %copy.27), channel_id=1, source_target_pairs={{0,1},{1,2},{2,3},{4,5},{5,6},{6,7},{8,9},{9,10},{10,11},{12,13},{... | collective-permute-start | bytes 201608 | tf_op jit(solution)/shard_map/ppermute | solution.py:19
  25.7 3.1 %copy.28 = f32[20,140,6]{1,0,2:T(8,128)} copy(f32[20,140,6]{2,0,1:T(8,128)} %get-tuple-element.31) | data formatting | bytes 134400 | tf_op jit(solution)/shard_map/slice | solution.py:18
  28.8 1.5 collective-permute-start.3
  32.0 3.0 %copy.29 = f32[20,140,6]{2,0,1:T(8,128)} copy(f32[20,140,6]{1,0,2:T(8,128)} %collective-permute-done.2) | data formatting | bytes 134400 | tf_op jit(solution)/shard_map/ppermute | solution.py:19
  36.2 3.1 %copy.30 = f32[20,140,6]{2,0,1:T(8,128)} copy(f32[20,140,6]{1,0,2:T(8,128)} %collective-permute-done.3) | data formatting | bytes 134400 | tf_op jit(solution)/shard_map/ppermute | solution.py:20
  39.2 8.6 %pad_maximum_fusion = f32[20,140,268]{2,0,1:T(8,128)S(1)} fusion(f32[20,140,6]{2,0,1:T(8,128)} %copy.30, f32[20,6,256]{2,0,1:T(8,128)} %collective-permute-done.1, f32[1,128,256]{2,0,1:T(1,128)S(1)} %broadcast_in_dim.5, f32[1,128,256]{2,0,1:T(1,128)S(1)} %broadcast_in_dim.4, f32[9,128,256]{2,0,1:T(8,128)S(1)} %copy.26, f32[9,128,256]{2,0,1:T(8,128)} %copy-done.2, ...), kind=kLoop, calls=%fused_computation | loop fusion | flops 5252800 | bytes 6003200 | tf_op jit(solution)/shard_map/concatenate | solution.py:21
  47.8 1.6 add_divide_fusion.1
  51.8 8.7 %fusion.4 = f32[9,136,264]{2,0,1:T(8,128)S(1)} fusion(f32[20,140,268]{2,0,1:T(8,128)S(1)} %pad_maximum_fusion, f32[1,136,264]{2,0,1:T(1,128)S(1)} %get-tuple-element.25, f32[8,136,264]{2,0,1:T(8,128)S(1)} %get-tuple-element.27, f32[8,136,264]{2,0,1:T(8,128)S(1)} %get-tuple-element.26, f32[136,264]{1,0:T(8,128)S(1)} %get-tuple-element.40, ...), kind=kLoop, calls=%fused_computation.7 | loop fusion | flops 6139584 | bytes 17090304 | tf_op jit(solution)/shard_map/mul | solution.py:111
  60.5 4.9 %bitcast_add_fusion = f32[9,136,264]{2,0,1:T(8,128)S(1)} fusion(f32[9,136,264]{2,0,1:T(8,128)S(1)} %fusion.4, f32[136,264]{1,0:T(8,128)} %get-tuple-element.39, f32[9,9]{1,0:T(8,128)S(1)} %copy-done), kind=kOutput, calls=%fused_computation.17 | convolution fusion | flops 35868096 | bytes 2729028 | tf_op jit(solution)/shard_map/lm,mxy->lxy/dot_general | solution.py:52
  67.2 7.3 %fusion.10 = f32[9,132,260]{2,0,1:T(8,128)S(1)} fusion(f32[9,136,264]{2,0,1:T(8,128)S(1)} %bitcast_add_fusion, f32[1,132,260]{2,0,1:T(1,128)S(1)} %slice.258, f32[8,132,260]{2,0,1:T(8,128)S(1)} %get-tuple-element.33, f32[8,132,260]{2,0,1:T(8,128)S(1)} %get-tuple-element.32, f32[132,260]{1,0:T(8,128)S(1)} %get-tuple-element.37, ...), kind=kLoop, calls=%fused_computation.21 | loop fusion | flops 5250960 | bytes 14963520 | tf_op jit(solution)/shard_map/add | solution.py:47
  74.5 3.9 %bitcast_add_fusion.1 = f32[9,132,260]{2,0,1:T(8,128)S(1)} fusion(f32[9,132,260]{2,0,1:T(8,128)S(1)} %fusion.10, f32[132,260]{1,0:T(8,128)S(1)} %get-tuple-element.36, f32[9,9]{1,0:T(8,128)S(1)} %copy-done), kind=kOutput, calls=%fused_computation.31 | convolution fusion | flops 34285680 | bytes 2608644 | tf_op jit(solution)/shard_map/lm,mxy->lxy/dot_general | solution.py:52
  79.6 6.7 %multiply_reduce_fusion.2 = (f32[]{:T(128)}, f32[]{:T(128)}, f32[]{:T(128)}, f32[]{:T(128)}, f32[]{:T(128)}) fusion(f32[9,136,264]{2,0,1:T(8,128)S(1)} %fusion.4, f32[9,132,260]{2,0,1:T(8,128)S(1)} %fusion.10, f32[1,128,256]{2,0,1:T(1,128)S(1)} %slice.275, f32[8,128,256]{2,0,1:T(8,128)S(1)} %get-tuple-element.35, f32[8,128,256]{2,0,1:T(8,128)S(1)} %get-tuple-element.34, ...), kind=kLoop, calls=%fused_computation.52 | loop fusion | flops 7962619 | bytes 15466516 | tf_op jit(solution)/shard_map/reduce_sum | solution.py:60
  86.3 42.8 %all-reduce.4 = (f32[]{:T(128)}, f32[]{:T(128)}, f32[]{:T(128)}, f32[]{:T(128)}, f32[]{:T(128)}) all-reduce(f32[]{:T(128)} %get-tuple-element.13, f32[]{:T(128)} %get-tuple-element.15, f32[]{:T(128)} %get-tuple-element.12, f32[]{:T(128)} %get-tuple-element.14, f32[]{:T(128)} %get-tuple-element.16), channel_id=1, replica_groups=mesh['gx'=8,'gy'=4] {'gx','gy'}, use_global_device_ids=true, to_apply=%region_1.0 | all-reduce | flops 5 | bytes 40 | tf_op jit(solution)/shard_map/psum | solution.py:56
  135.0 3.7 %multiply_add_fusion = f32[9,128,256]{2,0,1:T(8,128)S(1)} fusion(f32[9,136,264]{2,0,1:T(8,128)S(1)} %bitcast_add_fusion, f32[9,132,260]{2,0,1:T(8,128)} %copy-done.1, f32[]{:T(128)S(6)} %div.21, f32[]{:T(128)S(6)} %div.19, f32[9,128,256]{2,1,0:T(8,128)} %param.10), kind=kLoop, calls=%fused_computation.49 | loop fusion | flops 1769472 | bytes 4718600 | tf_op jit(solution)/shard_map/add | solution.py:80
  138.7 1.7 copy.38
  143.2 40.5 %all-reduce.3 = f32[6,64]{1,0:T(8,128)S(1)} all-reduce(f32[6,64]{1,0:T(8,128)S(1)} %fusion.31), channel_id=2, replica_groups=mesh['gx'=8,'gy'=4] {'gx','gy'}, use_global_device_ids=true, to_apply=%region_11.0.clone | all-reduce | flops 384 | bytes 3072
  184.0 66.0 %all-gather = f32[32,2,6]{2,1,0:T(2,128)S(1)} all-gather(f32[1,2,6]{2,1,0:T(2,128)S(1)} %bitcast.42), channel_id=1, replica_groups=mesh['gx'=8,'gy'=4] {'gx','gy'}, dimensions={0}, use_global_device_ids=true | all-gather | bytes 1584 | tf_op jit(solution)/shard_map/all_gather | solution.py:146
  (79 shorter events, 18.5 us)
Async XLA Ops:
  0.6 59.9 %copy-start = (f32[9,9]{1,0:T(8,128)S(1)}, f32[9,9]{1,0:T(8,128)}, u32[]{:S(2)}) copy-start(f32[9,9]{1,0:T(8,128)} %param.13) | copy-start | bytes 976
  0.6 2.2 copy-start.3
  0.7 2.9 %copy-start.13 = (f32[128,256]{1,0:T(8,128)S(1)}, f32[128,256]{1,0:T(8,128)}, u32[]{:S(2)}) copy-start(f32[128,256]{1,0:T(8,128)} %param.11) | copy-start | bytes 393220
  0.7 3.0 %copy-start.10 = (f32[128,256]{1,0:T(8,128)S(1)}, f32[128,256]{1,0:T(8,128)}, u32[]{:S(2)}) copy-start(f32[128,256]{1,0:T(8,128)} %param.12) | copy-start | bytes 393220
  3.6 1.3 copy-start.2
  5.7 5.0 %collective-permute-start = (f32[20,6,256]{2,0,1:T(8,128)}, f32[20,6,256]{2,0,1:T(8,128)}, u32[]{:S(2)}, u32[]{:S(2)}) collective-permute-start(f32[20,6,256]{2,0,1:T(8,128)} %get-tuple-element.28), channel_id=1, source_target_pairs={{0,4},{4,8},{8,12},{12,16},{16,20},{20,24},{24,28},{1,5},{5,9},{9,... | collective-permute-start | bytes 368648 | tf_op jit(solution)/shard_map/ppermute | solution.py:19
  8.7 5.2 %collective-permute-start.1 = (f32[20,6,256]{2,0,1:T(8,128)}, f32[20,6,256]{2,0,1:T(8,128)}, u32[]{:S(2)}, u32[]{:S(2)}) collective-permute-start(f32[20,6,256]{2,0,1:T(8,128)} %get-tuple-element.29), channel_id=1, source_target_pairs={{4,0},{8,4},{12,8},{16,12},{20,16},{24,20},{28,24},{5,1},{9,5},{13... | collective-permute-start | bytes 368648 | tf_op jit(solution)/shard_map/ppermute | solution.py:20
  10.7 19.6 %copy-start.16 = (pred[264]{0:T(512)(128)(4,1)}, pred[264]{0:T(512)(128)(4,1)S(1)}, u32[]{:S(2)}) copy-start(pred[264]{0:T(512)(128)(4,1)S(1)} %fusion.39) | copy-start | bytes 796
  21.7 10.3 %collective-permute-start.2 = (f32[20,140,6]{1,0,2:T(8,128)}, f32[20,140,6]{1,0,2:T(8,128)}, u32[]{:S(2)}, u32[]{:S(2)}) collective-permute-start(f32[20,140,6]{1,0,2:T(8,128)} %copy.27), channel_id=1, source_target_pairs={{0,1},{1,2},{2,3},{4,5},{5,6},{6,7},{8,9},{9,10},{10,11},{12,13},{... | collective-permute-start | bytes 201608 | tf_op jit(solution)/shard_map/ppermute | solution.py:19
  28.8 7.3 %collective-permute-start.3 = (f32[20,140,6]{1,0,2:T(8,128)}, f32[20,140,6]{1,0,2:T(8,128)}, u32[]{:S(2)}, u32[]{:S(2)}) collective-permute-start(f32[20,140,6]{1,0,2:T(8,128)} %copy.28), channel_id=1, source_target_pairs={{1,0},{2,1},{3,2},{5,4},{6,5},{7,6},{9,8},{10,9},{11,10},{13,12},{... | collective-permute-start | bytes 201608 | tf_op jit(solution)/shard_map/ppermute | solution.py:20
  39.2 8.6 %copy-start.17 = (pred[264]{0:T(512)(128)(4,1)S(1)}, pred[264]{0:T(512)(128)(4,1)}, u32[]{:S(2)}) copy-start(pred[264]{0:T(512)(128)(4,1)} %copy-done.16) | copy-start | bytes 796
  50.1 1.7 copy-start.7
  51.8 8.7 %copy-start.5 = (f32[136,264]{1,0:T(8,128)}, f32[136,264]{1,0:T(8,128)S(1)}, u32[]{:S(2)}) copy-start(f32[136,264]{1,0:T(8,128)S(1)} %get-tuple-element.40) | copy-start | bytes 430852
  65.5 1.4 copy-start.6
  65.5 1.4 copy-start.8
  65.5 1.4 copy-start.9
  78.3 8.0 %copy-start.1 = (f32[9,132,260]{2,0,1:T(8,128)}, f32[9,132,260]{2,0,1:T(8,128)S(1)}, u32[]{:S(2)}) copy-start(f32[9,132,260]{2,0,1:T(8,128)S(1)} %bitcast_add_fusion.1) | copy-start | bytes 3706564
  78.3 1.0 copy-start.11
  78.4 1.3 copy-start.12
  138.7 1.7 slice-start
  138.7 1.9 copy-start.4
  140.4 43.4 %copy-start.14 = (f32[6,6,2]{1,2,0:T(2,128)S(1)}, f32[6,6,2]{1,2,0:T(2,128)}, u32[]{:S(2)}) copy-start(f32[6,6,2]{1,2,0:T(2,128)} %param.16) | copy-start | bytes 868
  140.4 43.6 %copy-start.18 = (f32[6,2]{0,1:T(2,128)S(1)}, f32[6,2]{0,1:T(2,128)}, u32[]{:S(2)}) copy-start(f32[6,2]{0,1:T(2,128)} %param.17) | copy-start | bytes 148
  184.0 69.7 %copy-start.15 = (f32[6,2]{0,1:T(2,128)}, f32[6,2]{0,1:T(2,128)S(1)}, u32[]{:S(2)}) copy-start(f32[6,2]{0,1:T(2,128)S(1)} %bitcast_add_fusion.2) | copy-start | bytes 148
where the time goes:
time: 259 us; the launch traced here: 254 us
  blocking collectives  149 us (58%)
  other arithmetic  43.5 us (17%)
  local copies, waits for them, and re-layouts  30.7 us (12%)
  starting transfers between devices  9.79 us (4%)
  matrix products  9.35 us (4%)
  between operations  7.3 us (3%)
  waiting for transfers between devices  4.29 us (2%)
    all_gather x1, blocking collectives, per_device(): all_velocity = lax.all_gather(velocity, ('gx', 'gy'), axis=1, tiled=True)  66 us
    psum x1, blocking collectives, joint_steps(): lax.psum((jnp.sum(residual * first_img), jnp.sum(first_img * first_img),...  42.8 us
    unnamed x1, blocking collectives  40.5 us
    concatenate x2, other arithmetic, extended(): value = jnp.concatenate([before, value, after], axis=dim)  11 us
    dot_general x2, matrix products, precondition(): jnp.einsum('lm,mxy->lxy', vert_mix, weighted, precision=lax.Precision.HIG...  8.8 us
    mul x1, other arithmetic, per_device(): inside_mask * (forcing_wide - apply_operator(phi_wide, horiz_wide, vert_w...  8.69 us
    unnamed x46, local copies, waits for them, and re-layouts  8.39 us
    add x1, other arithmetic, apply_operator(): return horiz_coef * horizontal(padded) + vert_coef * vertical(interior)  7.28 us
  transfers between devices with their start and end apart: 4, of which 2 were waited for; matrix products, arithmetic and copies ran while one was open for 3% of the time, Pallas kernels for 0%

commit v1 on v0

v1 whole, which is shorter than its diff:
```python
import functools
import math

import jax
import jax.numpy as jnp
from jax import lax
from jax.experimental import pallas as pl
from jax.experimental.pallas import tpu as pltpu
from jax.sharding import PartitionSpec as P

FOOT = 8192
LANES = 128
SUB = 8
HALO = 6
F32 = jnp.float32
HBM = pl.BlockSpec(memory_space=pl.ANY)
VMEM = pl.BlockSpec(memory_space=pltpu.VMEM)
SMEM = pl.BlockSpec(memory_space=pltpu.SMEM)


def run_copies(copies):
    for copy in copies:
        copy.start()
    for copy in copies:
        copy.wait()


def pack_rows(phi, forcing, horiz, vert, near_out, far_out, sems):
    levels, rows, _ = phi.shape
    parity = lax.rem(lax.axis_index("gx"), 2)
    near_row = pl.multiple_of((1 - parity) * (rows - SUB), SUB)
    far_row = pl.multiple_of(parity * (rows - SUB), SUB)
    copies = []
    for out, row in ((near_out, near_row), (far_out, far_row)):
        pairs = (
            (phi.at[:, pl.ds(row, SUB), :], out.at[0:levels]),
            (forcing.at[:, pl.ds(row, SUB), :], out.at[levels : 2 * levels]),
            (horiz.at[pl.ds(row, SUB), :], out.at[2 * levels]),
            (vert.at[pl.ds(row, SUB), :], out.at[2 * levels + 1]),
        )
        for src, dst in pairs:
            copies.append(pltpu.make_async_copy(src, dst, sems.at[len(copies)]))
    run_copies(copies)


def pack_cols(phi, forcing, horiz, vert, near_in, far_in, near_out, far_out, strip, sems):
    levels, rows, cols = phi.shape
    planes = 2 * levels + 2
    row_par = lax.rem(lax.axis_index("gx"), 2)
    col_par = lax.rem(lax.axis_index("gy"), 2)
    near_row = pl.multiple_of((1 - row_par) * (rows + SUB), SUB)
    far_row = pl.multiple_of(row_par * (rows + SUB), SUB)
    copies = []
    for side, col in ((0, 0), (1, cols - LANES)):
        lanes = pl.ds(col, LANES)
        main = pl.ds(SUB, rows)
        pairs = (
            (phi.at[:, :, lanes], strip.at[side, 0:levels, main]),
            (forcing.at[:, :, lanes], strip.at[side, levels : 2 * levels, main]),
            (horiz.at[:, lanes], strip.at[side, 2 * levels, main]),
            (vert.at[:, lanes], strip.at[side, 2 * levels + 1, main]),
            (near_in.at[:, :, lanes], strip.at[side, :, pl.ds(near_row, SUB)]),
            (far_in.at[:, :, lanes], strip.at[side, :, pl.ds(far_row, SUB)]),
        )
        for src, dst in pairs:
            copies.append(pltpu.make_async_copy(src, dst, sems.at[len(copies)]))
    run_copies(copies)
    lane = lax.broadcasted_iota(jnp.int32, (SUB, LANES), 1)
    even = col_par == 0

    def body(i, carry):
        tile = pl.ds(pl.multiple_of(i * SUB, SUB), SUB)
        left = jnp.zeros((SUB, LANES), F32)
        right = jnp.zeros((SUB, LANES), F32)
        for p in range(planes):
            low = HALO * p
            here = (lane >= low) & (lane < low + HALO)
            left = jnp.where(here, pltpu.roll(strip[0, p, tile], low, 1), left)
            right = jnp.where(here, pltpu.roll(strip[1, p, tile], low + HALO, 1), right)
        near_out[tile] = jnp.where(even, right, left)
        far_out[tile] = jnp.where(even, left, right)
        return carry

    lax.fori_loop(0, (rows + 2 * SUB) // SUB, body, 0)


def stencil(ref, tile_row, wanted, tiles, levels, coefs, lane):
    center = [
        [ref[t, l, pl.ds(tile_row, SUB), :] for l in range(levels)] for t in range(tiles)
    ]
    result = []
    for t in wanted:
        after, before = center[(t + 1) % tiles], center[(t - 1) % tiles]
        mid_coef, last_coef, horiz12, vert = coefs[t]
        per_level = []
        for l in range(levels):
            x = center[t][l]

            def rows_at(offset):
                return ref[t, l, pl.ds(tile_row + offset, SUB), :]

            right1 = pltpu.roll(jnp.where(lane < 1, after[l], x), LANES - 1, 1)
            right2 = pltpu.roll(jnp.where(lane < 2, after[l], x), LANES - 2, 1)
            left1 = pltpu.roll(jnp.where(lane >= LANES - 1, before[l], x), 1, 1)
            left2 = pltpu.roll(jnp.where(lane >= LANES - 2, before[l], x), 2, 1)
            nearest = (rows_at(-1) + rows_at(1)) + (right1 + left1)
            farther = (rows_at(-2) + rows_at(2)) + (right2 + left2)
            if l == 0:
                beside = center[t][1]
            elif l == levels - 1:
                beside = center[t][l - 1]
            else:
                beside = center[t][l - 1] + center[t][l + 1]
            coef = last_coef if l == levels - 1 else mid_coef
            per_level.append(coef * x + horiz12 * (farther - 16.0 * nearest) - vert * beside)
        result.append(per_level)
    return result


def mix_levels(mix, weighted, levels):
    out = []
    for l in range(levels):
        total = (mix[l, l] + 1.0) * weighted[l]
        for m in range(levels):
            if m != l:
                total = total + mix[l, m] * weighted[m]
        out.append(total)
    return out


def body_hits(bodies_t, block, count, width):
    ids = bodies_t[block : block + 1, :]
    ids = jnp.where(ids < count, ids, -1)
    wanted = lax.broadcasted_iota(jnp.int32, (width, ids.shape[1]), 0)
    return (jnp.broadcast_to(ids, wanted.shape) == wanted).astype(F32)


def dot_nt(a, b):
    return lax.dot_general(
        a, b, (((1,), (1,)), ((), ())), precision=lax.Precision.HIGHEST, preferred_element_type=F32
    )


def main_kernel(
    body_total,
    phi,
    forcing,
    horiz,
    vert,
    row_near,
    row_far,
    col_near,
    col_far,
    mix,
    modes,
    bodies_t,
    response_t,
    old_t,
    dir_out,
    part_out,
    message,
    phi_s,
    res_s,
    horiz_s,
    vert_s,
    mid_s,
    last_s,
    scale_s,
    dir_s,
    img_s,
    part_s,
    mode_s,
    sums_s,
    small_s,
    sems,
    out_sems,
):
    levels, rows, cols = phi.shape
    mode_count = modes.shape[0]
    blocks = cols // LANES
    tiles = blocks + 1
    row_tiles = rows // SUB
    base = 2 * SUB
    gx, gy = lax.axis_index("gx"), lax.axis_index("gy")
    row_par, col_par = lax.rem(gx, 2), lax.rem(gy, 2)
    near_row = pl.multiple_of((1 - row_par) * (rows + SUB) + SUB, SUB)
    far_row = pl.multiple_of(row_par * (rows + SUB) + SUB, SUB)
    copies = []

    def start(src, dst):
        copy = pltpu.make_async_copy(src, dst, sems.at[len(copies)])
        copy.start()
        copies.append(copy)

    main = pl.ds(base, rows)
    for t in range(blocks):
        lanes = pl.ds(t * LANES, LANES)
        start(phi.at[:, :, lanes], phi_s.at[t, :, main])
        start(forcing.at[:, :, lanes], res_s.at[t, :, main])
        start(horiz.at[:, lanes], horiz_s.at[t, main])
        start(vert.at[:, lanes], vert_s.at[t, main])
        for got, row in ((row_near, near_row), (row_far, far_row)):
            here = pl.ds(row, SUB)
            start(got.at[0:levels, :, lanes], phi_s.at[t, :, here])
            start(got.at[levels : 2 * levels, :, lanes], res_s.at[t, :, here])
            start(got.at[2 * levels, :, lanes], horiz_s.at[t, here])
            start(got.at[2 * levels + 1, :, lanes], vert_s.at[t, here])
    needed = list(copies)
    for t in range(blocks):
        start(modes.at[:, :, pl.ds(t * LANES, LANES)], mode_s.at[t])
    mode_copies = copies[len(needed) :]

    lane = lax.broadcasted_iota(jnp.int32, (SUB, LANES), 1)
    sub = lax.broadcasted_iota(jnp.int32, (SUB, LANES), 0)
    side = tiles - 1
    even = col_par == 0
    planes = [phi_s.at[side, l] for l in range(levels)]
    planes += [res_s.at[side, l] for l in range(levels)]
    planes += [horiz_s.at[side], vert_s.at[side]]

    def unpack(i, carry):
        src = pl.ds(pl.multiple_of(i * SUB, SUB), SUB)
        dst = pl.ds(pl.multiple_of(i * SUB + SUB, SUB), SUB)
        near, far = col_near[src, :], col_far[src, :]
        right = jnp.where(even, near, far)
        left = jnp.where(even, far, near)
        for p, plane in enumerate(planes):
            low = HALO * p
            from_right = pltpu.roll(right, (LANES - low) % LANES, 1)
            from_left = pltpu.roll(left, (LANES - HALO - low) % LANES, 1)
            value = jnp.where(lane < HALO, from_right, 0.0)
            plane[dst, :] = jnp.where(lane >= LANES - HALO, from_left, value)
        return carry

    lax.fori_loop(0, row_tiles + 2, unpack, 0)
    for copy in needed:
        copy.wait()

    def coefficients(i, carry):
        here = pl.ds(pl.multiple_of(i * SUB + SUB, SUB), SUB)
        for t in range(tiles):
            h, v = horiz_s[t, here, :], vert_s[t, here, :]
            bottom = 5.0 * h + 2.0 * v
            inside = bottom > 0.0
            scale_s[t, here, :] = jnp.where(inside, 1.0 / jnp.where(inside, bottom, 1.0), 0.0)
            last = 5.0 * h + v
            mid_s[t, here, :] = last + v
            last_s[t, here, :] = last
            horiz_s[t, here, :] = h * (1.0 / 12.0)
        return carry

    lax.fori_loop(0, row_tiles + 2, coefficients, 0)

    def coefs_at(row, t):
        here = pl.ds(row, SUB)
        return (mid_s[t, here, :], last_s[t, here, :], horiz_s[t, here, :], vert_s[t, here, :])

    everything = range(tiles)

    def first(i, carry):
        row = pl.multiple_of(i * SUB + SUB, SUB)
        here = pl.ds(row, SUB)
        coefs = [coefs_at(row, t) for t in everything]
        image = stencil(phi_s, row, everything, tiles, levels, coefs, lane)
        for t in everything:
            scale = scale_s[t, here, :]
            weighted = []
            for l in range(levels):
                residual = res_s[t, l, here, :] - image[t][l]
                res_s[t, l, here, :] = residual
                weighted.append(residual * scale)
            for l, value in enumerate(mix_levels(mix, weighted, levels)):
                dir_s[t, l, here, :] = value
        return carry

    lax.fori_loop(0, row_tiles + 2, first, 0)
    outgoing = []

    def send(scratch, out, where):
        for t in range(blocks):
            copy = pltpu.make_async_copy(
                scratch.at[t, :, main], out.at[:, :, pl.ds(t * LANES, LANES)], where.at[t]
            )
            copy.start()
            outgoing.append(copy)

    send(dir_s, dir_out, out_sems.at[0])

    def second(i, carry):
        row = pl.multiple_of(i * SUB + SUB, SUB)
        here = pl.ds(row, SUB)
        coefs = [coefs_at(row, t) for t in everything]
        image = stencil(dir_s, row, everything, tiles, levels, coefs, lane)
        for t in everything:
            scale = scale_s[t, here, :]
            weighted = []
            for l in range(levels):
                img_s[t, l, here, :] = image[t][l]
                weighted.append(image[t][l] * scale)
            for l, value in enumerate(mix_levels(mix, weighted, levels)):
                part_s[t, l, here, :] = value
        return carry

    lax.fori_loop(0, row_tiles + 2, second, 0)
    send(part_s, part_out, out_sems.at[1])
    for copy in mode_copies:
        copy.wait()

    def third(i, totals):
        row = pl.multiple_of(i * SUB + base, SUB)
        here = pl.ds(row, SUB)
        own = pl.ds(pl.multiple_of(i * SUB, SUB), SUB)
        coefs = [coefs_at(row, t) for t in range(blocks)]
        image = stencil(part_s, row, range(blocks), tiles, levels, coefs, lane)
        totals = list(totals)
        for t in range(blocks):
            for l in range(levels):
                residual = res_s[t, l, here, :]
                img1 = img_s[t, l, here, :]
                img2 = image[t][l]
                products = (residual * img1, img1 * img1, residual * img2, img1 * img2, img2 * img2)
                totals = [total + product for total, product in zip(totals, products)]
        sums = jnp.zeros((SUB, LANES), F32)
        for t in range(blocks):
            for q, field in enumerate((dir_s, part_s)):
                surface = field[t, 0, here, :]
                for k in range(mode_count):
                    term = jnp.sum(mode_s[t, k, own, :] * surface, axis=1, keepdims=True)
                    sums = jnp.where(lane == (2 * t + q) * SUB + k, term, sums)
        sums_s[own, :] = sums
        return tuple(totals)

    zero = jnp.zeros((SUB, LANES), F32)
    totals = lax.fori_loop(0, row_tiles, third, (zero,) * 5)

    width = message.shape[1]
    sums_t = sums_s[...].T
    forces = jnp.zeros((SUB, width), F32)
    for t in range(blocks):
        hits = body_hits(bodies_t, t, body_total, width)
        first_sums = sums_t[2 * t * SUB : (2 * t + 1) * SUB, :]
        second_sums = sums_t[(2 * t + 1) * SUB : (2 * t + 2) * SUB, :]
        forces = forces + lax.dot_general(
            first_sums,
            hits,
            (((1,), (1,)), ((), ())),
            precision=lax.Precision.HIGHEST,
            preferred_element_type=F32,
        )
        forces = forces + pltpu.roll(dot_nt(second_sums, hits), body_total, 1)
    wide_sub = lax.broadcasted_iota(jnp.int32, (SUB, width), 0)
    wide_lane = lax.broadcasted_iota(jnp.int32, (SUB, width), 1)
    for q, total in enumerate(totals):
        forces = jnp.where((wide_sub == SUB - 2) & (wide_lane == q), jnp.sum(total), forces)
    message[0:SUB, :] = forces

    owned = old_t.shape[0]
    small_s[...] = jnp.zeros((LANES, LANES), F32)
    for k in range(mode_count):
        small_s[k * SUB : k * SUB + owned, 0:mode_count] = response_t[k]
        small_s[k * SUB : k * SUB + owned, mode_count : mode_count + 1] = old_t[:, k : k + 1]
    table = small_s[...].T[0:SUB, :]
    if width > LANES:
        table = jnp.concatenate([table, jnp.zeros((SUB, width - LANES), F32)], axis=1)
    me = (gx * lax.axis_size("gy") + gy) * owned
    for pair in range(mode_count // 2):
        tile = jnp.zeros((SUB, width), F32)
        for half in range(2):
            place = half * body_total + me
            shift = lax.rem(place - (2 * pair + half) * SUB + width, width)
            here = (wide_lane >= place) & (wide_lane < place + owned)
            tile = jnp.where(here, pltpu.roll(table, shift, 1), tile)
        message[(pair + 1) * SUB : (pair + 2) * SUB, :] = tile
    for copy in outgoing:
        copy.wait()


def last_kernel(
    body_total,
    message,
    phi,
    direction,
    part,
    modes,
    bodies_t,
    potential,
    velocity_t,
    flux,
    phi_s,
    dir_s,
    part_s,
    mode_s,
    flux_s,
    in_sems,
    mode_sem,
    out_sems,
):
    levels, rows, cols = phi.shape
    mode_count = modes.shape[0]
    blocks = cols // LANES
    width = message.shape[1]
    owned = velocity_t.shape[0]
    copies = []
    for l in range(levels):
        group = []
        for q, (src, dst) in enumerate(((phi, phi_s), (direction, dir_s), (part, part_s))):
            copy = pltpu.make_async_copy(src.at[l], dst.at[l], in_sems.at[l, q])
            copy.start()
            group.append(copy)
        copies.append(group)
    mode_copy = pltpu.make_async_copy(modes, mode_s, mode_sem.at[0])
    mode_copy.start()

    top = message[0:SUB, :]

    def scalar(q):
        return top[SUB - 2 : SUB - 1, q : q + 1]

    cross_first, square_first, cross_mixed, square_mixed, square_second = [
        scalar(q) for q in range(5)
    ]
    first_step = cross_first / square_first
    next_top = (
        cross_first
        - first_step * cross_mixed
        - first_step * square_first
        + first_step * first_step * square_mixed
    )
    next_bottom = (
        square_first - 2.0 * first_step * square_mixed + first_step * first_step * square_second
    )
    second_step = next_top / next_bottom
    on_dir = first_step + second_step
    on_part = first_step * second_step

    wide_sub = lax.broadcasted_iota(jnp.int32, (SUB, width), 0)
    wide_lane = lax.broadcasted_iota(jnp.int32, (SUB, width), 1)
    foot_scale = 1.0 / math.sqrt(FOOT)
    forces = foot_scale * (on_part * pltpu.roll(top, body_total, 1) - on_dir * top)
    forces = jnp.where(wide_sub == mode_count, 1.0, forces)
    forces = jnp.where(wide_lane < body_total, forces, 0.0)
    velocity = jnp.zeros((SUB, width), F32)
    for k in range(mode_count):
        table = message[(k // 2 + 1) * SUB : (k // 2 + 2) * SUB, :]
        if k % 2:
            table = pltpu.roll(table, body_total, 1)
        value = jnp.sum(table * forces, axis=0, keepdims=True)
        velocity = jnp.where(wide_sub == k, value, velocity)

    me = (lax.axis_index("gx") * lax.axis_size("gy") + lax.axis_index("gy")) * owned
    mine = ((wide_lane == me + wide_sub) & (wide_sub < owned)).astype(F32)
    velocity_t[...] = dot_nt(mine, velocity)[0:owned, 0:mode_count]

    per_row = []
    for t in range(blocks):
        hits = body_hits(bodies_t, t, body_total, width)
        per_row.append(
            lax.dot_general(
                velocity,
                hits,
                (((1,), (0,)), ((), ())),
                precision=lax.Precision.HIGHEST,
                preferred_element_type=F32,
            )
        )
    per_row.append(jnp.zeros((LANES - blocks * SUB, rows), F32))
    spread = jnp.concatenate(per_row, axis=0).T

    mode_copy.wait()
    for t in range(blocks):
        lanes = pl.ds(t * LANES, LANES)
        total = jnp.zeros((rows, LANES), F32)
        for k in range(mode_count):
            total = total + mode_s[k, :, lanes] * spread[:, t * SUB + k : t * SUB + k + 1]
        flux_s[:, lanes] = total
    flux_copy = pltpu.make_async_copy(flux_s, flux, out_sems.at[levels])
    flux_copy.start()
    outgoing = [flux_copy]
    for l in range(levels):
        for copy in copies[l]:
            copy.wait()
        phi_s[l] = phi_s[l] + (on_dir * dir_s[l] - on_part * part_s[l])
        copy = pltpu.make_async_copy(phi_s.at[l], potential.at[l], out_sems.at[l])
        copy.start()
        outgoing.append(copy)
    for copy in outgoing:
        copy.wait()


def swap_near(value, axis):
    size = lax.axis_size(axis)
    return lax.ppermute(value, axis, [(i, i ^ 1) for i in range(size)])


def swap_far(value, axis):
    size = lax.axis_size(axis)
    pairs = [(i, i + 1) for i in range(1, size - 1, 2)]
    return lax.ppermute(value, axis, pairs + [(j, i) for i, j in pairs])


def sum_over(value, axes):
    for axis in axes:
        size = lax.axis_size(axis)
        step = 1
        while step < size:
            value = value + lax.ppermute(value, axis, [(i, i ^ step) for i in range(size)])
            step *= 2
    return value


def per_device(
    forcing,
    start_potential,
    horiz_coef,
    vert_coef,
    vert_mix,
    mode_shapes,
    block_body,
    response,
    velocity_old,
):
    levels, rows, cols = forcing.shape
    mode_count = mode_shapes.shape[0]
    planes = 2 * levels + 2
    blocks = cols // LANES
    tiles = blocks + 1
    owned = velocity_old.shape[1]
    body_total = owned * lax.axis_size(("gx", "gy"))
    width = 2 * body_total
    bodies_t = block_body.T
    response_t = jnp.swapaxes(response, 1, 2)
    old_t = velocity_old.T
    limit = pltpu.CompilerParams(vmem_limit_bytes=40 * 2**20)

    row_message = jax.ShapeDtypeStruct((planes, SUB, cols), F32)
    near, far = pl.pallas_call(
        pack_rows,
        out_shape=(row_message, row_message),
        in_specs=[HBM] * 4,
        out_specs=(VMEM, VMEM),
        scratch_shapes=[pltpu.SemaphoreType.DMA((8,))],
        name="pack_rows",
    )(start_potential, forcing, horiz_coef, vert_coef)
    row_near, row_far = swap_near(near, "gx"), swap_far(far, "gx")

    col_message = jax.ShapeDtypeStruct((rows + 2 * SUB, LANES), F32)
    near, far = pl.pallas_call(
        pack_cols,
        out_shape=(col_message, col_message),
        in_specs=[HBM] * 6,
        out_specs=(VMEM, VMEM),
        scratch_shapes=[
            pltpu.VMEM((2, planes, rows + 2 * SUB, LANES), F32),
            pltpu.SemaphoreType.DMA((12,)),
        ],
        compiler_params=limit,
        name="pack_cols",
    )(start_potential, forcing, horiz_coef, vert_coef, row_near, row_far)
    col_near, col_far = swap_near(near, "gy"), swap_far(far, "gy")

    field = pltpu.VMEM((tiles, levels, rows + 4 * SUB, LANES), F32)
    plane = pltpu.VMEM((tiles, rows + 4 * SUB, LANES), F32)
    whole = jax.ShapeDtypeStruct((levels, rows, cols), F32)
    direction, part, message = pl.pallas_call(
        functools.partial(main_kernel, body_total),
        out_shape=(whole, whole, jax.ShapeDtypeStruct((4 * SUB, width), F32)),
        in_specs=[HBM] * 6 + [VMEM] * 2 + [SMEM, HBM] + [VMEM] * 3,
        out_specs=(HBM, HBM, VMEM),
        scratch_shapes=[
            field,
            field,
            plane,
            plane,
            plane,
            plane,
            plane,
            field,
            field,
            field,
            pltpu.VMEM((blocks, mode_count, rows, LANES), F32),
            pltpu.VMEM((rows, LANES), F32),
            pltpu.VMEM((LANES, LANES), F32),
            pltpu.SemaphoreType.DMA((13 * blocks,)),
            pltpu.SemaphoreType.DMA((2, blocks)),
        ],
        compiler_params=limit,
        name="main_kernel",
    )(
        start_potential,
        forcing,
        horiz_coef,
        vert_coef,
        row_near,
        row_far,
        col_near,
        col_far,
        vert_mix,
        mode_shapes,
        bodies_t,
        response_t,
        old_t,
    )
    message = sum_over(message, ("gx", "gy"))

    local = pltpu.VMEM((levels, rows, cols), F32)
    potential, velocity_t, flux = pl.pallas_call(
        functools.partial(last_kernel, body_total),
        out_shape=(
            whole,
            jax.ShapeDtypeStruct((owned, mode_count), F32),
            jax.ShapeDtypeStruct((rows, cols), F32),
        ),
        in_specs=[VMEM] + [HBM] * 4 + [VMEM],
        out_specs=(HBM, VMEM, HBM),
        scratch_shapes=[
            local,
            local,
            local,
            pltpu.VMEM((mode_count, rows, cols), F32),
            pltpu.VMEM((rows, cols), F32),
            pltpu.SemaphoreType.DMA((levels, 3)),
            pltpu.SemaphoreType.DMA((1,)),
            pltpu.SemaphoreType.DMA((levels + 1,)),
        ],
        compiler_params=limit,
        name="last_kernel",
    )(message, start_potential, direction, part, mode_shapes, bodies_t)
    return (potential, velocity_t.T, flux)


def solution(mesh):
    return jax.shard_map(
        per_device,
        mesh=mesh,
        in_specs=(
            P(None, "gx", "gy"),
            P(None, "gx", "gy"),
            P("gx", "gy"),
            P("gx", "gy"),
            P(),
            P(None, "gx", "gy"),
            P("gx", "gy"),
            P(None, None, ("gx", "gy")),
            P(None, ("gx", "gy")),
        ),
        out_specs=(P(None, "gx", "gy"), P(None, ("gx", "gy")), P("gx", "gy")),
        check_vma=False,
    )
```

time: 259 us -> 64.9 us (0.25); the launches traced: 254 us -> 64.7 us
  blocking collectives: 149 us -> 0 us
  other arithmetic: 43.5 us -> 0.02 us
  local copies, waits for them, and re-layouts: 30.7 us -> 0.04 us
  Pallas kernels: 0 us -> 30.4 us
  starting transfers between devices: 9.79 us -> 23.7 us
  matrix products: 9.35 us -> 0 us
  between operations: 7.3 us -> 0.77 us
  waiting for transfers between devices: 4.29 us -> 9.78 us
    all_gather x1 -> x0, blocking collectives: 66 us -> none  [per_device(): all_velocity = lax.all_gather(velocity, ('gx', 'gy'), axis=1, tiled=True)]
    psum x1 -> x0, blocking collectives: 42.8 us -> none  [joint_steps(): lax.psum((jnp.sum(residual * first_img), jnp.sum(first_img * first_img),...]
    unnamed x1 -> x0, blocking collectives: 40.5 us -> none
    pallas_call x0 -> x4, Pallas kernels: none -> 30.4 us  [the longest x1 18.6 us: per_device(): pl.pallas_call(functools.partial(main_kernel, body_total), out_shape=(who...]
    ppermute x4 -> x9, starting transfers between devices: 9.79 us -> 23.7 us  [the longest x5 18.8 us: sum_over(): lax.ppermute(value, axis, [(i, i ^ step) for i in range(size)])]
    slice x10 -> x0, local copies, waits for them, and re-layouts: 11.8 us -> none  [the longest x2 5.42 us: extended(): last = lax.slice_in_dim(value, length - width, length, axis=dim)]
    concatenate x2 -> x0, other arithmetic: 11 us -> none  [extended(): value = jnp.concatenate([before, value, after], axis=dim)]
    add x3 -> x5, other arithmetic: 11 us -> 0.02 us  [sum_over(): value + lax.ppermute(value, axis, [(i, i ^ step) for i in range(size)])]
  transfers between devices with their start and end apart: 4 -> 9, of which waited for: 2 -> 7; matrix products, arithmetic and copies ran while one was open for 3% -> 0% of each run, Pallas kernels for 0% -> 0%
where the time goes in v1:
time: 64.9 us; the launch traced here: 64.7 us
  Pallas kernels  30.4 us (47%)
  starting transfers between devices  23.7 us (37%)
  waiting for transfers between devices  9.78 us (15%)
  between operations  0.77 us (1%)
    ppermute x5, starting transfers between devices, sum_over(): lax.ppermute(value, axis, [(i, i ^ step) for i in range(size)])  18.8 us
    pallas_call x1, Pallas kernels, per_device(): pl.pallas_call(functools.partial(main_kernel, body_total), out_shape=(who...  18.6 us
    ppermute x5, waiting for transfers between devices, sum_over(): lax.ppermute(value, axis, [(i, i ^ step) for i in range(size)])  7.7 us
    pallas_call x1, Pallas kernels, per_device(): pl.pallas_call(functools.partial(last_kernel, body_total), out_shape=(who...  7.43 us
    ppermute x2, starting transfers between devices, swap_near(): return lax.ppermute(value, axis, [(i, i ^ 1) for i in range(size)])  3.44 us
    pallas_call x1, Pallas kernels, per_device(): pl.pallas_call(pack_cols, out_shape=(col_message, col_message), in_specs=...  2.34 us
    ppermute x2, waiting for transfers between devices, swap_near(): return lax.ppermute(value, axis, [(i, i ^ 1) for i in range(size)])  2.08 us
    pallas_call x1, Pallas kernels, per_device(): pl.pallas_call(pack_rows, out_shape=(row_message, row_message), in_specs=...  1.98 us
  transfers between devices with their start and end apart: 9, of which 7 were waited for; matrix products, arithmetic and copies ran while one was open for 0% of the time, Pallas kernels for 0%

profile of v1, /device:TPU:0, one launch (start us, length us, event | category | flops | bytes accessed | tf_op | source)
XLA Modules:
  0.0 64.7 jit_solution(10213319396930776540)
XLA Ops:
  0.6 0.0 copy-start
  0.7 2.0 %pack_rows.1 = (f32[20,8,256]{2,1,0:T(8,128)}, f32[20,8,256]{2,1,0:T(8,128)}) custom-call(f32[9,128,256]{2,1,0:T(8,128)} %phi.7, f32[9,128,256]{2,1,0:T(8,128)} %forcing.5, f32[128,256]{1,0:T(8,128)} %horiz.5, f32[128,256]{1,0:T(8,128)} %vert.5), custom_call_target="tpu_custom_call" | custom-call | tf_op jit(solution)/shard_map/pack_rows/pallas_call | solution.py:536
  2.7 0.5 collective-permute-start
  3.2 0.0 copy-start.8
  3.2 0.8 %collective-permute-start.1 = (f32[20,8,256]{2,1,0:T(8,128)}, f32[20,8,256]{2,1,0:T(8,128)S(1)}, u32[]{:S(2)}, u32[]{:S(2)}) collective-permute-start(f32[20,8,256]{2,1,0:T(8,128)} %get-tuple-element.14), channel_id=1, source_target_pairs={{4,8},{12,16},{20,24},{8,4},{16,12},{24,20},{5,9},{13,17},{21,25},... | collective-permute-start | bytes 491528 | tf_op jit(solution)/shard_map/ppermute | solution.py:498
  4.0 0.4 collective-permute-done.near_in.row_near
  4.4 0.0 collective-permute-done.1.far_in.row_far
  4.4 2.3 %pack_cols.1 = (f32[144,128]{1,0:T(8,128)S(1)}, f32[144,128]{1,0:T(8,128)S(1)}) custom-call(f32[9,128,256]{2,1,0:T(8,128)S(1)} %copy-done, f32[9,128,256]{2,1,0:T(8,128)S(1)} %copy-done.1, f32[128,256]{1,0:T(8,128)S(1)} %copy-done.3, f32[128,256]{1,0:T(8,128)S(1)} %copy-done.4, f32[20,8,256]{2,1,0:T(8,128)S(1)} %collective-permute-done.near_in.row_near, ...), custom_call_target="tpu_custom_call" | custom-call | tf_op jit(solution)/shard_map/pack_cols/pallas_call | solution.py:547
  6.8 2.9 %collective-permute-start.2 = (f32[144,128]{1,0:T(8,128)S(1)}, f32[144,128]{1,0:T(8,128)S(1)}, u32[]{:S(2)}, u32[]{:S(2)}) collective-permute-start(f32[144,128]{1,0:T(8,128)S(1)} %get-tuple-element.15), channel_id=1, source_target_pairs={{0,1},{1,0},{2,3},{3,2},{4,5},{5,4},{6,7},{7,6},{8,9},{9,8},{10,11... | collective-permute-start | bytes 221192 | tf_op jit(solution)/shard_map/ppermute | solution.py:492
  9.7 0.7 %collective-permute-start.3 = (f32[144,128]{1,0:T(8,128)S(1)}, f32[144,128]{1,0:T(8,128)S(1)}, u32[]{:S(2)}, u32[]{:S(2)}) collective-permute-start(f32[144,128]{1,0:T(8,128)S(1)} %get-tuple-element.16), channel_id=1, source_target_pairs={{1,2},{2,1},{5,6},{6,5},{9,10},{10,9},{13,14},{14,13},{17,18},{18,... | collective-permute-start | bytes 221192 | tf_op jit(solution)/shard_map/ppermute | solution.py:498
  10.4 1.7 %collective-permute-done.2.col_near = f32[144,128]{1,0:T(8,128)S(1)} collective-permute-done((f32[144,128]{1,0:T(8,128)S(1)}, f32[144,128]{1,0:T(8,128)S(1)}, u32[]{:S(2)}, u32[]{:S(2)}) %collective-permute-start.2) | collective-permute-done | bytes 73760 | tf_op jit(solution)/shard_map/ppermute | solution.py:492
  12.0 0.0 collective-permute-done.3.col_far
  12.1 18.6 %main_kernel.1 = (f32[9,128,256]{2,1,0:T(8,128)S(1)}, f32[9,128,256]{2,1,0:T(8,128)S(1)}, f32[32,128]{1,0:T(8,128)S(1)}) custom-call(f32[9,128,256]{2,1,0:T(8,128)S(1)} %copy-done, f32[9,128,256]{2,1,0:T(8,128)S(1)} %copy-done.1, f32[128,256]{1,0:T(8,128)S(1)} %copy-done.3, f32[128,256]{1,0:T(8,128)S(1)} %copy-done.4, ...), custom_call_target="tpu_custom_call" | custom-call | tf_op jit(solution)/shard_map/main_kernel/pallas_call | solution.py:564
  30.7 5.5 %collective-permute-start.4 = (f32[32,128]{1,0:T(8,128)S(1)}, f32[32,128]{1,0:T(8,128)S(1)}, u32[]{:S(2)}, u32[]{:S(2)}) collective-permute-start(f32[32,128]{1,0:T(8,128)S(1)} %get-tuple-element.17), channel_id=1, source_target_pairs={{0,4},{4,0},{8,12},{12,8},{16,20},{20,16},{24,28},{28,24},{1,5},{5... | collective-permute-start | bytes 49160 | tf_op jit(solution)/shard_map/ppermute | solution.py:506
  36.3 0.8 %collective-permute-done.4 = f32[32,128]{1,0:T(8,128)S(1)} collective-permute-done((f32[32,128]{1,0:T(8,128)S(1)}, f32[32,128]{1,0:T(8,128)S(1)}, u32[]{:S(2)}, u32[]{:S(2)}) %collective-permute-start.4) | collective-permute-done | bytes 16416 | tf_op jit(solution)/shard_map/ppermute | solution.py:506
  37.1 2.7 %collective-permute-start.5 = (f32[32,128]{1,0:T(8,128)S(1)}, f32[32,128]{1,0:T(8,128)S(1)}, u32[]{:S(2)}, u32[]{:S(2)}) collective-permute-start(f32[32,128]{1,0:T(8,128)S(1)} %add.15), channel_id=1, source_target_pairs={{0,8},{4,12},{8,0},{12,4},{16,24},{20,28},{24,16},{28,20},{1,9},{5... | collective-permute-start | bytes 49160 | tf_op jit(solution)/shard_map/ppermute | solution.py:506
  39.8 1.7 %collective-permute-done.5 = f32[32,128]{1,0:T(8,128)S(1)} collective-permute-done((f32[32,128]{1,0:T(8,128)S(1)}, f32[32,128]{1,0:T(8,128)S(1)}, u32[]{:S(2)}, u32[]{:S(2)}) %collective-permute-start.5) | collective-permute-done | bytes 16416 | tf_op jit(solution)/shard_map/ppermute | solution.py:506
  41.5 3.0 %collective-permute-start.6 = (f32[32,128]{1,0:T(8,128)S(1)}, f32[32,128]{1,0:T(8,128)S(1)}, u32[]{:S(2)}, u32[]{:S(2)}) collective-permute-start(f32[32,128]{1,0:T(8,128)S(1)} %add.16), channel_id=1, source_target_pairs={{0,16},{4,20},{8,24},{12,28},{16,0},{20,4},{24,8},{28,12},{1,17},{... | collective-permute-start | bytes 49160 | tf_op jit(solution)/shard_map/ppermute | solution.py:506
  44.6 1.7 %collective-permute-done.6 = f32[32,128]{1,0:T(8,128)S(1)} collective-permute-done((f32[32,128]{1,0:T(8,128)S(1)}, f32[32,128]{1,0:T(8,128)S(1)}, u32[]{:S(2)}, u32[]{:S(2)}) %collective-permute-start.6) | collective-permute-done | bytes 16416 | tf_op jit(solution)/shard_map/ppermute | solution.py:506
  46.3 4.5 %collective-permute-start.7 = (f32[32,128]{1,0:T(8,128)S(1)}, f32[32,128]{1,0:T(8,128)S(1)}, u32[]{:S(2)}, u32[]{:S(2)}) collective-permute-start(f32[32,128]{1,0:T(8,128)S(1)} %add.17), channel_id=1, source_target_pairs={{0,1},{1,0},{2,3},{3,2},{4,5},{5,4},{6,7},{7,6},{8,9},{9,8},{10,11... | collective-permute-start | bytes 49160 | tf_op jit(solution)/shard_map/ppermute | solution.py:506
  50.8 1.7 %collective-permute-done.7 = f32[32,128]{1,0:T(8,128)S(1)} collective-permute-done((f32[32,128]{1,0:T(8,128)S(1)}, f32[32,128]{1,0:T(8,128)S(1)}, u32[]{:S(2)}, u32[]{:S(2)}) %collective-permute-start.7) | collective-permute-done | bytes 16416 | tf_op jit(solution)/shard_map/ppermute | solution.py:506
  52.5 3.0 %collective-permute-start.8 = (f32[32,128]{1,0:T(8,128)S(1)}, f32[32,128]{1,0:T(8,128)S(1)}, u32[]{:S(2)}, u32[]{:S(2)}) collective-permute-start(f32[32,128]{1,0:T(8,128)S(1)} %add.18), channel_id=1, source_target_pairs={{0,2},{1,3},{2,0},{3,1},{4,6},{5,7},{6,4},{7,5},{8,10},{9,11},{10,... | collective-permute-start | bytes 49160 | tf_op jit(solution)/shard_map/ppermute | solution.py:506
  55.5 1.7 %collective-permute-done.8 = f32[32,128]{1,0:T(8,128)S(1)} collective-permute-done((f32[32,128]{1,0:T(8,128)S(1)}, f32[32,128]{1,0:T(8,128)S(1)}, u32[]{:S(2)}, u32[]{:S(2)}) %collective-permute-start.8) | collective-permute-done | bytes 16416 | tf_op jit(solution)/shard_map/ppermute | solution.py:506
  57.3 7.4 %last_kernel.1 = (f32[9,128,256]{2,1,0:T(8,128)}, f32[2,6]{1,0:T(2,128)}, f32[128,256]{1,0:T(8,128)}) custom-call(f32[32,128]{1,0:T(8,128)S(1)} %add.19.message, f32[9,128,256]{2,1,0:T(8,128)S(1)} %copy-done, f32[9,128,256]{2,1,0:T(8,128)S(1)} %get-tuple-element.18.direction, f32[9,128,256]{2,1,0:T(8,128)S(1)} %get-tuple-element.19.part, ...), custom_call_target="tpu_custom_call" | custom-call | tf_op jit(solution)/shard_map/last_kernel/pallas_call | solution.py:606
  (21 shorter events, 0.1 us)
Async XLA Ops:
  0.6 3.8 %copy-start = (f32[9,128,256]{2,1,0:T(8,128)S(1)}, f32[9,128,256]{2,1,0:T(8,128)}, u32[]{:S(2)}) copy-start(f32[9,128,256]{2,1,0:T(8,128)} %phi.7) | copy-start | bytes 3538948
  0.6 3.8 %copy-start.4 = (f32[128,256]{1,0:T(8,128)S(1)}, f32[128,256]{1,0:T(8,128)}, u32[]{:S(2)}) copy-start(f32[128,256]{1,0:T(8,128)} %vert.5) | copy-start | bytes 393220
  0.7 3.8 %copy-start.3 = (f32[128,256]{1,0:T(8,128)S(1)}, f32[128,256]{1,0:T(8,128)}, u32[]{:S(2)}) copy-start(f32[128,256]{1,0:T(8,128)} %horiz.5) | copy-start | bytes 393220
  0.7 3.8 %copy-start.1 = (f32[9,128,256]{2,1,0:T(8,128)S(1)}, f32[9,128,256]{2,1,0:T(8,128)}, u32[]{:S(2)}) copy-start(f32[9,128,256]{2,1,0:T(8,128)} %forcing.5) | copy-start | bytes 3538948
  2.7 1.8 %collective-permute-start = (f32[20,8,256]{2,1,0:T(8,128)}, f32[20,8,256]{2,1,0:T(8,128)S(1)}, u32[]{:S(2)}, u32[]{:S(2)}) collective-permute-start(f32[20,8,256]{2,1,0:T(8,128)} %get-tuple-element.13), channel_id=1, source_target_pairs={{0,4},{4,0},{8,12},{12,8},{16,20},{20,16},{24,28},{28,24},{1,5},{5... | collective-permute-start | bytes 491528 | tf_op jit(solution)/shard_map/ppermute | solution.py:492
  3.2 8.9 %copy-start.2 = (f32[6,128,256]{2,1,0:T(8,128)S(1)}, f32[6,128,256]{2,1,0:T(8,128)}, u32[]{:S(2)}) copy-start(f32[6,128,256]{2,1,0:T(8,128)} %modes.3) | copy-start | bytes 2359300
  3.2 8.9 %copy-start.5 = (f32[9,9]{1,0:T(8,128)S(1)}, f32[9,9]{1,0:T(8,128)}, u32[]{:S(2)}) copy-start(f32[9,9]{1,0:T(8,128)} %mix.1) | copy-start | bytes 976
  3.2 8.9 %copy-start.6 = (f32[6,6,2]{1,2,0:T(2,128)S(1)}, f32[6,6,2]{1,2,0:T(2,128)}, u32[]{:S(2)}) copy-start(f32[6,6,2]{1,2,0:T(2,128)} %param.16) | copy-start | bytes 868
  3.2 8.9 %copy-start.7 = (s32[128,2]{0,1:T(2,128)S(1)}, s32[128,2]{0,1:T(2,128)}, u32[]{:S(2)}) copy-start(s32[128,2]{0,1:T(2,128)} %param.15) | copy-start | bytes 3076
  3.2 8.9 %copy-start.8 = (f32[6,2]{0,1:T(2,128)S(1)}, f32[6,2]{0,1:T(2,128)}, u32[]{:S(2)}) copy-start(f32[6,2]{0,1:T(2,128)} %param.17) | copy-start | bytes 148
  3.2 1.2 %collective-permute-start.1 = (f32[20,8,256]{2,1,0:T(8,128)}, f32[20,8,256]{2,1,0:T(8,128)S(1)}, u32[]{:S(2)}, u32[]{:S(2)}) collective-permute-start(f32[20,8,256]{2,1,0:T(8,128)} %get-tuple-element.14), channel_id=1, source_target_pairs={{4,8},{12,16},{20,24},{8,4},{16,12},{24,20},{5,9},{13,17},{21,25},... | collective-permute-start | bytes 491528 | tf_op jit(solution)/shard_map/ppermute | solution.py:498
  6.8 5.3 %collective-permute-start.2 = (f32[144,128]{1,0:T(8,128)S(1)}, f32[144,128]{1,0:T(8,128)S(1)}, u32[]{:S(2)}, u32[]{:S(2)}) collective-permute-start(f32[144,128]{1,0:T(8,128)S(1)} %get-tuple-element.15), channel_id=1, source_target_pairs={{0,1},{1,0},{2,3},{3,2},{4,5},{5,4},{6,7},{7,6},{8,9},{9,8},{10,11... | collective-permute-start | bytes 221192 | tf_op jit(solution)/shard_map/ppermute | solution.py:492
  9.7 2.3 %collective-permute-start.3 = (f32[144,128]{1,0:T(8,128)S(1)}, f32[144,128]{1,0:T(8,128)S(1)}, u32[]{:S(2)}, u32[]{:S(2)}) collective-permute-start(f32[144,128]{1,0:T(8,128)S(1)} %get-tuple-element.16), channel_id=1, source_target_pairs={{1,2},{2,1},{5,6},{6,5},{9,10},{10,9},{13,14},{14,13},{17,18},{18,... | collective-permute-start | bytes 221192 | tf_op jit(solution)/shard_map/ppermute | solution.py:498
  30.7 6.4 %collective-permute-start.4 = (f32[32,128]{1,0:T(8,128)S(1)}, f32[32,128]{1,0:T(8,128)S(1)}, u32[]{:S(2)}, u32[]{:S(2)}) collective-permute-start(f32[32,128]{1,0:T(8,128)S(1)} %get-tuple-element.17), channel_id=1, source_target_pairs={{0,4},{4,0},{8,12},{12,8},{16,20},{20,16},{24,28},{28,24},{1,5},{5... | collective-permute-start | bytes 49160 | tf_op jit(solution)/shard_map/ppermute | solution.py:506
  37.1 4.4 %collective-permute-start.5 = (f32[32,128]{1,0:T(8,128)S(1)}, f32[32,128]{1,0:T(8,128)S(1)}, u32[]{:S(2)}, u32[]{:S(2)}) collective-permute-start(f32[32,128]{1,0:T(8,128)S(1)} %add.15), channel_id=1, source_target_pairs={{0,8},{4,12},{8,0},{12,4},{16,24},{20,28},{24,16},{28,20},{1,9},{5... | collective-permute-start | bytes 49160 | tf_op jit(solution)/shard_map/ppermute | solution.py:506
  41.5 4.8 %collective-permute-start.6 = (f32[32,128]{1,0:T(8,128)S(1)}, f32[32,128]{1,0:T(8,128)S(1)}, u32[]{:S(2)}, u32[]{:S(2)}) collective-permute-start(f32[32,128]{1,0:T(8,128)S(1)} %add.16), channel_id=1, source_target_pairs={{0,16},{4,20},{8,24},{12,28},{16,0},{20,4},{24,8},{28,12},{1,17},{... | collective-permute-start | bytes 49160 | tf_op jit(solution)/shard_map/ppermute | solution.py:506
  46.3 6.2 %collective-permute-start.7 = (f32[32,128]{1,0:T(8,128)S(1)}, f32[32,128]{1,0:T(8,128)S(1)}, u32[]{:S(2)}, u32[]{:S(2)}) collective-permute-start(f32[32,128]{1,0:T(8,128)S(1)} %add.17), channel_id=1, source_target_pairs={{0,1},{1,0},{2,3},{3,2},{4,5},{5,4},{6,7},{7,6},{8,9},{9,8},{10,11... | collective-permute-start | bytes 49160 | tf_op jit(solution)/shard_map/ppermute | solution.py:506
  52.5 4.7 %collective-permute-start.8 = (f32[32,128]{1,0:T(8,128)S(1)}, f32[32,128]{1,0:T(8,128)S(1)}, u32[]{:S(2)}, u32[]{:S(2)}) collective-permute-start(f32[32,128]{1,0:T(8,128)S(1)} %add.18), channel_id=1, source_target_pairs={{0,2},{1,3},{2,0},{3,1},{4,6},{5,7},{6,4},{7,5},{8,10},{9,11},{10,... | collective-permute-start | bytes 49160 | tf_op jit(solution)/shard_map/ppermute | solution.py:506

commit v2 on v0

v2 whole, which is shorter than its diff:
```python
import functools
import math

import jax
import jax.numpy as jnp
from jax import lax
from jax.experimental import pallas as pl
from jax.experimental.pallas import tpu as pltpu
from jax.sharding import PartitionSpec as P

FOOT = 8192
LANES = 128
SUB = 8
FAR = 16.0
F32 = jnp.float32
HBM = pl.BlockSpec(memory_space=pltpu.HBM)
VMEM = pl.BlockSpec(memory_space=pltpu.VMEM)
SMEM = pl.BlockSpec(memory_space=pltpu.SMEM)


def iota(shape, dim):
    return lax.broadcasted_iota(jnp.int32, shape, dim)


def tile_at(index):
    return pl.ds(pl.multiple_of(index * SUB, SUB), SUB)


def stencil(ref, row, wanted, tiles, levels, coefs, lane, wrap):
    center = [[ref[t, l, pl.ds(row, SUB), :] for l in range(levels)] for t in range(tiles)]
    result = []
    for t in wanted:
        horiz, vert = coefs[t]
        last_coef = 5.0 * horiz + vert
        mid_coef = last_coef + vert
        horiz12 = horiz * (1.0 / 12.0)
        per_level = []
        for l in range(levels):
            x = center[t][l]
            after = center[(t + 1) % tiles][l] if wrap or t + 1 < tiles else 0.0
            before = center[(t - 1) % tiles][l] if wrap or t > 0 else 0.0

            def rows_at(offset):
                return ref[t, l, pl.ds(row + offset, SUB), :]

            right1 = pltpu.roll(jnp.where(lane < 1, after, x), LANES - 1, 1)
            right2 = pltpu.roll(jnp.where(lane < 2, after, x), LANES - 2, 1)
            left1 = pltpu.roll(jnp.where(lane >= LANES - 1, before, x), 1, 1)
            left2 = pltpu.roll(jnp.where(lane >= LANES - 2, before, x), 2, 1)
            nearest = (rows_at(-1) + rows_at(1)) + (right1 + left1)
            farther = (rows_at(-2) + rows_at(2)) + (right2 + left2)
            if l == 0:
                beside = center[t][1]
            elif l == levels - 1:
                beside = center[t][l - 1]
            else:
                beside = center[t][l - 1] + center[t][l + 1]
            coef = last_coef if l == levels - 1 else mid_coef
            per_level.append(coef * x + horiz12 * (farther - FAR * nearest) - vert * beside)
        result.append(per_level)
    return result


def residual_kernel(
    phi, forcing, horiz_in, vert_in, res, near_out, far_out, phi_s, horiz, vert, sems
):
    levels, rows, cols = phi.shape
    blocks = cols // LANES
    row_tiles = rows // SUB
    lane, sub = iota((SUB, LANES), 1), iota((SUB, LANES), 0)
    zero = jnp.zeros((SUB, LANES), F32)
    pairs = [(horiz_in, horiz), (vert_in, vert)]
    for t in range(blocks):
        lanes = pl.ds(t * LANES, LANES)
        pairs.append((phi.at[:, :, lanes], phi_s.at[t, :, pl.ds(SUB, rows)]))
        pairs.append((forcing.at[:, :, lanes], res.at[t]))
    copies = [pltpu.make_async_copy(a, b, sems.at[n]) for n, (a, b) in enumerate(pairs)]
    for copy in copies:
        copy.start()
    for t in range(blocks):
        for l in range(levels):
            phi_s[t, l, 0:SUB, :] = zero
            phi_s[t, l, rows + SUB : rows + 2 * SUB, :] = zero
    for copy in copies:
        copy.wait()

    def body(i, carry):
        here = tile_at(i)
        row = pl.multiple_of(i * SUB + SUB, SUB)
        coefs = []
        for t in range(blocks):
            lanes = pl.ds(t * LANES, LANES)
            coefs.append((horiz[here, lanes], vert[here, lanes]))
        image = stencil(phi_s, row, range(blocks), blocks, levels, coefs, lane, False)
        for t in range(blocks):
            for l in range(levels):
                res[t, l, here, :] = res[t, l, here, :] - image[t][l]
        return carry

    lax.fori_loop(0, row_tiles, body, 0, unroll=2)

    even = lax.rem(lax.axis_index("gx"), 2) == 0
    upper = sub < SUB // 2
    first, last = pl.ds(0, SUB), pl.ds(rows - SUB, SUB)
    for t in range(blocks):
        lanes = pl.ds(t * LANES, LANES)
        for l in range(levels + 1):
            if l < levels:
                pairs = [
                    (res[t, l, at, :], phi_s[t, l, pl.ds(row, SUB), :])
                    for at, row in ((first, SUB), (last, rows))
                ]
            else:
                pairs = [(horiz[at, lanes], vert[at, lanes]) for at in (first, last)]
            (a_top, b_top), (a_low, b_low) = pairs
            top = jnp.where(upper, a_top, pltpu.roll(b_top, SUB // 2, 0))
            low = jnp.where(upper, pltpu.roll(b_low, SUB // 2, 0), a_low)
            near_out[l, :, lanes] = jnp.where(even, low, top)
            far_out[l, :, lanes] = jnp.where(even, top, low)


def lane_kinds(lane, levels):
    pair = (lane >= 8 * levels) & (lane < 12 * levels)
    from_left = jnp.where(pair, lane & 2, 4 - (lane & 4)) != 0
    return pair, from_left


def coef_slot(levels):
    return (12 * levels + 7) // 8 * 8


def pack_tile(res, phi, coefs, lane):
    levels = len(res)
    packed = jnp.zeros((SUB, LANES), F32)
    slots = [(8 * l, 8, value) for l, value in enumerate(res)]
    slots += [(coef_slot(levels) + 8 * n, 8, value) for n, value in enumerate(coefs)]
    slots += [(8 * levels + 4 * l, 4, value) for l, value in enumerate(phi)]
    for low, size, value in slots:
        here = (lane >= low) & (lane < low + size)
        packed = jnp.where(here, pltpu.roll(value, low + size // 2, 1), packed)
    pair = (lane >= 8 * levels) & (lane < 12 * levels)
    after = jnp.where(pair & ((lane & 3) == 0), pltpu.roll(packed, LANES - 1, 1), 0.0)
    before = jnp.where(pair & ((lane & 3) == 3), pltpu.roll(packed, 1, 1), 0.0)
    return packed - FAR * (after + before)


def inner_kernel(
    body_total, res, phi, horiz, vert, response_t, old_t, packed, table, small_s
):
    blocks, levels, rows, _ = res.shape
    cols = phi.shape[2]
    right = pl.ds(cols - LANES, LANES)
    left = pl.ds(0, LANES)
    lane = iota((SUB, LANES), 1)
    first = lane < LANES // 2

    def body(i, carry):
        here = tile_at(i)
        packed[tile_at(i + 1), :] = pack_tile(
            [jnp.where(first, res[0, l, here, :], res[blocks - 1, l, here, :]) for l in range(levels)],
            [jnp.where(first, phi[l, here, left], phi[l, here, right]) for l in range(levels)],
            [jnp.where(first, ref[here, left], ref[here, right]) for ref in (horiz, vert)],
            lane,
        )
        return carry

    lax.fori_loop(1, rows // SUB - 1, body, 0, unroll=2)

    owned, mode_count = old_t.shape
    width = table.shape[1]
    small_s[...] = jnp.zeros((LANES, LANES), F32)
    for k in range(mode_count):
        small_s[k * SUB : k * SUB + owned, 0:mode_count] = response_t[k]
        small_s[k * SUB : k * SUB + owned, mode_count : mode_count + 1] = old_t[:, k : k + 1]
    values = small_s[...].T[0:SUB, :]
    if width > LANES:
        values = jnp.concatenate([values, jnp.zeros((SUB, width - LANES), F32)], axis=1)
    wide_lane = iota((SUB, width), 1)
    me = (lax.axis_index("gx") * lax.axis_size("gy") + lax.axis_index("gy")) * owned
    for pair in range(mode_count // 2):
        tile = jnp.zeros((SUB, width), F32)
        for half in range(2):
            place = half * body_total + me
            shift = lax.rem(place - (2 * pair + half) * SUB + width, width)
            here = (wide_lane >= place) & (wide_lane < place + owned)
            tile = jnp.where(here, pltpu.roll(values, shift, 1), tile)
        table[pair * SUB : (pair + 1) * SUB, :] = tile


def edge_kernel(
    res, phi, horiz, vert, row_near, row_far, packed, edge, edge_coef, own, near_out, far_out
):
    blocks, levels, rows, _ = res.shape
    row_tiles = rows // SUB
    lane, sub = iota((SUB, LANES), 1), iota((SUB, LANES), 0)
    even = lax.rem(lax.axis_index("gx"), 2) == 0
    upper = sub < SUB // 2
    half = SUB // 2
    values = {}
    for t in range(blocks):
        lanes = pl.ds(t * LANES, LANES)
        near, far = row_near[levels, :, lanes], row_far[levels, :, lanes]
        above, below = jnp.where(even, far, near), jnp.where(even, near, far)
        h_up, v_up = jnp.where(upper, 0.0, above), jnp.where(upper, 0.0, pltpu.roll(above, half, 0))
        h_down = jnp.where(upper, below, 0.0)
        v_down = jnp.where(upper, pltpu.roll(below, half, 0), 0.0)
        edge_coef[0, 0, t], edge_coef[0, 1, t] = h_up, v_up
        edge_coef[1, 0, t], edge_coef[1, 1, t] = h_down, v_down
        first, last = pl.ds(0, SUB), pl.ds(rows - SUB, SUB)
        h_first, h_last = horiz[first, lanes], horiz[last, lanes]
        coefs = [(h_up, v_up), (h_first, vert[first, lanes]), (h_last, vert[last, lanes])]
        coefs.append((h_down, v_down))
        for n, pair in enumerate(coefs):
            values[n, t, "coef"] = pair
        scaled = [h * (1.0 / 12.0) for h, _ in coefs]

        def from_above(value):
            near_row = jnp.where(sub < 1, pltpu.roll(value, 1, 0), 0.0)
            far_row = jnp.where(sub < 2, pltpu.roll(value, 2, 0), 0.0)
            return far_row - FAR * near_row

        def from_below(value):
            near_row = jnp.where(sub >= SUB - 1, pltpu.roll(value, SUB - 1, 0), 0.0)
            far_row = jnp.where(sub >= SUB - 2, pltpu.roll(value, SUB - 2, 0), 0.0)
            return far_row - FAR * near_row

        for l in range(levels):
            near, far = row_near[l, :, lanes], row_far[l, :, lanes]
            above, below = jnp.where(even, far, near), jnp.where(even, near, far)
            res_up = jnp.where(upper, 0.0, above)
            phi_up = jnp.where(upper, 0.0, pltpu.roll(above, half, 0))
            res_down = jnp.where(upper, below, 0.0)
            phi_down = jnp.where(upper, pltpu.roll(below, half, 0), 0.0)
            phi_first, phi_last = phi[l, first, lanes], phi[l, last, lanes]
            fixed = (
                res_up - scaled[0] * from_below(phi_first),
                res[t, l, first, :] - scaled[1] * from_above(phi_up),
                res[t, l, last, :] - scaled[2] * from_below(phi_down),
                res_down - scaled[3] * from_above(phi_last),
            )
            for n, value in enumerate(fixed):
                edge[n, t, l] = value
                values[n, t, l] = value
            for n, value in enumerate((phi_up, phi_first, phi_last, phi_down)):
                values[n, t, l, "phi"] = value

    start = lane < LANES // 2
    end = blocks - 1
    tiles = [packed[i * SUB : (i + 1) * SUB, :] for i in range(row_tiles + 2)]
    for n, place in enumerate((0, 1, row_tiles, row_tiles + 1)):
        tiles[place] = pack_tile(
            [jnp.where(start, values[n, 0, l], values[n, end, l]) for l in range(levels)],
            [
                jnp.where(start, values[n, 0, l, "phi"], values[n, end, l, "phi"])
                for l in range(levels)
            ],
            [jnp.where(start, values[n, 0, "coef"][c], values[n, end, "coef"][c]) for c in range(2)],
            lane,
        )
    pair, from_left = lane_kinds(lane, levels)
    col_even = lax.rem(lax.axis_index("gy"), 2) == 0
    turned = []
    for i, tile in enumerate(tiles):
        moved = jnp.where((lane & 2) == 0, pltpu.roll(tile, LANES - 2, 1), pltpu.roll(tile, 2, 1))
        turned.append(jnp.where(pair, moved, tile))
        own[i * SUB : (i + 1) * SUB, :] = turned[i]
    fold = (row_tiles + 2) // 2
    for i in range(fold):
        other = tiles[i + fold]
        to_right = jnp.where(pair, other, pltpu.roll(other, 4, 1))
        to_right = jnp.where(from_left, turned[i], to_right)
        to_left = jnp.where(pair, other, pltpu.roll(other, LANES - 4, 1))
        to_left = jnp.where(from_left, to_left, turned[i])
        near_out[i * SUB : (i + 1) * SUB, :] = jnp.where(col_even, to_right, to_left)
        far_out[i * SUB : (i + 1) * SUB, :] = jnp.where(col_even, to_left, to_right)


def lane_sums(entries, lane):
    step = 1
    while len(entries) > 1:
        low = (lane & step) == 0
        merged = []
        for a, b in zip(entries[::2], entries[1::2]):
            if a is None:
                merged.append(None)
                continue
            b = jnp.zeros_like(a) if b is None else b
            merged.append(jnp.where(low, a, b) + pltpu.roll(jnp.where(low, b, a), step, 1))
        entries = merged
        step *= 2
    total = entries[0]
    while step < LANES:
        total = total + pltpu.roll(total, step, 1)
        step *= 2
    return total


def main_kernel(
    body_total,
    res,
    edge,
    horiz,
    vert,
    edge_coef,
    own,
    col_near,
    col_far,
    table,
    mix,
    modes,
    bodies_t,
    dir_s,
    part_s,
    message,
    res_s,
    img_s,
    horiz_s,
    vert_s,
    scale_s,
    got_s,
    sums_s,
):
    blocks, levels, rows, _ = res.shape
    mode_count = modes.shape[0]
    tiles = blocks + 1
    side = blocks
    row_tiles = rows // SUB
    base = 2 * SUB
    lane = iota((SUB, LANES), 1)
    everything = range(tiles)

    pair, from_left = lane_kinds(lane, levels)
    even = lax.rem(lax.axis_index("gy"), 2) == 0
    fold = (row_tiles + 2) // 2
    for i in range(fold):
        here = pl.ds(i * SUB, SUB)
        near, far = col_near[here, :], col_far[here, :]
        left, right = jnp.where(even, far, near), jnp.where(even, near, far)
        got_s[here, :] = jnp.where(from_left, left, right)
        left = jnp.where(pair, pltpu.roll(left, 2, 1), pltpu.roll(left, LANES - 4, 1))
        right = jnp.where(pair, pltpu.roll(right, LANES - 2, 1), pltpu.roll(right, 4, 1))
        there = pl.ds((i + fold) * SUB, SUB)
        got_s[there, :] = jnp.where(from_left, left, right)

    def first(i, inner, residuals, coefs):
        here = tile_at(i)
        there = tile_at(i + 1)
        got, mine = got_s[here, :], own[here, :]
        halo = (lane < 4) | (lane >= LANES - 4)
        slot = coef_slot(levels)
        side_coef = [
            jnp.where(halo, pltpu.roll(got, (LANES - 4 - slot - 8 * n) % LANES, 1), 0.0) for n in range(2)
        ]
        coefs = list(coefs) + [tuple(side_coef)]
        outer = (lane < 2, lane >= LANES - 2, (lane < 2) | (lane >= LANES - 2))
        scales, edges = [], []
        for t in everything:
            h, v = coefs[t]
            bottom = 5.0 * h + 2.0 * v
            inside = bottom > 0.0
            scale = jnp.where(inside, 1.0 / jnp.where(inside, bottom, 1.0), 0.0)
            scales.append(scale)
            scale_s[t, there, :] = scale
            horiz_s[t, there, :] = h
            vert_s[t, there, :] = v
            if t == side:
                mask = outer[2]
            elif blocks == 1:
                mask = outer[2]
            elif t == 0:
                mask = outer[0]
            elif t == blocks - 1:
                mask = outer[1]
            else:
                mask = None
            edges.append(None if mask is None else jnp.where(mask, h * (1.0 / 12.0), 0.0))
        weighted = [[] for _ in everything]
        for l in range(levels):
            place = (LANES - 2 - 8 * levels - 4 * l) % LANES
            theirs = pltpu.roll(got, place, 1)
            ours = pltpu.roll(mine, place, 1)
            for t in everything:
                if t == side:
                    value = pltpu.roll(got, (LANES - 4 - 8 * l) % LANES, 1) - edges[t] * ours
                else:
                    value = residuals[t][l]
                    if edges[t] is not None:
                        value = value - edges[t] * theirs
                    if inner:
                        res_s[t, l, there, :] = value
                weighted[t].append(value * scales[t])
        for t in everything:
            for l, value in enumerate(mix_levels(mix, weighted[t], levels)):
                dir_s[t, l, there, :] = value

    def own_coefs(i):
        here = tile_at(i)
        result = []
        for t in range(blocks):
            lanes = pl.ds(t * LANES, LANES)
            result.append((horiz[here, lanes], vert[here, lanes]))
        return result

    for n, i in enumerate((0, 1, row_tiles, row_tiles + 1)):
        residuals = [[edge[n, t, l] for l in range(levels)] for t in range(blocks)]
        if 1 <= i <= row_tiles:
            coefs = own_coefs(i - 1)
        else:
            coefs = [(edge_coef[n // 2, 0, t], edge_coef[n // 2, 1, t]) for t in range(blocks)]
        first(i, 1 <= i <= row_tiles, residuals, coefs)

    def first_body(i, carry):
        here = tile_at(i - 1)
        residuals = [[res[t, l, here, :] for l in range(levels)] for t in range(blocks)]
        first(i, True, residuals, own_coefs(i - 1))
        return carry

    lax.fori_loop(2, row_tiles, first_body, 0, unroll=2)

    def coefs_at(row, count):
        here = pl.ds(row, SUB)
        return [(horiz_s[t, here, :], vert_s[t, here, :]) for t in range(count)]

    def second(i, carry):
        row = pl.multiple_of(i * SUB + SUB, SUB)
        here = pl.ds(row, SUB)
        image = stencil(
            dir_s, row, everything, tiles, levels, coefs_at(row, tiles), lane, True
        )
        for t in everything:
            scale = scale_s[t, here, :]
            weighted = []
            for l in range(levels):
                img_s[t, l, here, :] = image[t][l]
                weighted.append(image[t][l] * scale)
            for l, value in enumerate(mix_levels(mix, weighted, levels)):
                part_s[t, l, here, :] = value
        return carry

    lax.fori_loop(0, row_tiles + 2, second, 0, unroll=3)

    for i in range(row_tiles):
        row = pl.ds(base + i * SUB, SUB)
        here = pl.ds(i * SUB, SUB)
        entries = [None] * 32
        for t in range(blocks):
            lanes = pl.ds(t * LANES, LANES)
            for q, field in enumerate((dir_s, part_s)):
                surface = field[t, 0, row, :]
                for k in range(mode_count):
                    entries[(2 * t + q) * SUB + k] = modes[k, here, lanes] * surface
        sums_s[here, :] = lane_sums(entries, lane)

    def third(i, totals):
        row = pl.multiple_of(i * SUB + base, SUB)
        here = pl.ds(row, SUB)
        image = stencil(
            part_s, row, range(blocks), tiles, levels, coefs_at(row, blocks), lane, True
        )
        totals = list(totals)
        for t in range(blocks):
            for l in range(levels):
                residual = res_s[t, l, here, :]
                img1 = img_s[t, l, here, :]
                img2 = image[t][l]
                products = (residual * img1, img1 * img1, residual * img2, img1 * img2, img2 * img2)
                totals = [total + product for total, product in zip(totals, products)]
        return tuple(totals)

    zero = jnp.zeros((SUB, LANES), F32)
    totals = lax.fori_loop(0, row_tiles, third, (zero,) * 5, unroll=2)

    width = message.shape[1]
    sums_t = sums_s[...].T
    forces = jnp.zeros((SUB, width), F32)
    for t in range(blocks):
        hits = body_hits(bodies_t, t, body_total, width)
        first_sums = sums_t[2 * t * SUB : (2 * t + 1) * SUB, :]
        second_sums = sums_t[(2 * t + 1) * SUB : (2 * t + 2) * SUB, :]
        forces = forces + dot_nt(first_sums, hits)
        forces = forces + pltpu.roll(dot_nt(second_sums, hits), body_total, 1)
    wide_sub, wide_lane = iota((SUB, width), 0), iota((SUB, width), 1)
    for q, total in enumerate(totals):
        forces = jnp.where((wide_sub == SUB - 2) & (wide_lane == q), jnp.sum(total), forces)
    message[0:SUB, :] = forces
    message[SUB:, :] = table[...]


def mix_levels(mix, weighted, levels):
    out = []
    for l in range(levels):
        total = (mix[l, l] + 1.0) * weighted[l]
        for m in range(levels):
            if m != l:
                total = total + mix[l, m] * weighted[m]
        out.append(total)
    return out


def body_hits(bodies_t, block, count, width):
    ids = bodies_t[block : block + 1, :]
    ids = jnp.where(ids < count, ids, -1)
    wanted = lax.broadcasted_iota(jnp.int32, (width, ids.shape[1]), 0)
    return (jnp.broadcast_to(ids, wanted.shape) == wanted).astype(F32)


def dot_nt(a, b):
    return lax.dot_general(
        a, b, (((1,), (1,)), ((), ())), precision=lax.Precision.HIGHEST, preferred_element_type=F32
    )


def last_kernel(
    body_total,
    message,
    phi,
    direction,
    part,
    modes,
    bodies_t,
    potential,
    velocity_t,
    flux,
    phi_s,
    flux_s,
    out_sems,
):
    levels, rows, cols = phi.shape
    mode_count = modes.shape[0]
    blocks = cols // LANES
    width = message.shape[1]
    owned = velocity_t.shape[0]
    main = pl.ds(2 * SUB, rows)
    top = message[0:SUB, :]

    def scalar(q):
        return top[SUB - 2 : SUB - 1, q : q + 1]

    cross_first, square_first, cross_mixed, square_mixed, square_second = [
        scalar(q) for q in range(5)
    ]
    first_step = cross_first / square_first
    next_top = (
        cross_first
        - first_step * cross_mixed
        - first_step * square_first
        + first_step * first_step * square_mixed
    )
    next_bottom = (
        square_first - 2.0 * first_step * square_mixed + first_step * first_step * square_second
    )
    second_step = next_top / next_bottom
    on_dir = first_step + second_step
    on_part = first_step * second_step

    wide_sub = lax.broadcasted_iota(jnp.int32, (SUB, width), 0)
    wide_lane = lax.broadcasted_iota(jnp.int32, (SUB, width), 1)
    foot_scale = 1.0 / math.sqrt(FOOT)
    forces = foot_scale * (on_part * pltpu.roll(top, body_total, 1) - on_dir * top)
    forces = jnp.where(wide_sub == mode_count, 1.0, forces)
    forces = jnp.where(wide_lane < body_total, forces, 0.0)
    velocity = jnp.zeros((SUB, width), F32)
    for k in range(mode_count):
        table = message[(k // 2 + 1) * SUB : (k // 2 + 2) * SUB, :]
        if k % 2:
            table = pltpu.roll(table, body_total, 1)
        value = jnp.sum(table * forces, axis=0, keepdims=True)
        velocity = jnp.where(wide_sub == k, value, velocity)

    me = (lax.axis_index("gx") * lax.axis_size("gy") + lax.axis_index("gy")) * owned
    mine = ((wide_lane == me + wide_sub) & (wide_sub < owned)).astype(F32)
    velocity_t[...] = dot_nt(mine, velocity)[0:owned, 0:mode_count]

    per_row = []
    for t in range(blocks):
        hits = body_hits(bodies_t, t, body_total, width)
        per_row.append(
            lax.dot_general(
                velocity,
                hits,
                (((1,), (0,)), ((), ())),
                precision=lax.Precision.HIGHEST,
                preferred_element_type=F32,
            )
        )
    per_row.append(jnp.zeros((LANES - blocks * SUB, rows), F32))
    spread = jnp.concatenate(per_row, axis=0).T

    for t in range(blocks):
        lanes = pl.ds(t * LANES, LANES)
        total = jnp.zeros((rows, LANES), F32)
        for k in range(mode_count):
            total = total + modes[k, :, lanes] * spread[:, t * SUB + k : t * SUB + k + 1]
        flux_s[:, lanes] = total
    flux_copy = pltpu.make_async_copy(flux_s, flux, out_sems.at[levels])
    flux_copy.start()
    outgoing = [flux_copy]
    for l in range(levels):
        for t in range(blocks):
            lanes = pl.ds(t * LANES, LANES)
            change = on_dir * direction[t, l, main, :] - on_part * part[t, l, main, :]
            phi_s[l, :, lanes] = phi[l, :, lanes] + change
        copy = pltpu.make_async_copy(phi_s.at[l], potential.at[l], out_sems.at[l])
        copy.start()
        outgoing.append(copy)
    for copy in outgoing:
        copy.wait()


def swap_near(value, axis):
    size = lax.axis_size(axis)
    return lax.ppermute(value, axis, [(i, i ^ 1) for i in range(size)])


def swap_far(value, axis):
    size = lax.axis_size(axis)
    pairs = [(i, i + 1) for i in range(1, size - 1, 2)]
    return lax.ppermute(value, axis, pairs + [(j, i) for i, j in pairs])


def sum_over(value, axes):
    for axis in axes:
        size = lax.axis_size(axis)
        step = 1
        while step < size:
            value = value + lax.ppermute(value, axis, [(i, i ^ step) for i in range(size)])
            step *= 2
    return value


def per_device(
    forcing,
    start_potential,
    horiz_coef,
    vert_coef,
    vert_mix,
    mode_shapes,
    block_body,
    response,
    velocity_old,
):
    levels, rows, cols = forcing.shape
    mode_count = mode_shapes.shape[0]
    blocks = cols // LANES
    tiles = blocks + 1
    padded = rows + 4 * SUB
    owned = velocity_old.shape[1]
    body_total = owned * lax.axis_size(("gx", "gy"))
    width = 2 * body_total
    bodies_t = block_body.T
    response_t = jnp.swapaxes(response, 1, 2)
    old_t = velocity_old.T
    limit = pltpu.CompilerParams(vmem_limit_bytes=24 * 2**20)

    def call(kernel, name, outs, ins, args, scratch=()):
        return pl.pallas_call(
            kernel,
            out_shape=tuple(jax.ShapeDtypeStruct(shape, F32) for shape, _ in outs),
            in_specs=ins,
            out_specs=tuple(spec for _, spec in outs),
            scratch_shapes=list(scratch),
            compiler_params=limit,
            name=name,
        )(*args)

    strip = (levels + 1, SUB, cols)
    inner = (blocks, levels, rows, LANES)
    res, near, far = call(
        residual_kernel,
        "residual_kernel",
        [(inner, VMEM), (strip, VMEM), (strip, VMEM)],
        [HBM] * 4,
        [
            pltpu.with_memory_space_constraint(value, pltpu.HBM)
            for value in (start_potential, forcing, horiz_coef, vert_coef)
        ],
        [
            pltpu.VMEM((blocks, levels, rows + 2 * SUB, LANES), F32),
            pltpu.VMEM((rows, cols), F32),
            pltpu.VMEM((rows, cols), F32),
            pltpu.SemaphoreType.DMA((2 + 2 * blocks,)),
        ],
    )
    row_near, row_far = swap_near(near, "gx"), swap_far(far, "gx")
    packed_shape = (rows + 2 * SUB, LANES)
    packed, table = call(
        functools.partial(inner_kernel, body_total),
        "inner_kernel",
        [(packed_shape, VMEM), ((3 * SUB, width), VMEM)],
        [VMEM] * 6,
        (res, start_potential, horiz_coef, vert_coef, response_t, old_t),
        [pltpu.VMEM((LANES, LANES), F32)],
    )
    strip = (rows // 2 + SUB, LANES)
    edge, edge_coef, own, near, far = call(
        edge_kernel,
        "edge_kernel",
        [
            ((4, blocks, levels, SUB, LANES), VMEM),
            ((2, 2, blocks, SUB, LANES), VMEM),
            (packed_shape, VMEM),
            (strip, VMEM),
            (strip, VMEM),
        ],
        [VMEM] * 7,
        (res, start_potential, horiz_coef, vert_coef, row_near, row_far, packed),
    )
    col_near, col_far = swap_near(near, "gy"), swap_far(far, "gy")

    field = (tiles, levels, padded, LANES)
    plane = pltpu.VMEM((tiles, padded, LANES), F32)
    direction, part, message = call(
        functools.partial(main_kernel, body_total),
        "main_kernel",
        [(field, VMEM), (field, VMEM), ((4 * SUB, width), VMEM)],
        [VMEM] * 9 + [SMEM] + [VMEM] * 2,
        (
            res,
            edge,
            horiz_coef,
            vert_coef,
            edge_coef,
            own,
            col_near,
            col_far,
            table,
            vert_mix,
            mode_shapes,
            bodies_t,
        ),
        [
            pltpu.VMEM((blocks, levels, padded, LANES), F32),
            pltpu.VMEM(field, F32),
            plane,
            plane,
            plane,
            pltpu.VMEM(packed_shape, F32),
            pltpu.VMEM((rows, LANES), F32),
        ],
    )
    message = sum_over(message, ("gx", "gy"))

    potential, velocity_t, flux = call(
        functools.partial(last_kernel, body_total),
        "last_kernel",
        [((levels, rows, cols), HBM), ((owned, mode_count), VMEM), ((rows, cols), HBM)],
        [VMEM] * 6,
        (message, start_potential, direction, part, mode_shapes, bodies_t),
        [
            pltpu.VMEM((levels, rows, cols), F32),
            pltpu.VMEM((rows, cols), F32),
            pltpu.SemaphoreType.DMA((levels + 1,)),
        ],
    )
    return (potential, velocity_t.T, flux)


def solution(mesh):
    return jax.shard_map(
        per_device,
        mesh=mesh,
        in_specs=(
            P(None, "gx", "gy"),
            P(None, "gx", "gy"),
            P("gx", "gy"),
            P("gx", "gy"),
            P(),
            P(None, "gx", "gy"),
            P("gx", "gy"),
            P(None, None, ("gx", "gy")),
            P(None, ("gx", "gy")),
        ),
        out_specs=(P(None, "gx", "gy"), P(None, ("gx", "gy")), P("gx", "gy")),
        check_vma=False,
    )
```

time: 259 us -> 49.9 us (0.19); the launches traced: 254 us -> 49.7 us
  blocking collectives: 149 us -> 0 us
  other arithmetic: 43.5 us -> 0.02 us
  local copies, waits for them, and re-layouts: 30.7 us -> 0.04 us
  Pallas kernels: 0 us -> 18.6 us
  starting transfers between devices: 9.79 us -> 21.2 us
  matrix products: 9.35 us -> 0 us
  between operations: 7.3 us -> 0.8 us
  waiting for transfers between devices: 4.29 us -> 9.01 us
    all_gather x1 -> x0, blocking collectives: 66 us -> none  [per_device(): all_velocity = lax.all_gather(velocity, ('gx', 'gy'), axis=1, tiled=True)]
    psum x1 -> x0, blocking collectives: 42.8 us -> none  [joint_steps(): lax.psum((jnp.sum(residual * first_img), jnp.sum(first_img * first_img),...]
    unnamed x1 -> x0, blocking collectives: 40.5 us -> none
    pallas_call x0 -> x5, Pallas kernels: none -> 18.6 us  [call(): pl.pallas_call(kernel, out_shape=tuple((jax.ShapeDtypeStruct(shape, F32)...]
    slice x10 -> x0, local copies, waits for them, and re-layouts: 11.8 us -> none  [the longest x2 5.42 us: extended(): last = lax.slice_in_dim(value, length - width, length, axis=dim)]
    ppermute x4 -> x9, starting transfers between devices: 9.79 us -> 21.2 us  [the longest x5 16.8 us: sum_over(): lax.ppermute(value, axis, [(i, i ^ step) for i in range(size)])]
    concatenate x2 -> x0, other arithmetic: 11 us -> none  [extended(): value = jnp.concatenate([before, value, after], axis=dim)]
    add x3 -> x5, other arithmetic: 11 us -> 0.02 us  [sum_over(): value + lax.ppermute(value, axis, [(i, i ^ step) for i in range(size)])]
  transfers between devices with their start and end apart: 4 -> 9, of which waited for: 2 -> 6; matrix products, arithmetic and copies ran while one was open for 3% -> 0% of each run, Pallas kernels for 0% -> 3%
where the time goes in v2:
time: 49.9 us; the launch traced here: 49.7 us
  starting transfers between devices  21.2 us (42%)
  Pallas kernels  18.6 us (37%)
  waiting for transfers between devices  9.01 us (18%)
  between operations  0.8 us (2%)
    pallas_call x5, Pallas kernels, call(): pl.pallas_call(kernel, out_shape=tuple((jax.ShapeDtypeStruct(shape, F32)...  18.6 us
    ppermute x5, starting transfers between devices, sum_over(): lax.ppermute(value, axis, [(i, i ^ step) for i in range(size)])  16.8 us
    ppermute x5, waiting for transfers between devices, sum_over(): lax.ppermute(value, axis, [(i, i ^ step) for i in range(size)])  7.7 us
    ppermute x2, starting transfers between devices, swap_near(): return lax.ppermute(value, axis, [(i, i ^ 1) for i in range(size)])  3.09 us
    ppermute x2, starting transfers between devices, swap_far(): return lax.ppermute(value, axis, pairs + [(j, i) for i, j in pairs])  1.31 us
    ppermute x2, waiting for transfers between devices, swap_near(): return lax.ppermute(value, axis, [(i, i ^ 1) for i in range(size)])  1.3 us
  transfers between devices with their start and end apart: 9, of which 6 were waited for; matrix products, arithmetic and copies ran while one was open for 0% of the time, Pallas kernels for 3%

profile of v2, /device:TPU:0, one launch (start us, length us, event | category | flops | bytes accessed | tf_op | source)
XLA Modules:
  0.0 49.7 jit_solution(13807584456131946129)
XLA Ops:
  0.7 3.8 %residual_kernel.1 = (f32[2,9,128,128]{3,2,1,0:T(8,128)S(1)}, f32[10,8,256]{2,1,0:T(8,128)S(1)}, f32[10,8,256]{2,1,0:T(8,128)S(1)}) custom-call(f32[9,128,256]{2,1,0:T(8,128)} %phi.7, f32[9,128,256]{2,1,0:T(8,128)} %forcing.1, f32[128,256]{1,0:T(8,128)} %horiz.5, f32[128,256]{1,0:T(8,128)} %vert.5), custom_call_target="tpu_custom_call" | custom-call | tf_op jit(solution)/shard_map/residual_kernel/pallas_call | solution.py:656
  4.5 0.5 %collective-permute-start = (f32[10,8,256]{2,1,0:T(8,128)S(1)}, f32[10,8,256]{2,1,0:T(8,128)S(1)}, u32[]{:S(2)}, u32[]{:S(2)}) collective-permute-start(f32[10,8,256]{2,1,0:T(8,128)S(1)} %get-tuple-element.20), channel_id=1, source_target_pairs={{0,4},{4,0},{8,12},{12,8},{16,20},{20,16},{24,28},{28,24},{1,5},{5... | collective-permute-start | bytes 245768 | tf_op jit(solution)/shard_map/ppermute | solution.py:612
  5.0 0.7 %collective-permute-start.1 = (f32[10,8,256]{2,1,0:T(8,128)S(1)}, f32[10,8,256]{2,1,0:T(8,128)S(1)}, u32[]{:S(2)}, u32[]{:S(2)}) collective-permute-start(f32[10,8,256]{2,1,0:T(8,128)S(1)} %get-tuple-element.21), channel_id=1, source_target_pairs={{4,8},{12,16},{20,24},{8,4},{16,12},{24,20},{5,9},{13,17},{21,25},... | collective-permute-start | bytes 245768 | tf_op jit(solution)/shard_map/ppermute | solution.py:618
  5.7 1.4 %inner_kernel.1 = (f32[144,128]{1,0:T(8,128)S(1)}, f32[24,128]{1,0:T(8,128)S(1)}) custom-call(f32[2,9,128,128]{3,2,1,0:T(8,128)S(1)} %get-tuple-element.19.res, f32[9,128,256]{2,1,0:T(8,128)S(1)} %copy-done, f32[128,256]{1,0:T(8,128)S(1)} %copy-done.2, f32[128,256]{1,0:T(8,128)S(1)} %copy-done.3, f32[6,2,6]{2,1,0:T(2,128)S(1)} %bitcast.4, f32[2,6]{1,0:T(2,128)S(1)} %bitcast.7), custom_call_target="tpu_custom_call" | custom-call | tf_op jit(solution)/shard_map/inner_kernel/pallas_call | solution.py:656
  7.1 0.0 collective-permute-done.row_near
  7.2 0.0 copy-start.1
  7.2 0.0 copy-start.4
  7.2 0.0 copy-start.6
  7.2 0.4 edge_kernel.1
  7.6 2.6 %collective-permute-start.2 = (f32[72,128]{1,0:T(8,128)S(1)}, f32[72,128]{1,0:T(8,128)S(1)}, u32[]{:S(2)}, u32[]{:S(2)}) collective-permute-start(f32[72,128]{1,0:T(8,128)S(1)} %get-tuple-element.26), channel_id=1, source_target_pairs={{0,1},{1,0},{2,3},{3,2},{4,5},{5,4},{6,7},{7,6},{8,9},{9,8},{10,11... | collective-permute-start | bytes 110600 | tf_op jit(solution)/shard_map/ppermute | solution.py:612
  10.2 0.7 %collective-permute-start.3 = (f32[72,128]{1,0:T(8,128)S(1)}, f32[72,128]{1,0:T(8,128)S(1)}, u32[]{:S(2)}, u32[]{:S(2)}) collective-permute-start(f32[72,128]{1,0:T(8,128)S(1)} %get-tuple-element.27), channel_id=1, source_target_pairs={{1,2},{2,1},{5,6},{6,5},{9,10},{10,9},{13,14},{14,13},{17,18},{18,... | collective-permute-start | bytes 110600 | tf_op jit(solution)/shard_map/ppermute | solution.py:618
  10.8 1.3 %collective-permute-done.2.col_near = f32[72,128]{1,0:T(8,128)S(1)} collective-permute-done((f32[72,128]{1,0:T(8,128)S(1)}, f32[72,128]{1,0:T(8,128)S(1)}, u32[]{:S(2)}, u32[]{:S(2)}) %collective-permute-start.2) | collective-permute-done | bytes 36896 | tf_op jit(solution)/shard_map/ppermute | solution.py:612
  12.1 10.4 %main_kernel.1 = (f32[3,9,160,128]{3,2,1,0:T(8,128)S(1)}, f32[3,9,160,128]{3,2,1,0:T(8,128)S(1)}, f32[32,128]{1,0:T(8,128)S(1)}) custom-call(f32[2,9,128,128]{3,2,1,0:T(8,128)S(1)} %get-tuple-element.19.res, f32[4,2,9,8,128]{4,3,2,1,0:T(8,128)S(1)} %get-tuple-element.23.edge, f32[128,256]{1,0:T(8,128)S(1)} %copy-done.2, f32[128,256]{1,0:T(8,128)S(1)} %copy-done.3, ...), custom_call_target="tpu_custom_call" | custom-call | tf_op jit(solution)/shard_map/main_kernel/pallas_call | solution.py:656
  22.5 3.5 %collective-permute-start.4 = (f32[32,128]{1,0:T(8,128)S(1)}, f32[32,128]{1,0:T(8,128)S(1)}, u32[]{:S(2)}, u32[]{:S(2)}) collective-permute-start(f32[32,128]{1,0:T(8,128)S(1)} %get-tuple-element.29), channel_id=1, source_target_pairs={{0,4},{4,0},{8,12},{12,8},{16,20},{20,16},{24,28},{28,24},{1,5},{5... | collective-permute-start | bytes 49160 | tf_op jit(solution)/shard_map/ppermute | solution.py:626
  26.0 0.8 %collective-permute-done.4 = f32[32,128]{1,0:T(8,128)S(1)} collective-permute-done((f32[32,128]{1,0:T(8,128)S(1)}, f32[32,128]{1,0:T(8,128)S(1)}, u32[]{:S(2)}, u32[]{:S(2)}) %collective-permute-start.4) | collective-permute-done | bytes 16416 | tf_op jit(solution)/shard_map/ppermute | solution.py:626
  26.8 2.5 %collective-permute-start.5 = (f32[32,128]{1,0:T(8,128)S(1)}, f32[32,128]{1,0:T(8,128)S(1)}, u32[]{:S(2)}, u32[]{:S(2)}) collective-permute-start(f32[32,128]{1,0:T(8,128)S(1)} %add.15), channel_id=1, source_target_pairs={{0,8},{4,12},{8,0},{12,4},{16,24},{20,28},{24,16},{28,20},{1,9},{5... | collective-permute-start | bytes 49160 | tf_op jit(solution)/shard_map/ppermute | solution.py:626
  29.4 1.7 %collective-permute-done.5 = f32[32,128]{1,0:T(8,128)S(1)} collective-permute-done((f32[32,128]{1,0:T(8,128)S(1)}, f32[32,128]{1,0:T(8,128)S(1)}, u32[]{:S(2)}, u32[]{:S(2)}) %collective-permute-start.5) | collective-permute-done | bytes 16416 | tf_op jit(solution)/shard_map/ppermute | solution.py:626
  31.1 3.0 %collective-permute-start.6 = (f32[32,128]{1,0:T(8,128)S(1)}, f32[32,128]{1,0:T(8,128)S(1)}, u32[]{:S(2)}, u32[]{:S(2)}) collective-permute-start(f32[32,128]{1,0:T(8,128)S(1)} %add.16), channel_id=1, source_target_pairs={{0,16},{4,20},{8,24},{12,28},{16,0},{20,4},{24,8},{28,12},{1,17},{... | collective-permute-start | bytes 49160 | tf_op jit(solution)/shard_map/ppermute | solution.py:626
  34.1 1.7 %collective-permute-done.6 = f32[32,128]{1,0:T(8,128)S(1)} collective-permute-done((f32[32,128]{1,0:T(8,128)S(1)}, f32[32,128]{1,0:T(8,128)S(1)}, u32[]{:S(2)}, u32[]{:S(2)}) %collective-permute-start.6) | collective-permute-done | bytes 16416 | tf_op jit(solution)/shard_map/ppermute | solution.py:626
  35.8 4.8 %collective-permute-start.7 = (f32[32,128]{1,0:T(8,128)S(1)}, f32[32,128]{1,0:T(8,128)S(1)}, u32[]{:S(2)}, u32[]{:S(2)}) collective-permute-start(f32[32,128]{1,0:T(8,128)S(1)} %add.17), channel_id=1, source_target_pairs={{0,1},{1,0},{2,3},{3,2},{4,5},{5,4},{6,7},{7,6},{8,9},{9,8},{10,11... | collective-permute-start | bytes 49160 | tf_op jit(solution)/shard_map/ppermute | solution.py:626
  40.6 1.7 %collective-permute-done.7 = f32[32,128]{1,0:T(8,128)S(1)} collective-permute-done((f32[32,128]{1,0:T(8,128)S(1)}, f32[32,128]{1,0:T(8,128)S(1)}, u32[]{:S(2)}, u32[]{:S(2)}) %collective-permute-start.7) | collective-permute-done | bytes 16416 | tf_op jit(solution)/shard_map/ppermute | solution.py:626
  42.4 3.0 %collective-permute-start.8 = (f32[32,128]{1,0:T(8,128)S(1)}, f32[32,128]{1,0:T(8,128)S(1)}, u32[]{:S(2)}, u32[]{:S(2)}) collective-permute-start(f32[32,128]{1,0:T(8,128)S(1)} %add.18), channel_id=1, source_target_pairs={{0,2},{1,3},{2,0},{3,1},{4,6},{5,7},{6,4},{7,5},{8,10},{9,11},{10,... | collective-permute-start | bytes 49160 | tf_op jit(solution)/shard_map/ppermute | solution.py:626
  45.4 1.7 %collective-permute-done.8 = f32[32,128]{1,0:T(8,128)S(1)} collective-permute-done((f32[32,128]{1,0:T(8,128)S(1)}, f32[32,128]{1,0:T(8,128)S(1)}, u32[]{:S(2)}, u32[]{:S(2)}) %collective-permute-start.8) | collective-permute-done | bytes 16416 | tf_op jit(solution)/shard_map/ppermute | solution.py:626
  47.1 2.7 %last_kernel.1 = (f32[9,128,256]{2,1,0:T(8,128)}, f32[2,6]{1,0:T(2,128)}, f32[128,256]{1,0:T(8,128)}) custom-call(f32[32,128]{1,0:T(8,128)S(1)} %add.19.message, f32[9,128,256]{2,1,0:T(8,128)S(1)} %copy-done, f32[3,9,160,128]{3,2,1,0:T(8,128)S(1)} %get-tuple-element.30.direction, f32[3,9,160,128]{3,2,1,0:T(8,128)S(1)} %get-tuple-element.31.part, ...), custom_call_target="tpu_custom_call" | custom-call | tf_op jit(solution)/shard_map/last_kernel/pallas_call | solution.py:656
  (20 shorter events, 0.1 us)
Async XLA Ops:
  0.6 5.0 %copy-start.3 = (f32[128,256]{1,0:T(8,128)S(1)}, f32[128,256]{1,0:T(8,128)}, u32[]{:S(2)}) copy-start(f32[128,256]{1,0:T(8,128)} %vert.5) | copy-start | bytes 393220
  0.6 5.0 %copy-start.2 = (f32[128,256]{1,0:T(8,128)S(1)}, f32[128,256]{1,0:T(8,128)}, u32[]{:S(2)}) copy-start(f32[128,256]{1,0:T(8,128)} %horiz.5) | copy-start | bytes 393220
  0.7 5.0 %copy-start = (f32[9,128,256]{2,1,0:T(8,128)S(1)}, f32[9,128,256]{2,1,0:T(8,128)}, u32[]{:S(2)}) copy-start(f32[9,128,256]{2,1,0:T(8,128)} %phi.7) | copy-start | bytes 3538948
  0.7 5.0 %copy-start.7 = (f32[6,2]{0,1:T(2,128)S(1)}, f32[6,2]{0,1:T(2,128)}, u32[]{:S(2)}) copy-start(f32[6,2]{0,1:T(2,128)} %param.17) | copy-start | bytes 148
  0.7 5.0 %copy-start.5 = (f32[6,6,2]{1,2,0:T(2,128)S(1)}, f32[6,6,2]{1,2,0:T(2,128)}, u32[]{:S(2)}) copy-start(f32[6,6,2]{1,2,0:T(2,128)} %param.16) | copy-start | bytes 868
  4.5 2.7 %collective-permute-start = (f32[10,8,256]{2,1,0:T(8,128)S(1)}, f32[10,8,256]{2,1,0:T(8,128)S(1)}, u32[]{:S(2)}, u32[]{:S(2)}) collective-permute-start(f32[10,8,256]{2,1,0:T(8,128)S(1)} %get-tuple-element.20), channel_id=1, source_target_pairs={{0,4},{4,0},{8,12},{12,8},{16,20},{20,16},{24,28},{28,24},{1,5},{5... | collective-permute-start | bytes 245768 | tf_op jit(solution)/shard_map/ppermute | solution.py:612
  5.0 2.2 %collective-permute-start.1 = (f32[10,8,256]{2,1,0:T(8,128)S(1)}, f32[10,8,256]{2,1,0:T(8,128)S(1)}, u32[]{:S(2)}, u32[]{:S(2)}) collective-permute-start(f32[10,8,256]{2,1,0:T(8,128)S(1)} %get-tuple-element.21), channel_id=1, source_target_pairs={{4,8},{12,16},{20,24},{8,4},{16,12},{24,20},{5,9},{13,17},{21,25},... | collective-permute-start | bytes 245768 | tf_op jit(solution)/shard_map/ppermute | solution.py:618
  7.2 4.9 %copy-start.1 = (f32[6,128,256]{2,1,0:T(8,128)S(1)}, f32[6,128,256]{2,1,0:T(8,128)}, u32[]{:S(2)}) copy-start(f32[6,128,256]{2,1,0:T(8,128)} %modes.3) | copy-start | bytes 2359300
  7.2 4.9 %copy-start.4 = (f32[9,9]{1,0:T(8,128)S(1)}, f32[9,9]{1,0:T(8,128)}, u32[]{:S(2)}) copy-start(f32[9,9]{1,0:T(8,128)} %mix.1) | copy-start | bytes 976
  7.2 4.9 %copy-start.6 = (s32[128,2]{0,1:T(2,128)S(1)}, s32[128,2]{0,1:T(2,128)}, u32[]{:S(2)}) copy-start(s32[128,2]{0,1:T(2,128)} %param.15) | copy-start | bytes 3076
  7.6 4.5 %collective-permute-start.2 = (f32[72,128]{1,0:T(8,128)S(1)}, f32[72,128]{1,0:T(8,128)S(1)}, u32[]{:S(2)}, u32[]{:S(2)}) collective-permute-start(f32[72,128]{1,0:T(8,128)S(1)} %get-tuple-element.26), channel_id=1, source_target_pairs={{0,1},{1,0},{2,3},{3,2},{4,5},{5,4},{6,7},{7,6},{8,9},{9,8},{10,11... | collective-permute-start | bytes 110600 | tf_op jit(solution)/shard_map/ppermute | solution.py:612
  10.2 1.9 %collective-permute-start.3 = (f32[72,128]{1,0:T(8,128)S(1)}, f32[72,128]{1,0:T(8,128)S(1)}, u32[]{:S(2)}, u32[]{:S(2)}) collective-permute-start(f32[72,128]{1,0:T(8,128)S(1)} %get-tuple-element.27), channel_id=1, source_target_pairs={{1,2},{2,1},{5,6},{6,5},{9,10},{10,9},{13,14},{14,13},{17,18},{18,... | collective-permute-start | bytes 110600 | tf_op jit(solution)/shard_map/ppermute | solution.py:618
  22.5 4.3 %collective-permute-start.4 = (f32[32,128]{1,0:T(8,128)S(1)}, f32[32,128]{1,0:T(8,128)S(1)}, u32[]{:S(2)}, u32[]{:S(2)}) collective-permute-start(f32[32,128]{1,0:T(8,128)S(1)} %get-tuple-element.29), channel_id=1, source_target_pairs={{0,4},{4,0},{8,12},{12,8},{16,20},{20,16},{24,28},{28,24},{1,5},{5... | collective-permute-start | bytes 49160 | tf_op jit(solution)/shard_map/ppermute | solution.py:626
  26.8 4.3 %collective-permute-start.5 = (f32[32,128]{1,0:T(8,128)S(1)}, f32[32,128]{1,0:T(8,128)S(1)}, u32[]{:S(2)}, u32[]{:S(2)}) collective-permute-start(f32[32,128]{1,0:T(8,128)S(1)} %add.15), channel_id=1, source_target_pairs={{0,8},{4,12},{8,0},{12,4},{16,24},{20,28},{24,16},{28,20},{1,9},{5... | collective-permute-start | bytes 49160 | tf_op jit(solution)/shard_map/ppermute | solution.py:626
  31.1 4.8 %collective-permute-start.6 = (f32[32,128]{1,0:T(8,128)S(1)}, f32[32,128]{1,0:T(8,128)S(1)}, u32[]{:S(2)}, u32[]{:S(2)}) collective-permute-start(f32[32,128]{1,0:T(8,128)S(1)} %add.16), channel_id=1, source_target_pairs={{0,16},{4,20},{8,24},{12,28},{16,0},{20,4},{24,8},{28,12},{1,17},{... | collective-permute-start | bytes 49160 | tf_op jit(solution)/shard_map/ppermute | solution.py:626
  35.8 6.5 %collective-permute-start.7 = (f32[32,128]{1,0:T(8,128)S(1)}, f32[32,128]{1,0:T(8,128)S(1)}, u32[]{:S(2)}, u32[]{:S(2)}) collective-permute-start(f32[32,128]{1,0:T(8,128)S(1)} %add.17), channel_id=1, source_target_pairs={{0,1},{1,0},{2,3},{3,2},{4,5},{5,4},{6,7},{7,6},{8,9},{9,8},{10,11... | collective-permute-start | bytes 49160 | tf_op jit(solution)/shard_map/ppermute | solution.py:626
  42.4 4.7 %collective-permute-start.8 = (f32[32,128]{1,0:T(8,128)S(1)}, f32[32,128]{1,0:T(8,128)S(1)}, u32[]{:S(2)}, u32[]{:S(2)}) collective-permute-start(f32[32,128]{1,0:T(8,128)S(1)} %add.18), channel_id=1, source_target_pairs={{0,2},{1,3},{2,0},{3,1},{4,6},{5,7},{6,4},{7,5},{8,10},{9,11},{10,... | collective-permute-start | bytes 49160 | tf_op jit(solution)/shard_map/ppermute | solution.py:626

commit v3 on v2

--- a/solution.py
+++ b/solution.py
@@ -27,9 +27,11 @@
 
 
 def stencil(ref, row, wanted, tiles, levels, coefs, lane, wrap):
-    center = [[ref[t, l, pl.ds(row, SUB), :] for l in range(levels)] for t in range(tiles)]
-    result = []
     for t in wanted:
+        center = {
+            u: [ref[u % tiles, l, pl.ds(row, SUB), :] for l in range(levels)]
+            for u in (t - 1, t, t + 1)
+        }
         horiz, vert = coefs[t]
         last_coef = 5.0 * horiz + vert
         mid_coef = last_coef + vert
@@ -37,8 +39,8 @@
         per_level = []
         for l in range(levels):
             x = center[t][l]
-            after = center[(t + 1) % tiles][l] if wrap or t + 1 < tiles else 0.0
-            before = center[(t - 1) % tiles][l] if wrap or t > 0 else 0.0
+            after = center[t + 1][l] if wrap or t + 1 < tiles else 0.0
+            before = center[t - 1][l] if wrap or t > 0 else 0.0
 
             def rows_at(offset):
                 return ref[t, l, pl.ds(row + offset, SUB), :]
@@ -57,66 +59,57 @@
                 beside = center[t][l - 1] + center[t][l + 1]
             coef = last_coef if l == levels - 1 else mid_coef
             per_level.append(coef * x + horiz12 * (farther - FAR * nearest) - vert * beside)
-        result.append(per_level)
-    return result
-
-
-def residual_kernel(
-    phi, forcing, horiz_in, vert_in, res, near_out, far_out, phi_s, horiz, vert, sems
-):
+        yield t, per_level
+
+
+def strip_kernel(phi, forcing, horiz_in, vert_in, near_out, far_out, phi_s, res_s, horiz, vert, sems):
     levels, rows, cols = phi.shape
     blocks = cols // LANES
-    row_tiles = rows // SUB
     lane, sub = iota((SUB, LANES), 1), iota((SUB, LANES), 0)
-    zero = jnp.zeros((SUB, LANES), F32)
-    pairs = [(horiz_in, horiz), (vert_in, vert)]
-    for t in range(blocks):
-        lanes = pl.ds(t * LANES, LANES)
-        pairs.append((phi.at[:, :, lanes], phi_s.at[t, :, pl.ds(SUB, rows)]))
-        pairs.append((forcing.at[:, :, lanes], res.at[t]))
+    pairs = []
+    for end, row in enumerate((0, rows - SUB)):
+        here = pl.ds(row, SUB)
+        pairs.append((horiz_in.at[here], horiz.at[end]))
+        pairs.append((vert_in.at[here], vert.at[end]))
+        for t in range(blocks):
+            lanes = pl.ds(t * LANES, LANES)
+            pairs.append((phi.at[:, here, lanes], phi_s.at[end, t, :, pl.ds(SUB, SUB)]))
+            pairs.append((forcing.at[:, here, lanes], res_s.at[end, t]))
     copies = [pltpu.make_async_copy(a, b, sems.at[n]) for n, (a, b) in enumerate(pairs)]
     for copy in copies:
         copy.start()
-    for t in range(blocks):
-        for l in range(levels):
-            phi_s[t, l, 0:SUB, :] = zero
-            phi_s[t, l, rows + SUB : rows + 2 * SUB, :] = zero
+    zero = jnp.zeros((SUB, LANES), F32)
+    for end in range(2):
+        for t in range(blocks):
+            for l in range(levels):
+                phi_s[end, t, l, 0:SUB, :] = zero
+                phi_s[end, t, l, 2 * SUB : 3 * SUB, :] = zero
     for copy in copies:
         copy.wait()
-
-    def body(i, carry):
-        here = tile_at(i)
-        row = pl.multiple_of(i * SUB + SUB, SUB)
-        coefs = []
-        for t in range(blocks):
-            lanes = pl.ds(t * LANES, LANES)
-            coefs.append((horiz[here, lanes], vert[here, lanes]))
-        image = stencil(phi_s, row, range(blocks), blocks, levels, coefs, lane, False)
-        for t in range(blocks):
-            for l in range(levels):
-                res[t, l, here, :] = res[t, l, here, :] - image[t][l]
-        return carry
-
-    lax.fori_loop(0, row_tiles, body, 0, unroll=2)
-
     even = lax.rem(lax.axis_index("gx"), 2) == 0
     upper = sub < SUB // 2
-    first, last = pl.ds(0, SUB), pl.ds(rows - SUB, SUB)
-    for t in range(blocks):
+    kept = []
+    for end in range(2):
+        coefs = [
+            (horiz[end, :, t * LANES : (t + 1) * LANES], vert[end, :, t * LANES : (t + 1) * LANES])
+            for t in range(blocks)
+        ]
+        image = stencil(phi_s.at[end], SUB, range(blocks), blocks, levels, coefs, lane, False)
+        strips = {}
+        for t, image_t in image:
+            for l in range(levels):
+                potential = phi_s[end, t, l, SUB : 2 * SUB, :]
+                strips[t, l] = (res_s[end, t, l] - image_t[l], potential)
+            strips[t, levels] = coefs[t]
+        kept.append(strips)
+    for place, (a_top, b_top) in kept[0].items():
+        a_low, b_low = kept[1][place]
+        t, l = place
         lanes = pl.ds(t * LANES, LANES)
-        for l in range(levels + 1):
-            if l < levels:
-                pairs = [
-                    (res[t, l, at, :], phi_s[t, l, pl.ds(row, SUB), :])
-                    for at, row in ((first, SUB), (last, rows))
-                ]
-            else:
-                pairs = [(horiz[at, lanes], vert[at, lanes]) for at in (first, last)]
-            (a_top, b_top), (a_low, b_low) = pairs
-            top = jnp.where(upper, a_top, pltpu.roll(b_top, SUB // 2, 0))
-            low = jnp.where(upper, pltpu.roll(b_low, SUB // 2, 0), a_low)
-            near_out[l, :, lanes] = jnp.where(even, low, top)
-            far_out[l, :, lanes] = jnp.where(even, top, low)
+        top = jnp.where(upper, a_top, pltpu.roll(b_top, SUB // 2, 0))
+        low = jnp.where(upper, pltpu.roll(b_low, SUB // 2, 0), a_low)
+        near_out[l, :, lanes] = jnp.where(even, low, top)
+        far_out[l, :, lanes] = jnp.where(even, top, low)
 
 
 def lane_kinds(lane, levels):
@@ -145,14 +138,36 @@
 
 
 def inner_kernel(
-    body_total, res, phi, horiz, vert, response_t, old_t, packed, table, small_s
+    body_total, phi, forcing, horiz, vert, response_t, old_t, res, packed, table, phi_s, small_s
 ):
     blocks, levels, rows, _ = res.shape
     cols = phi.shape[2]
+    zero = jnp.zeros((SUB, LANES), F32)
+    for t in range(blocks):
+        for l in range(levels):
+            phi_s[t, l, 0:SUB, :] = zero
+            phi_s[t, l, rows + SUB : rows + 2 * SUB, :] = zero
+            phi_s[t, l, SUB : rows + SUB, :] = phi[l, :, t * LANES : (t + 1) * LANES]
     right = pl.ds(cols - LANES, LANES)
     left = pl.ds(0, LANES)
     lane = iota((SUB, LANES), 1)
     first = lane < LANES // 2
+
+    def residual(i, carry):
+        here = tile_at(i)
+        row = pl.multiple_of(i * SUB + SUB, SUB)
+        coefs = []
+        for t in range(blocks):
+            lanes = pl.ds(t * LANES, LANES)
+            coefs.append((horiz[here, lanes], vert[here, lanes]))
+        image = stencil(phi_s, row, range(blocks), blocks, levels, coefs, lane, False)
+        for t, image_t in image:
+            for l in range(levels):
+                own = forcing[l, here, pl.ds(t * LANES, LANES)]
+                res[t, l, here, :] = own - image_t[l]
+        return carry
+
+    lax.fori_loop(0, rows // SUB, residual, 0, unroll=2)
 
     def body(i, carry):
         here = tile_at(i)
@@ -164,7 +179,7 @@
         )
         return carry
 
-    lax.fori_loop(1, rows // SUB - 1, body, 0, unroll=2)
+    lax.fori_loop(1, rows // SUB - 1, body, 0, unroll=7)
 
     owned, mode_count = old_t.shape
     width = table.shape[1]
@@ -288,11 +303,7 @@
             merged.append(jnp.where(low, a, b) + pltpu.roll(jnp.where(low, b, a), step, 1))
         entries = merged
         step *= 2
-    total = entries[0]
-    while step < LANES:
-        total = total + pltpu.roll(total, step, 1)
-        step *= 2
-    return total
+    return entries[0]
 
 
 def main_kernel(
@@ -415,7 +426,7 @@
         first(i, True, residuals, own_coefs(i - 1))
         return carry
 
-    lax.fori_loop(2, row_tiles, first_body, 0, unroll=2)
+    lax.fori_loop(2, row_tiles, first_body, 0, unroll=7)
 
     def coefs_at(row, count):
         here = pl.ds(row, SUB)
@@ -427,12 +438,12 @@
         image = stencil(
             dir_s, row, everything, tiles, levels, coefs_at(row, tiles), lane, True
         )
-        for t in everything:
+        for t, image_t in image:
             scale = scale_s[t, here, :]
             weighted = []
             for l in range(levels):
-                img_s[t, l, here, :] = image[t][l]
-                weighted.append(image[t][l] * scale)
+                img_s[t, l, here, :] = image_t[l]
+                weighted.append(image_t[l] * scale)
             for l, value in enumerate(mix_levels(mix, weighted, levels)):
                 part_s[t, l, here, :] = value
         return carry
@@ -442,7 +453,7 @@
     for i in range(row_tiles):
         row = pl.ds(base + i * SUB, SUB)
         here = pl.ds(i * SUB, SUB)
-        entries = [None] * 32
+        entries = [None] * (LANES // 4)
         for t in range(blocks):
             lanes = pl.ds(t * LANES, LANES)
             for q, field in enumerate((dir_s, part_s)):
@@ -458,11 +469,11 @@
             part_s, row, range(blocks), tiles, levels, coefs_at(row, blocks), lane, True
         )
         totals = list(totals)
-        for t in range(blocks):
+        for t, image_t in image:
             for l in range(levels):
                 residual = res_s[t, l, here, :]
                 img1 = img_s[t, l, here, :]
-                img2 = image[t][l]
+                img2 = image_t[l]
                 products = (residual * img1, img1 * img1, residual * img2, img1 * img2, img2 * img2)
                 totals = [total + product for total, product in zip(totals, products)]
         return tuple(totals)
@@ -472,6 +483,7 @@
 
     width = message.shape[1]
     sums_t = sums_s[...].T
+    sums_t = sum(sums_t[n * (LANES // 4) : (n + 1) * (LANES // 4), :] for n in range(4))
     forces = jnp.zeros((SUB, width), F32)
     for t in range(blocks):
         hits = body_hits(bodies_t, t, body_total, width)
@@ -479,10 +491,14 @@
         second_sums = sums_t[(2 * t + 1) * SUB : (2 * t + 2) * SUB, :]
         forces = forces + dot_nt(first_sums, hits)
         forces = forces + pltpu.roll(dot_nt(second_sums, hits), body_total, 1)
-    wide_sub, wide_lane = iota((SUB, width), 0), iota((SUB, width), 1)
+    wide_sub = iota((SUB, width), 0)
+    gathered = jnp.zeros((SUB, LANES), F32)
     for q, total in enumerate(totals):
-        forces = jnp.where((wide_sub == SUB - 2) & (wide_lane == q), jnp.sum(total), forces)
-    message[0:SUB, :] = forces
+        gathered = jnp.where(lane == q, jnp.sum(total, axis=1, keepdims=True), gathered)
+    gathered = jnp.sum(gathered, axis=0, keepdims=True)
+    if width > LANES:
+        gathered = jnp.concatenate([gathered, jnp.zeros((1, width - LANES), F32)], axis=1)
+    message[0:SUB, :] = jnp.where(wide_sub == SUB - 2, gathered, forces)
     message[SUB:, :] = table[...]
 
 
@@ -553,6 +569,16 @@
     on_dir = first_step + second_step
     on_part = first_step * second_step
 
+    outgoing = []
+    for l in range(levels):
+        for t in range(blocks):
+            lanes = pl.ds(t * LANES, LANES)
+            change = on_dir * direction[t, l, main, :] - on_part * part[t, l, main, :]
+            phi_s[l, :, lanes] = phi[l, :, lanes] + change
+        copy = pltpu.make_async_copy(phi_s.at[l], potential.at[l], out_sems.at[l])
+        copy.start()
+        outgoing.append(copy)
+
     wide_sub = lax.broadcasted_iota(jnp.int32, (SUB, width), 0)
     wide_lane = lax.broadcasted_iota(jnp.int32, (SUB, width), 1)
     foot_scale = 1.0 / math.sqrt(FOOT)
@@ -594,15 +620,7 @@
         flux_s[:, lanes] = total
     flux_copy = pltpu.make_async_copy(flux_s, flux, out_sems.at[levels])
     flux_copy.start()
-    outgoing = [flux_copy]
-    for l in range(levels):
-        for t in range(blocks):
-            lanes = pl.ds(t * LANES, LANES)
-            change = on_dir * direction[t, l, main, :] - on_part * part[t, l, main, :]
-            phi_s[l, :, lanes] = phi[l, :, lanes] + change
-        copy = pltpu.make_async_copy(phi_s.at[l], potential.at[l], out_sems.at[l])
-        copy.start()
-        outgoing.append(copy)
+    outgoing.append(flux_copy)
     for copy in outgoing:
         copy.wait()
 
@@ -665,31 +683,35 @@
 
     strip = (levels + 1, SUB, cols)
     inner = (blocks, levels, rows, LANES)
-    res, near, far = call(
-        residual_kernel,
-        "residual_kernel",
-        [(inner, VMEM), (strip, VMEM), (strip, VMEM)],
+    near, far = call(
+        strip_kernel,
+        "strip_kernel",
+        [(strip, VMEM), (strip, VMEM)],
         [HBM] * 4,
         [
             pltpu.with_memory_space_constraint(value, pltpu.HBM)
             for value in (start_potential, forcing, horiz_coef, vert_coef)
         ],
         [
-            pltpu.VMEM((blocks, levels, rows + 2 * SUB, LANES), F32),
-            pltpu.VMEM((rows, cols), F32),
-            pltpu.VMEM((rows, cols), F32),
-            pltpu.SemaphoreType.DMA((2 + 2 * blocks,)),
+            pltpu.VMEM((2, blocks, levels, 3 * SUB, LANES), F32),
+            pltpu.VMEM((2, blocks, levels, SUB, LANES), F32),
+            pltpu.VMEM((2, SUB, cols), F32),
+            pltpu.VMEM((2, SUB, cols), F32),
+            pltpu.SemaphoreType.DMA((4 + 4 * blocks,)),
         ],
     )
     row_near, row_far = swap_near(near, "gx"), swap_far(far, "gx")
     packed_shape = (rows + 2 * SUB, LANES)
-    packed, table = call(
+    res, packed, table = call(
         functools.partial(inner_kernel, body_total),
         "inner_kernel",
-        [(packed_shape, VMEM), ((3 * SUB, width), VMEM)],
+        [(inner, VMEM), (packed_shape, VMEM), ((3 * SUB, width), VMEM)],
         [VMEM] * 6,
-        (res, start_potential, horiz_coef, vert_coef, response_t, old_t),
-        [pltpu.VMEM((LANES, LANES), F32)],
+        (start_potential, forcing, horiz_coef, vert_coef, response_t, old_t),
+        [
+            pltpu.VMEM((blocks, levels, rows + 2 * SUB, LANES), F32),
+            pltpu.VMEM((LANES, LANES), F32),
+        ],
     )
     strip = (rows // 2 + SUB, LANES)
     edge, edge_coef, own, near, far = call(

time: 49.9 us -> 47 us (0.942)
  Pallas kernels: 18.6 us -> 17.2 us
  starting transfers between devices: 21.2 us -> 19.8 us
    pallas_call x5, Pallas kernels: 18.6 us -> 17.2 us  [call(): pl.pallas_call(kernel, out_shape=tuple((jax.ShapeDtypeStruct(shape, F32)...]
    ppermute x5, starting transfers between devices: 16.8 us -> 15.4 us  [sum_over(): lax.ppermute(value, axis, [(i, i ^ step) for i in range(size)])]
  transfers between devices with their start and end apart: 9 -> 9, of which waited for: 6 -> 6; matrix products, arithmetic and copies ran while one was open for 0% -> 0% of each run, Pallas kernels for 3% -> 6%
where the time goes in v3:
time: 47 us; the launch traced here: 46.9 us
  starting transfers between devices  19.8 us (42%)
  Pallas kernels  17.2 us (37%)
  waiting for transfers between devices  9.01 us (19%)
  between operations  0.82 us (2%)
    pallas_call x5, Pallas kernels, call(): pl.pallas_call(kernel, out_shape=tuple((jax.ShapeDtypeStruct(shape, F32)...  17.2 us
    ppermute x5, starting transfers between devices, sum_over(): lax.ppermute(value, axis, [(i, i ^ step) for i in range(size)])  15.4 us
    ppermute x5, waiting for transfers between devices, sum_over(): lax.ppermute(value, axis, [(i, i ^ step) for i in range(size)])  7.7 us
    ppermute x2, starting transfers between devices, swap_near(): return lax.ppermute(value, axis, [(i, i ^ 1) for i in range(size)])  3.09 us
    ppermute x2, starting transfers between devices, swap_far(): return lax.ppermute(value, axis, pairs + [(j, i) for i, j in pairs])  1.31 us
    ppermute x2, waiting for transfers between devices, swap_near(): return lax.ppermute(value, axis, [(i, i ^ 1) for i in range(size)])  1.3 us
  transfers between devices with their start and end apart: 9, of which 6 were waited for; matrix products, arithmetic and copies ran while one was open for 0% of the time, Pallas kernels for 6%

profile of v3, /device:TPU:0, one launch (start us, length us, event | category | flops | bytes accessed | tf_op | source)
XLA Modules:
  0.0 46.9 jit_solution(13221441704189995831)
XLA Ops:
  0.7 1.4 %strip_kernel.1 = (f32[10,8,256]{2,1,0:T(8,128)S(1)}, f32[10,8,256]{2,1,0:T(8,128)S(1)}) custom-call(f32[9,128,256]{2,1,0:T(8,128)} %phi.7, f32[9,128,256]{2,1,0:T(8,128)} %forcing.3, f32[128,256]{1,0:T(8,128)} %horiz.5, f32[128,256]{1,0:T(8,128)} %vert.5), custom_call_target="tpu_custom_call" | custom-call | tf_op jit(solution)/shard_map/strip_kernel/pallas_call | solution.py:674
  2.1 0.5 %collective-permute-start = (f32[10,8,256]{2,1,0:T(8,128)S(1)}, f32[10,8,256]{2,1,0:T(8,128)S(1)}, u32[]{:S(2)}, u32[]{:S(2)}) collective-permute-start(f32[10,8,256]{2,1,0:T(8,128)S(1)} %get-tuple-element.20), channel_id=1, source_target_pairs={{0,4},{4,0},{8,12},{12,8},{16,20},{20,16},{24,28},{28,24},{1,5},{5... | collective-permute-start | bytes 245768 | tf_op jit(solution)/shard_map/ppermute | solution.py:630
  2.6 0.7 %collective-permute-start.1 = (f32[10,8,256]{2,1,0:T(8,128)S(1)}, f32[10,8,256]{2,1,0:T(8,128)S(1)}, u32[]{:S(2)}, u32[]{:S(2)}) collective-permute-start(f32[10,8,256]{2,1,0:T(8,128)S(1)} %get-tuple-element.21), channel_id=1, source_target_pairs={{4,8},{12,16},{20,24},{8,4},{16,12},{24,20},{5,9},{13,17},{21,25},... | collective-permute-start | bytes 245768 | tf_op jit(solution)/shard_map/ppermute | solution.py:636
  3.4 2.9 %inner_kernel.1 = (f32[2,9,128,128]{3,2,1,0:T(8,128)S(1)}, f32[144,128]{1,0:T(8,128)S(1)}, f32[24,128]{1,0:T(8,128)S(1)}) custom-call(f32[9,128,256]{2,1,0:T(8,128)S(1)} %copy-done, f32[9,128,256]{2,1,0:T(8,128)S(1)} %copy-done.1, f32[128,256]{1,0:T(8,128)S(1)} %copy-done.3, f32[128,256]{1,0:T(8,128)S(1)} %copy-done.4, f32[6,2,6]{2,1,0:T(2,128)S(1)} %bitcast.4, ...), custom_call_target="tpu_custom_call" | custom-call | tf_op jit(solution)/shard_map/inner_kernel/pallas_call | solution.py:674
  6.2 0.0 collective-permute-done.row_near
  6.2 0.0 copy-start.2
  6.3 0.0 copy-start.5
  6.3 0.0 copy-start.7
  6.3 0.4 edge_kernel.1
  6.7 2.6 %collective-permute-start.2 = (f32[72,128]{1,0:T(8,128)S(1)}, f32[72,128]{1,0:T(8,128)S(1)}, u32[]{:S(2)}, u32[]{:S(2)}) collective-permute-start(f32[72,128]{1,0:T(8,128)S(1)} %get-tuple-element.26), channel_id=1, source_target_pairs={{0,1},{1,0},{2,3},{3,2},{4,5},{5,4},{6,7},{7,6},{8,9},{9,8},{10,11... | collective-permute-start | bytes 110600 | tf_op jit(solution)/shard_map/ppermute | solution.py:630
  9.2 0.7 %collective-permute-start.3 = (f32[72,128]{1,0:T(8,128)S(1)}, f32[72,128]{1,0:T(8,128)S(1)}, u32[]{:S(2)}, u32[]{:S(2)}) collective-permute-start(f32[72,128]{1,0:T(8,128)S(1)} %get-tuple-element.27), channel_id=1, source_target_pairs={{1,2},{2,1},{5,6},{6,5},{9,10},{10,9},{13,14},{14,13},{17,18},{18,... | collective-permute-start | bytes 110600 | tf_op jit(solution)/shard_map/ppermute | solution.py:636
  9.9 1.3 %collective-permute-done.2.col_near = f32[72,128]{1,0:T(8,128)S(1)} collective-permute-done((f32[72,128]{1,0:T(8,128)S(1)}, f32[72,128]{1,0:T(8,128)S(1)}, u32[]{:S(2)}, u32[]{:S(2)}) %collective-permute-start.2) | collective-permute-done | bytes 36896 | tf_op jit(solution)/shard_map/ppermute | solution.py:630
  11.2 10.2 %main_kernel.1 = (f32[3,9,160,128]{3,2,1,0:T(8,128)S(1)}, f32[3,9,160,128]{3,2,1,0:T(8,128)S(1)}, f32[32,128]{1,0:T(8,128)S(1)}) custom-call(f32[2,9,128,128]{3,2,1,0:T(8,128)S(1)} %get-tuple-element.19.res, f32[4,2,9,8,128]{4,3,2,1,0:T(8,128)S(1)} %get-tuple-element.23.edge, f32[128,256]{1,0:T(8,128)S(1)} %copy-done.3, f32[128,256]{1,0:T(8,128)S(1)} %copy-done.4, ...), custom_call_target="tpu_custom_call" | custom-call | tf_op jit(solution)/shard_map/main_kernel/pallas_call | solution.py:674
  21.4 2.3 %collective-permute-start.4 = (f32[32,128]{1,0:T(8,128)S(1)}, f32[32,128]{1,0:T(8,128)S(1)}, u32[]{:S(2)}, u32[]{:S(2)}) collective-permute-start(f32[32,128]{1,0:T(8,128)S(1)} %get-tuple-element.29), channel_id=1, source_target_pairs={{0,4},{4,0},{8,12},{12,8},{16,20},{20,16},{24,28},{28,24},{1,5},{5... | collective-permute-start | bytes 49160 | tf_op jit(solution)/shard_map/ppermute | solution.py:644
  23.7 0.8 %collective-permute-done.4 = f32[32,128]{1,0:T(8,128)S(1)} collective-permute-done((f32[32,128]{1,0:T(8,128)S(1)}, f32[32,128]{1,0:T(8,128)S(1)}, u32[]{:S(2)}, u32[]{:S(2)}) %collective-permute-start.4) | collective-permute-done | bytes 16416 | tf_op jit(solution)/shard_map/ppermute | solution.py:644
  24.5 2.5 %collective-permute-start.5 = (f32[32,128]{1,0:T(8,128)S(1)}, f32[32,128]{1,0:T(8,128)S(1)}, u32[]{:S(2)}, u32[]{:S(2)}) collective-permute-start(f32[32,128]{1,0:T(8,128)S(1)} %add.15), channel_id=1, source_target_pairs={{0,8},{4,12},{8,0},{12,4},{16,24},{20,28},{24,16},{28,20},{1,9},{5... | collective-permute-start | bytes 49160 | tf_op jit(solution)/shard_map/ppermute | solution.py:644
  27.0 1.7 %collective-permute-done.5 = f32[32,128]{1,0:T(8,128)S(1)} collective-permute-done((f32[32,128]{1,0:T(8,128)S(1)}, f32[32,128]{1,0:T(8,128)S(1)}, u32[]{:S(2)}, u32[]{:S(2)}) %collective-permute-start.5) | collective-permute-done | bytes 16416 | tf_op jit(solution)/shard_map/ppermute | solution.py:644
  28.7 3.0 %collective-permute-start.6 = (f32[32,128]{1,0:T(8,128)S(1)}, f32[32,128]{1,0:T(8,128)S(1)}, u32[]{:S(2)}, u32[]{:S(2)}) collective-permute-start(f32[32,128]{1,0:T(8,128)S(1)} %add.16), channel_id=1, source_target_pairs={{0,16},{4,20},{8,24},{12,28},{16,0},{20,4},{24,8},{28,12},{1,17},{... | collective-permute-start | bytes 49160 | tf_op jit(solution)/shard_map/ppermute | solution.py:644
  31.8 1.7 %collective-permute-done.6 = f32[32,128]{1,0:T(8,128)S(1)} collective-permute-done((f32[32,128]{1,0:T(8,128)S(1)}, f32[32,128]{1,0:T(8,128)S(1)}, u32[]{:S(2)}, u32[]{:S(2)}) %collective-permute-start.6) | collective-permute-done | bytes 16416 | tf_op jit(solution)/shard_map/ppermute | solution.py:644
  33.5 4.5 %collective-permute-start.7 = (f32[32,128]{1,0:T(8,128)S(1)}, f32[32,128]{1,0:T(8,128)S(1)}, u32[]{:S(2)}, u32[]{:S(2)}) collective-permute-start(f32[32,128]{1,0:T(8,128)S(1)} %add.17), channel_id=1, source_target_pairs={{0,1},{1,0},{2,3},{3,2},{4,5},{5,4},{6,7},{7,6},{8,9},{9,8},{10,11... | collective-permute-start | bytes 49160 | tf_op jit(solution)/shard_map/ppermute | solution.py:644
  38.0 1.7 %collective-permute-done.7 = f32[32,128]{1,0:T(8,128)S(1)} collective-permute-done((f32[32,128]{1,0:T(8,128)S(1)}, f32[32,128]{1,0:T(8,128)S(1)}, u32[]{:S(2)}, u32[]{:S(2)}) %collective-permute-start.7) | collective-permute-done | bytes 16416 | tf_op jit(solution)/shard_map/ppermute | solution.py:644
  39.8 3.0 %collective-permute-start.8 = (f32[32,128]{1,0:T(8,128)S(1)}, f32[32,128]{1,0:T(8,128)S(1)}, u32[]{:S(2)}, u32[]{:S(2)}) collective-permute-start(f32[32,128]{1,0:T(8,128)S(1)} %add.18), channel_id=1, source_target_pairs={{0,2},{1,3},{2,0},{3,1},{4,6},{5,7},{6,4},{7,5},{8,10},{9,11},{10,... | collective-permute-start | bytes 49160 | tf_op jit(solution)/shard_map/ppermute | solution.py:644
  42.8 1.7 %collective-permute-done.8 = f32[32,128]{1,0:T(8,128)S(1)} collective-permute-done((f32[32,128]{1,0:T(8,128)S(1)}, f32[32,128]{1,0:T(8,128)S(1)}, u32[]{:S(2)}, u32[]{:S(2)}) %collective-permute-start.8) | collective-permute-done | bytes 16416 | tf_op jit(solution)/shard_map/ppermute | solution.py:644
  44.5 2.4 %last_kernel.1 = (f32[9,128,256]{2,1,0:T(8,128)}, f32[2,6]{1,0:T(2,128)}, f32[128,256]{1,0:T(8,128)}) custom-call(f32[32,128]{1,0:T(8,128)S(1)} %add.19.message, f32[9,128,256]{2,1,0:T(8,128)S(1)} %copy-done, f32[3,9,160,128]{3,2,1,0:T(8,128)S(1)} %get-tuple-element.30.direction, f32[3,9,160,128]{3,2,1,0:T(8,128)S(1)} %get-tuple-element.31.part, ...), custom_call_target="tpu_custom_call" | custom-call | tf_op jit(solution)/shard_map/last_kernel/pallas_call | solution.py:674
  (22 shorter events, 0.1 us)
Async XLA Ops:
  0.6 2.7 %copy-start.4 = (f32[128,256]{1,0:T(8,128)S(1)}, f32[128,256]{1,0:T(8,128)}, u32[]{:S(2)}) copy-start(f32[128,256]{1,0:T(8,128)} %vert.5) | copy-start | bytes 393220
  0.6 2.7 %copy-start.3 = (f32[128,256]{1,0:T(8,128)S(1)}, f32[128,256]{1,0:T(8,128)}, u32[]{:S(2)}) copy-start(f32[128,256]{1,0:T(8,128)} %horiz.5) | copy-start | bytes 393220
  0.7 2.7 %copy-start = (f32[9,128,256]{2,1,0:T(8,128)S(1)}, f32[9,128,256]{2,1,0:T(8,128)}, u32[]{:S(2)}) copy-start(f32[9,128,256]{2,1,0:T(8,128)} %phi.7) | copy-start | bytes 3538948
  0.7 2.7 %copy-start.1 = (f32[9,128,256]{2,1,0:T(8,128)S(1)}, f32[9,128,256]{2,1,0:T(8,128)}, u32[]{:S(2)}) copy-start(f32[9,128,256]{2,1,0:T(8,128)} %forcing.3) | copy-start | bytes 3538948
  0.7 2.7 %copy-start.8 = (f32[6,2]{0,1:T(2,128)S(1)}, f32[6,2]{0,1:T(2,128)}, u32[]{:S(2)}) copy-start(f32[6,2]{0,1:T(2,128)} %param.17) | copy-start | bytes 148
  0.7 2.7 %copy-start.6 = (f32[6,6,2]{1,2,0:T(2,128)S(1)}, f32[6,6,2]{1,2,0:T(2,128)}, u32[]{:S(2)}) copy-start(f32[6,6,2]{1,2,0:T(2,128)} %param.16) | copy-start | bytes 868
  2.1 4.1 %collective-permute-start = (f32[10,8,256]{2,1,0:T(8,128)S(1)}, f32[10,8,256]{2,1,0:T(8,128)S(1)}, u32[]{:S(2)}, u32[]{:S(2)}) collective-permute-start(f32[10,8,256]{2,1,0:T(8,128)S(1)} %get-tuple-element.20), channel_id=1, source_target_pairs={{0,4},{4,0},{8,12},{12,8},{16,20},{20,16},{24,28},{28,24},{1,5},{5... | collective-permute-start | bytes 245768 | tf_op jit(solution)/shard_map/ppermute | solution.py:630
  2.6 3.6 %collective-permute-start.1 = (f32[10,8,256]{2,1,0:T(8,128)S(1)}, f32[10,8,256]{2,1,0:T(8,128)S(1)}, u32[]{:S(2)}, u32[]{:S(2)}) collective-permute-start(f32[10,8,256]{2,1,0:T(8,128)S(1)} %get-tuple-element.21), channel_id=1, source_target_pairs={{4,8},{12,16},{20,24},{8,4},{16,12},{24,20},{5,9},{13,17},{21,25},... | collective-permute-start | bytes 245768 | tf_op jit(solution)/shard_map/ppermute | solution.py:636
  6.2 4.9 %copy-start.2 = (f32[6,128,256]{2,1,0:T(8,128)S(1)}, f32[6,128,256]{2,1,0:T(8,128)}, u32[]{:S(2)}) copy-start(f32[6,128,256]{2,1,0:T(8,128)} %modes.3) | copy-start | bytes 2359300
  6.3 4.9 %copy-start.5 = (f32[9,9]{1,0:T(8,128)S(1)}, f32[9,9]{1,0:T(8,128)}, u32[]{:S(2)}) copy-start(f32[9,9]{1,0:T(8,128)} %mix.1) | copy-start | bytes 976
  6.3 4.9 %copy-start.7 = (s32[128,2]{0,1:T(2,128)S(1)}, s32[128,2]{0,1:T(2,128)}, u32[]{:S(2)}) copy-start(s32[128,2]{0,1:T(2,128)} %param.15) | copy-start | bytes 3076
  6.7 4.5 %collective-permute-start.2 = (f32[72,128]{1,0:T(8,128)S(1)}, f32[72,128]{1,0:T(8,128)S(1)}, u32[]{:S(2)}, u32[]{:S(2)}) collective-permute-start(f32[72,128]{1,0:T(8,128)S(1)} %get-tuple-element.26), channel_id=1, source_target_pairs={{0,1},{1,0},{2,3},{3,2},{4,5},{5,4},{6,7},{7,6},{8,9},{9,8},{10,11... | collective-permute-start | bytes 110600 | tf_op jit(solution)/shard_map/ppermute | solution.py:630
  9.2 1.9 %collective-permute-start.3 = (f32[72,128]{1,0:T(8,128)S(1)}, f32[72,128]{1,0:T(8,128)S(1)}, u32[]{:S(2)}, u32[]{:S(2)}) collective-permute-start(f32[72,128]{1,0:T(8,128)S(1)} %get-tuple-element.27), channel_id=1, source_target_pairs={{1,2},{2,1},{5,6},{6,5},{9,10},{10,9},{13,14},{14,13},{17,18},{18,... | collective-permute-start | bytes 110600 | tf_op jit(solution)/shard_map/ppermute | solution.py:636
  21.4 3.2 %collective-permute-start.4 = (f32[32,128]{1,0:T(8,128)S(1)}, f32[32,128]{1,0:T(8,128)S(1)}, u32[]{:S(2)}, u32[]{:S(2)}) collective-permute-start(f32[32,128]{1,0:T(8,128)S(1)} %get-tuple-element.29), channel_id=1, source_target_pairs={{0,4},{4,0},{8,12},{12,8},{16,20},{20,16},{24,28},{28,24},{1,5},{5... | collective-permute-start | bytes 49160 | tf_op jit(solution)/shard_map/ppermute | solution.py:644
  24.5 4.2 %collective-permute-start.5 = (f32[32,128]{1,0:T(8,128)S(1)}, f32[32,128]{1,0:T(8,128)S(1)}, u32[]{:S(2)}, u32[]{:S(2)}) collective-permute-start(f32[32,128]{1,0:T(8,128)S(1)} %add.15), channel_id=1, source_target_pairs={{0,8},{4,12},{8,0},{12,4},{16,24},{20,28},{24,16},{28,20},{1,9},{5... | collective-permute-start | bytes 49160 | tf_op jit(solution)/shard_map/ppermute | solution.py:644
  28.7 4.8 %collective-permute-start.6 = (f32[32,128]{1,0:T(8,128)S(1)}, f32[32,128]{1,0:T(8,128)S(1)}, u32[]{:S(2)}, u32[]{:S(2)}) collective-permute-start(f32[32,128]{1,0:T(8,128)S(1)} %add.16), channel_id=1, source_target_pairs={{0,16},{4,20},{8,24},{12,28},{16,0},{20,4},{24,8},{28,12},{1,17},{... | collective-permute-start | bytes 49160 | tf_op jit(solution)/shard_map/ppermute | solution.py:644
  33.5 6.3 %collective-permute-start.7 = (f32[32,128]{1,0:T(8,128)S(1)}, f32[32,128]{1,0:T(8,128)S(1)}, u32[]{:S(2)}, u32[]{:S(2)}) collective-permute-start(f32[32,128]{1,0:T(8,128)S(1)} %add.17), channel_id=1, source_target_pairs={{0,1},{1,0},{2,3},{3,2},{4,5},{5,4},{6,7},{7,6},{8,9},{9,8},{10,11... | collective-permute-start | bytes 49160 | tf_op jit(solution)/shard_map/ppermute | solution.py:644
  39.8 4.7 %collective-permute-start.8 = (f32[32,128]{1,0:T(8,128)S(1)}, f32[32,128]{1,0:T(8,128)S(1)}, u32[]{:S(2)}, u32[]{:S(2)}) collective-permute-start(f32[32,128]{1,0:T(8,128)S(1)} %add.18), channel_id=1, source_target_pairs={{0,2},{1,3},{2,0},{3,1},{4,6},{5,7},{6,4},{7,5},{8,10},{9,11},{10,... | collective-permute-start | bytes 49160 | tf_op jit(solution)/shard_map/ppermute | solution.py:644

commit v4 on v3

--- a/solution.py
+++ b/solution.py
@@ -290,20 +290,12 @@
         far_out[i * SUB : (i + 1) * SUB, :] = jnp.where(col_even, to_left, to_right)
 
 
-def lane_sums(entries, lane):
-    step = 1
-    while len(entries) > 1:
-        low = (lane & step) == 0
-        merged = []
-        for a, b in zip(entries[::2], entries[1::2]):
-            if a is None:
-                merged.append(None)
-                continue
-            b = jnp.zeros_like(a) if b is None else b
-            merged.append(jnp.where(low, a, b) + pltpu.roll(jnp.where(low, b, a), step, 1))
-        entries = merged
-        step *= 2
-    return entries[0]
+def ahead_kernel(body_total, after, modes, bodies_t, modes_t, hits):
+    mode_count = modes.shape[0]
+    for t in range(hits.shape[0]):
+        for k in range(mode_count):
+            modes_t[t, k] = modes[k, :, t * LANES : (t + 1) * LANES].T
+        hits[t] = body_hits(bodies_t, t, body_total, hits.shape[1])
 
 
 def main_kernel(
@@ -318,8 +310,8 @@
     col_far,
     table,
     mix,
-    modes,
-    bodies_t,
+    modes_t,
+    hits,
     dir_s,
     part_s,
     message,
@@ -329,10 +321,9 @@
     vert_s,
     scale_s,
     got_s,
-    sums_s,
 ):
     blocks, levels, rows, _ = res.shape
-    mode_count = modes.shape[0]
+    mode_count = modes_t.shape[1]
     tiles = blocks + 1
     side = blocks
     row_tiles = rows // SUB
@@ -448,22 +439,8 @@
                 part_s[t, l, here, :] = value
         return carry
 
-    lax.fori_loop(0, row_tiles + 2, second, 0, unroll=3)
-
-    for i in range(row_tiles):
-        row = pl.ds(base + i * SUB, SUB)
-        here = pl.ds(i * SUB, SUB)
-        entries = [None] * (LANES // 4)
-        for t in range(blocks):
-            lanes = pl.ds(t * LANES, LANES)
-            for q, field in enumerate((dir_s, part_s)):
-                surface = field[t, 0, row, :]
-                for k in range(mode_count):
-                    entries[(2 * t + q) * SUB + k] = modes[k, here, lanes] * surface
-        sums_s[here, :] = lane_sums(entries, lane)
-
     def third(i, totals):
-        row = pl.multiple_of(i * SUB + base, SUB)
+        row = pl.multiple_of(i * SUB + SUB, SUB)
         here = pl.ds(row, SUB)
         image = stencil(
             part_s, row, range(blocks), tiles, levels, coefs_at(row, blocks), lane, True
@@ -479,18 +456,21 @@
         return tuple(totals)
 
     zero = jnp.zeros((SUB, LANES), F32)
-    totals = lax.fori_loop(0, row_tiles, third, (zero,) * 5, unroll=2)
+    lax.fori_loop(0, row_tiles + 2, second, 0, unroll=3)
+    totals = lax.fori_loop(1, row_tiles + 1, third, (zero,) * 5, unroll=4)
 
     width = message.shape[1]
-    sums_t = sums_s[...].T
-    sums_t = sum(sums_t[n * (LANES // 4) : (n + 1) * (LANES // 4), :] for n in range(4))
+    surface_rows = pl.ds(base, rows)
     forces = jnp.zeros((SUB, width), F32)
     for t in range(blocks):
-        hits = body_hits(bodies_t, t, body_total, width)
-        first_sums = sums_t[2 * t * SUB : (2 * t + 1) * SUB, :]
-        second_sums = sums_t[(2 * t + 1) * SUB : (2 * t + 2) * SUB, :]
-        forces = forces + dot_nt(first_sums, hits)
-        forces = forces + pltpu.roll(dot_nt(second_sums, hits), body_total, 1)
+        for q, field in enumerate((dir_s, part_s)):
+            surface = field[t, 0, surface_rows, :].T
+            sums = [
+                jnp.sum(modes_t[t, k] * surface, axis=0, keepdims=True) for k in range(mode_count)
+            ]
+            sums.append(jnp.zeros((SUB - mode_count, rows), F32))
+            share = dot_nt(jnp.concatenate(sums, axis=0), hits[t])
+            forces = forces + (pltpu.roll(share, body_total, 1) if q else share)
     wide_sub = iota((SUB, width), 0)
     gathered = jnp.zeros((SUB, LANES), F32)
     for q, total in enumerate(totals):
@@ -636,13 +616,17 @@
     return lax.ppermute(value, axis, pairs + [(j, i) for i, j in pairs])
 
 
-def sum_over(value, axes):
-    for axis in axes:
-        size = lax.axis_size(axis)
-        step = 1
-        while step < size:
-            value = value + lax.ppermute(value, axis, [(i, i ^ step) for i in range(size)])
-            step *= 2
+def sum_over(value, axis, together):
+    size = lax.axis_size(axis)
+    step = 1
+    while step < size:
+        count = min(together, size // step)
+        total = value
+        for n in range(1, count):
+            pairs = [(i, i ^ (n * step)) for i in range(size)]
+            total = total + lax.ppermute(value, axis, pairs)
+        value = total
+        step *= count
     return value
 
 
@@ -728,6 +712,13 @@
         (res, start_potential, horiz_coef, vert_coef, row_near, row_far, packed),
     )
     col_near, col_far = swap_near(near, "gy"), swap_far(far, "gy")
+    modes_t, hits = call(
+        functools.partial(ahead_kernel, body_total),
+        "ahead_kernel",
+        [((blocks, mode_count, LANES, rows), VMEM), ((blocks, width, rows), VMEM)],
+        [VMEM] * 3,
+        (edge_coef, mode_shapes, bodies_t),
+    )
 
     field = (tiles, levels, padded, LANES)
     plane = pltpu.VMEM((tiles, padded, LANES), F32)
@@ -747,8 +738,8 @@
             col_far,
             table,
             vert_mix,
-            mode_shapes,
-            bodies_t,
+            modes_t,
+            hits,
         ),
         [
             pltpu.VMEM((blocks, levels, padded, LANES), F32),
@@ -757,10 +748,9 @@
             plane,
             plane,
             pltpu.VMEM(packed_shape, F32),
-            pltpu.VMEM((rows, LANES), F32),
         ],
     )
-    message = sum_over(message, ("gx", "gy"))
+    message = sum_over(sum_over(message, "gx", 2), "gy", 4)
 
     potential, velocity_t, flux = call(
         functools.partial(last_kernel, body_total),

time: 47 us -> 44.4 us (0.945)
  Pallas kernels: 17.2 us -> 16 us
  waiting for transfers between devices: 9.01 us -> 8.03 us
  starting transfers between devices: 19.8 us -> 19.2 us
    pallas_call x5 -> x6, Pallas kernels: 17.2 us -> 16 us  [call(): pl.pallas_call(kernel, out_shape=tuple((jax.ShapeDtypeStruct(shape, F32)...]
    ppermute x5 -> x6, waiting for transfers between devices: 7.7 us -> 7.02 us  [sum_over(): total = total + lax.ppermute(value, axis, pairs)]
    ppermute x5 -> x6, starting transfers between devices: 15.4 us -> 14.9 us  [sum_over(): total = total + lax.ppermute(value, axis, pairs)]
  transfers between devices with their start and end apart: 9 -> 10, of which waited for: 6 -> 6; matrix products, arithmetic and copies ran while one was open for 0% -> 0% of each run, Pallas kernels for 6% -> 7%
where the time goes in v4:
time: 44.4 us; the launch traced here: 44.2 us
  starting transfers between devices  19.2 us (43%)
  Pallas kernels  16 us (36%)
  waiting for transfers between devices  8.03 us (18%)
  between operations  0.83 us (2%)
    pallas_call x6, Pallas kernels, call(): pl.pallas_call(kernel, out_shape=tuple((jax.ShapeDtypeStruct(shape, F32)...  16 us
    ppermute x6, starting transfers between devices, sum_over(): total = total + lax.ppermute(value, axis, pairs)  14.9 us
    ppermute x6, waiting for transfers between devices, sum_over(): total = total + lax.ppermute(value, axis, pairs)  7.02 us
    ppermute x2, starting transfers between devices, swap_near(): return lax.ppermute(value, axis, [(i, i ^ 1) for i in range(size)])  3.09 us
    ppermute x2, starting transfers between devices, swap_far(): return lax.ppermute(value, axis, pairs + [(j, i) for i, j in pairs])  1.31 us
    ppermute x2, waiting for transfers between devices, swap_near(): return lax.ppermute(value, axis, [(i, i ^ 1) for i in range(size)])  1.01 us
  transfers between devices with their start and end apart: 10, of which 6 were waited for; matrix products, arithmetic and copies ran while one was open for 0% of the time, Pallas kernels for 7%

profile of v4, /device:TPU:0, one launch (start us, length us, event | category | flops | bytes accessed | tf_op | source)
XLA Modules:
  0.0 44.2 jit_solution(16058667480362163170)
XLA Ops:
  0.7 1.4 %strip_kernel.1 = (f32[10,8,256]{2,1,0:T(8,128)S(1)}, f32[10,8,256]{2,1,0:T(8,128)S(1)}) custom-call(f32[9,128,256]{2,1,0:T(8,128)} %phi.7, f32[9,128,256]{2,1,0:T(8,128)} %forcing.3, f32[128,256]{1,0:T(8,128)} %horiz.5, f32[128,256]{1,0:T(8,128)} %vert.5), custom_call_target="tpu_custom_call" | custom-call | tf_op jit(solution)/shard_map/strip_kernel/pallas_call | solution.py:658
  2.1 0.5 %collective-permute-start = (f32[10,8,256]{2,1,0:T(8,128)S(1)}, f32[10,8,256]{2,1,0:T(8,128)S(1)}, u32[]{:S(2)}, u32[]{:S(2)}) collective-permute-start(f32[10,8,256]{2,1,0:T(8,128)S(1)} %get-tuple-element.22), channel_id=1, source_target_pairs={{0,4},{4,0},{8,12},{12,8},{16,20},{20,16},{24,28},{28,24},{1,5},{5... | collective-permute-start | bytes 245768 | tf_op jit(solution)/shard_map/ppermute | solution.py:610
  2.6 0.7 %collective-permute-start.1 = (f32[10,8,256]{2,1,0:T(8,128)S(1)}, f32[10,8,256]{2,1,0:T(8,128)S(1)}, u32[]{:S(2)}, u32[]{:S(2)}) collective-permute-start(f32[10,8,256]{2,1,0:T(8,128)S(1)} %get-tuple-element.23), channel_id=1, source_target_pairs={{4,8},{12,16},{20,24},{8,4},{16,12},{24,20},{5,9},{13,17},{21,25},... | collective-permute-start | bytes 245768 | tf_op jit(solution)/shard_map/ppermute | solution.py:616
  3.4 2.9 %inner_kernel.1 = (f32[2,9,128,128]{3,2,1,0:T(8,128)S(1)}, f32[144,128]{1,0:T(8,128)S(1)}, f32[24,128]{1,0:T(8,128)S(1)}) custom-call(f32[9,128,256]{2,1,0:T(8,128)S(1)} %copy-done, f32[9,128,256]{2,1,0:T(8,128)S(1)} %copy-done.1, f32[128,256]{1,0:T(8,128)S(1)} %copy-done.3, f32[128,256]{1,0:T(8,128)S(1)} %copy-done.4, f32[6,2,6]{2,1,0:T(2,128)S(1)} %bitcast.4, ...), custom_call_target="tpu_custom_call" | custom-call | tf_op jit(solution)/shard_map/inner_kernel/pallas_call | solution.py:658
  6.2 0.0 collective-permute-done.row_near
  6.3 0.0 copy-start.5
  6.3 0.4 edge_kernel.1
  6.7 2.6 %collective-permute-start.2 = (f32[72,128]{1,0:T(8,128)S(1)}, f32[72,128]{1,0:T(8,128)S(1)}, u32[]{:S(2)}, u32[]{:S(2)}) collective-permute-start(f32[72,128]{1,0:T(8,128)S(1)} %get-tuple-element.28), channel_id=1, source_target_pairs={{0,1},{1,0},{2,3},{3,2},{4,5},{5,4},{6,7},{7,6},{8,9},{9,8},{10,11... | collective-permute-start | bytes 110600 | tf_op jit(solution)/shard_map/ppermute | solution.py:610
  9.2 0.7 %collective-permute-start.3 = (f32[72,128]{1,0:T(8,128)S(1)}, f32[72,128]{1,0:T(8,128)S(1)}, u32[]{:S(2)}, u32[]{:S(2)}) collective-permute-start(f32[72,128]{1,0:T(8,128)S(1)} %get-tuple-element.29), channel_id=1, source_target_pairs={{1,2},{2,1},{5,6},{6,5},{9,10},{10,9},{13,14},{14,13},{17,18},{18,... | collective-permute-start | bytes 110600 | tf_op jit(solution)/shard_map/ppermute | solution.py:616
  9.9 0.3 ahead_kernel.1
  10.2 1.0 %collective-permute-done.2.col_near = f32[72,128]{1,0:T(8,128)S(1)} collective-permute-done((f32[72,128]{1,0:T(8,128)S(1)}, f32[72,128]{1,0:T(8,128)S(1)}, u32[]{:S(2)}, u32[]{:S(2)}) %collective-permute-start.2) | collective-permute-done | bytes 36896 | tf_op jit(solution)/shard_map/ppermute | solution.py:610
  11.2 8.7 %main_kernel.1 = (f32[3,9,160,128]{3,2,1,0:T(8,128)S(1)}, f32[3,9,160,128]{3,2,1,0:T(8,128)S(1)}, f32[32,128]{1,0:T(8,128)S(1)}) custom-call(f32[2,9,128,128]{3,2,1,0:T(8,128)S(1)} %get-tuple-element.21.res, f32[4,2,9,8,128]{4,3,2,1,0:T(8,128)S(1)} %get-tuple-element.25.edge, f32[128,256]{1,0:T(8,128)S(1)} %copy-done.3, f32[128,256]{1,0:T(8,128)S(1)} %copy-done.4, ...), custom_call_target="tpu_custom_call" | custom-call | tf_op jit(solution)/shard_map/main_kernel/pallas_call | solution.py:658
  19.9 2.3 %collective-permute-start.4 = (f32[32,128]{1,0:T(8,128)S(1)}, f32[32,128]{1,0:T(8,128)S(1)}, u32[]{:S(2)}, u32[]{:S(2)}) collective-permute-start(f32[32,128]{1,0:T(8,128)S(1)} %get-tuple-element.33), channel_id=1, source_target_pairs={{0,4},{4,0},{8,12},{12,8},{16,20},{20,16},{24,28},{28,24},{1,5},{5... | collective-permute-start | bytes 49160 | tf_op jit(solution)/shard_map/ppermute | solution.py:627
  22.3 0.8 %collective-permute-done.4 = f32[32,128]{1,0:T(8,128)S(1)} collective-permute-done((f32[32,128]{1,0:T(8,128)S(1)}, f32[32,128]{1,0:T(8,128)S(1)}, u32[]{:S(2)}, u32[]{:S(2)}) %collective-permute-start.4) | collective-permute-done | bytes 16416 | tf_op jit(solution)/shard_map/ppermute | solution.py:627
  23.1 2.5 %collective-permute-start.5 = (f32[32,128]{1,0:T(8,128)S(1)}, f32[32,128]{1,0:T(8,128)S(1)}, u32[]{:S(2)}, u32[]{:S(2)}) collective-permute-start(f32[32,128]{1,0:T(8,128)S(1)} %add.18), channel_id=1, source_target_pairs={{0,8},{4,12},{8,0},{12,4},{16,24},{20,28},{24,16},{28,20},{1,9},{5... | collective-permute-start | bytes 49160 | tf_op jit(solution)/shard_map/ppermute | solution.py:627
  25.6 1.7 %collective-permute-done.5 = f32[32,128]{1,0:T(8,128)S(1)} collective-permute-done((f32[32,128]{1,0:T(8,128)S(1)}, f32[32,128]{1,0:T(8,128)S(1)}, u32[]{:S(2)}, u32[]{:S(2)}) %collective-permute-start.5) | collective-permute-done | bytes 16416 | tf_op jit(solution)/shard_map/ppermute | solution.py:627
  27.3 3.0 %collective-permute-start.6 = (f32[32,128]{1,0:T(8,128)S(1)}, f32[32,128]{1,0:T(8,128)S(1)}, u32[]{:S(2)}, u32[]{:S(2)}) collective-permute-start(f32[32,128]{1,0:T(8,128)S(1)} %add.19), channel_id=1, source_target_pairs={{0,16},{4,20},{8,24},{12,28},{16,0},{20,4},{24,8},{28,12},{1,17},{... | collective-permute-start | bytes 49160 | tf_op jit(solution)/shard_map/ppermute | solution.py:627
  30.3 1.7 %collective-permute-done.6 = f32[32,128]{1,0:T(8,128)S(1)} collective-permute-done((f32[32,128]{1,0:T(8,128)S(1)}, f32[32,128]{1,0:T(8,128)S(1)}, u32[]{:S(2)}, u32[]{:S(2)}) %collective-permute-start.6) | collective-permute-done | bytes 16416 | tf_op jit(solution)/shard_map/ppermute | solution.py:627
  32.1 2.4 %collective-permute-start.9 = (f32[32,128]{1,0:T(8,128)S(1)}, f32[32,128]{1,0:T(8,128)S(1)}, u32[]{:S(2)}, u32[]{:S(2)}) collective-permute-start(f32[32,128]{1,0:T(8,128)S(1)} %add.20), channel_id=1, source_target_pairs={{0,3},{1,2},{2,1},{3,0},{4,7},{5,6},{6,5},{7,4},{8,11},{9,10},{10,... | collective-permute-start | bytes 49160 | tf_op jit(solution)/shard_map/ppermute | solution.py:627
  34.5 3.6 %collective-permute-start.8 = (f32[32,128]{1,0:T(8,128)S(1)}, f32[32,128]{1,0:T(8,128)S(1)}, u32[]{:S(2)}, u32[]{:S(2)}) collective-permute-start(f32[32,128]{1,0:T(8,128)S(1)} %add.20), channel_id=1, source_target_pairs={{0,2},{1,3},{2,0},{3,1},{4,6},{5,7},{6,4},{7,5},{8,10},{9,11},{10,... | collective-permute-start | bytes 49160 | tf_op jit(solution)/shard_map/ppermute | solution.py:627
  38.1 1.0 %collective-permute-start.7 = (f32[32,128]{1,0:T(8,128)S(1)}, f32[32,128]{1,0:T(8,128)S(1)}, u32[]{:S(2)}, u32[]{:S(2)}) collective-permute-start(f32[32,128]{1,0:T(8,128)S(1)} %add.20), channel_id=1, source_target_pairs={{0,1},{1,0},{2,3},{3,2},{4,5},{5,4},{6,7},{7,6},{8,9},{9,8},{10,11... | collective-permute-start | bytes 49160 | tf_op jit(solution)/shard_map/ppermute | solution.py:627
  39.1 0.7 %collective-permute-done.8 = f32[32,128]{1,0:T(8,128)S(1)} collective-permute-done((f32[32,128]{1,0:T(8,128)S(1)}, f32[32,128]{1,0:T(8,128)S(1)}, u32[]{:S(2)}, u32[]{:S(2)}) %collective-permute-start.8) | collective-permute-done | bytes 16416 | tf_op jit(solution)/shard_map/ppermute | solution.py:627
  39.8 2.0 %collective-permute-done.7 = f32[32,128]{1,0:T(8,128)S(1)} collective-permute-done((f32[32,128]{1,0:T(8,128)S(1)}, f32[32,128]{1,0:T(8,128)S(1)}, u32[]{:S(2)}, u32[]{:S(2)}) %collective-permute-start.7) | collective-permute-done | bytes 16416 | tf_op jit(solution)/shard_map/ppermute | solution.py:627
  41.8 2.4 %last_kernel.1 = (f32[9,128,256]{2,1,0:T(8,128)}, f32[2,6]{1,0:T(2,128)}, f32[128,256]{1,0:T(8,128)}) custom-call(f32[32,128]{1,0:T(8,128)S(1)} %add_add_fusion.message, f32[9,128,256]{2,1,0:T(8,128)S(1)} %copy-done, f32[3,9,160,128]{3,2,1,0:T(8,128)S(1)} %get-tuple-element.34.direction, f32[3,9,160,128]{3,2,1,0:T(8,128)S(1)} %get-tuple-element.35.part, ...), custom_call_target="tpu_custom_call" | custom-call | tf_op jit(solution)/shard_map/last_kernel/pallas_call | solution.py:658
  (24 shorter events, 0.1 us)
Async XLA Ops:
  0.6 2.7 %copy-start.4 = (f32[128,256]{1,0:T(8,128)S(1)}, f32[128,256]{1,0:T(8,128)}, u32[]{:S(2)}) copy-start(f32[128,256]{1,0:T(8,128)} %vert.5) | copy-start | bytes 393220
  0.6 2.7 %copy-start.3 = (f32[128,256]{1,0:T(8,128)S(1)}, f32[128,256]{1,0:T(8,128)}, u32[]{:S(2)}) copy-start(f32[128,256]{1,0:T(8,128)} %horiz.5) | copy-start | bytes 393220
  0.7 2.7 %copy-start = (f32[9,128,256]{2,1,0:T(8,128)S(1)}, f32[9,128,256]{2,1,0:T(8,128)}, u32[]{:S(2)}) copy-start(f32[9,128,256]{2,1,0:T(8,128)} %phi.7) | copy-start | bytes 3538948
  0.7 2.7 %copy-start.1 = (f32[9,128,256]{2,1,0:T(8,128)S(1)}, f32[9,128,256]{2,1,0:T(8,128)}, u32[]{:S(2)}) copy-start(f32[9,128,256]{2,1,0:T(8,128)} %forcing.3) | copy-start | bytes 3538948
  0.7 2.7 %copy-start.8 = (f32[6,2]{0,1:T(2,128)S(1)}, f32[6,2]{0,1:T(2,128)}, u32[]{:S(2)}) copy-start(f32[6,2]{0,1:T(2,128)} %param.17) | copy-start | bytes 148
  0.7 2.7 %copy-start.6 = (f32[6,6,2]{1,2,0:T(2,128)S(1)}, f32[6,6,2]{1,2,0:T(2,128)}, u32[]{:S(2)}) copy-start(f32[6,6,2]{1,2,0:T(2,128)} %param.16) | copy-start | bytes 868
  2.1 4.1 %collective-permute-start = (f32[10,8,256]{2,1,0:T(8,128)S(1)}, f32[10,8,256]{2,1,0:T(8,128)S(1)}, u32[]{:S(2)}, u32[]{:S(2)}) collective-permute-start(f32[10,8,256]{2,1,0:T(8,128)S(1)} %get-tuple-element.22), channel_id=1, source_target_pairs={{0,4},{4,0},{8,12},{12,8},{16,20},{20,16},{24,28},{28,24},{1,5},{5... | collective-permute-start | bytes 245768 | tf_op jit(solution)/shard_map/ppermute | solution.py:610
  2.6 3.6 %collective-permute-start.1 = (f32[10,8,256]{2,1,0:T(8,128)S(1)}, f32[10,8,256]{2,1,0:T(8,128)S(1)}, u32[]{:S(2)}, u32[]{:S(2)}) collective-permute-start(f32[10,8,256]{2,1,0:T(8,128)S(1)} %get-tuple-element.23), channel_id=1, source_target_pairs={{4,8},{12,16},{20,24},{8,4},{16,12},{24,20},{5,9},{13,17},{21,25},... | collective-permute-start | bytes 245768 | tf_op jit(solution)/shard_map/ppermute | solution.py:616
  6.2 3.7 %copy-start.2 = (f32[6,128,256]{2,1,0:T(8,128)S(1)}, f32[6,128,256]{2,1,0:T(8,128)}, u32[]{:S(2)}) copy-start(f32[6,128,256]{2,1,0:T(8,128)} %modes.3) | copy-start | bytes 2359300
  6.3 3.7 %copy-start.7 = (s32[128,2]{0,1:T(2,128)S(1)}, s32[128,2]{0,1:T(2,128)}, u32[]{:S(2)}) copy-start(s32[128,2]{0,1:T(2,128)} %param.15) | copy-start | bytes 3076
  6.3 4.9 %copy-start.5 = (f32[9,9]{1,0:T(8,128)S(1)}, f32[9,9]{1,0:T(8,128)}, u32[]{:S(2)}) copy-start(f32[9,9]{1,0:T(8,128)} %mix.1) | copy-start | bytes 976
  6.7 4.5 %collective-permute-start.2 = (f32[72,128]{1,0:T(8,128)S(1)}, f32[72,128]{1,0:T(8,128)S(1)}, u32[]{:S(2)}, u32[]{:S(2)}) collective-permute-start(f32[72,128]{1,0:T(8,128)S(1)} %get-tuple-element.28), channel_id=1, source_target_pairs={{0,1},{1,0},{2,3},{3,2},{4,5},{5,4},{6,7},{7,6},{8,9},{9,8},{10,11... | collective-permute-start | bytes 110600 | tf_op jit(solution)/shard_map/ppermute | solution.py:610
  9.2 1.9 %collective-permute-start.3 = (f32[72,128]{1,0:T(8,128)S(1)}, f32[72,128]{1,0:T(8,128)S(1)}, u32[]{:S(2)}, u32[]{:S(2)}) collective-permute-start(f32[72,128]{1,0:T(8,128)S(1)} %get-tuple-element.29), channel_id=1, source_target_pairs={{1,2},{2,1},{5,6},{6,5},{9,10},{10,9},{13,14},{14,13},{17,18},{18,... | collective-permute-start | bytes 110600 | tf_op jit(solution)/shard_map/ppermute | solution.py:616
  19.9 3.2 %collective-permute-start.4 = (f32[32,128]{1,0:T(8,128)S(1)}, f32[32,128]{1,0:T(8,128)S(1)}, u32[]{:S(2)}, u32[]{:S(2)}) collective-permute-start(f32[32,128]{1,0:T(8,128)S(1)} %get-tuple-element.33), channel_id=1, source_target_pairs={{0,4},{4,0},{8,12},{12,8},{16,20},{20,16},{24,28},{28,24},{1,5},{5... | collective-permute-start | bytes 49160 | tf_op jit(solution)/shard_map/ppermute | solution.py:627
  23.1 4.2 %collective-permute-start.5 = (f32[32,128]{1,0:T(8,128)S(1)}, f32[32,128]{1,0:T(8,128)S(1)}, u32[]{:S(2)}, u32[]{:S(2)}) collective-permute-start(f32[32,128]{1,0:T(8,128)S(1)} %add.18), channel_id=1, source_target_pairs={{0,8},{4,12},{8,0},{12,4},{16,24},{20,28},{24,16},{28,20},{1,9},{5... | collective-permute-start | bytes 49160 | tf_op jit(solution)/shard_map/ppermute | solution.py:627
  27.3 4.8 %collective-permute-start.6 = (f32[32,128]{1,0:T(8,128)S(1)}, f32[32,128]{1,0:T(8,128)S(1)}, u32[]{:S(2)}, u32[]{:S(2)}) collective-permute-start(f32[32,128]{1,0:T(8,128)S(1)} %add.19), channel_id=1, source_target_pairs={{0,16},{4,20},{8,24},{12,28},{16,0},{20,4},{24,8},{28,12},{1,17},{... | collective-permute-start | bytes 49160 | tf_op jit(solution)/shard_map/ppermute | solution.py:627
  32.1 7.0 %collective-permute-start.9 = (f32[32,128]{1,0:T(8,128)S(1)}, f32[32,128]{1,0:T(8,128)S(1)}, u32[]{:S(2)}, u32[]{:S(2)}) collective-permute-start(f32[32,128]{1,0:T(8,128)S(1)} %add.20), channel_id=1, source_target_pairs={{0,3},{1,2},{2,1},{3,0},{4,7},{5,6},{6,5},{7,4},{8,11},{9,10},{10,... | collective-permute-start | bytes 49160 | tf_op jit(solution)/shard_map/ppermute | solution.py:627
  34.5 5.3 %collective-permute-start.8 = (f32[32,128]{1,0:T(8,128)S(1)}, f32[32,128]{1,0:T(8,128)S(1)}, u32[]{:S(2)}, u32[]{:S(2)}) collective-permute-start(f32[32,128]{1,0:T(8,128)S(1)} %add.20), channel_id=1, source_target_pairs={{0,2},{1,3},{2,0},{3,1},{4,6},{5,7},{6,4},{7,5},{8,10},{9,11},{10,... | collective-permute-start | bytes 49160 | tf_op jit(solution)/shard_map/ppermute | solution.py:627
  38.1 3.7 %collective-permute-start.7 = (f32[32,128]{1,0:T(8,128)S(1)}, f32[32,128]{1,0:T(8,128)S(1)}, u32[]{:S(2)}, u32[]{:S(2)}) collective-permute-start(f32[32,128]{1,0:T(8,128)S(1)} %add.20), channel_id=1, source_target_pairs={{0,1},{1,0},{2,3},{3,2},{4,5},{5,4},{6,7},{7,6},{8,9},{9,8},{10,11... | collective-permute-start | bytes 49160 | tf_op jit(solution)/shard_map/ppermute | solution.py:627

commit v5 on v4

--- a/solution.py
+++ b/solution.py
@@ -290,12 +290,14 @@
         far_out[i * SUB : (i + 1) * SUB, :] = jnp.where(col_even, to_left, to_right)
 
 
-def ahead_kernel(body_total, after, modes, bodies_t, modes_t, hits):
+def ahead_kernel(body_total, after, modes, bodies_t, modes_t, hits, hits_t):
     mode_count = modes.shape[0]
     for t in range(hits.shape[0]):
         for k in range(mode_count):
             modes_t[t, k] = modes[k, :, t * LANES : (t + 1) * LANES].T
-        hits[t] = body_hits(bodies_t, t, body_total, hits.shape[1])
+        found = body_hits(bodies_t, t, body_total, hits.shape[1])
+        hits[t] = found
+        hits_t[t] = found.T
 
 
 def main_kernel(
@@ -311,7 +313,7 @@
     table,
     mix,
     modes_t,
-    hits,
+    hits_t,
     dir_s,
     part_s,
     message,
@@ -469,7 +471,7 @@
                 jnp.sum(modes_t[t, k] * surface, axis=0, keepdims=True) for k in range(mode_count)
             ]
             sums.append(jnp.zeros((SUB - mode_count, rows), F32))
-            share = dot_nt(jnp.concatenate(sums, axis=0), hits[t])
+            share = exact_dot(jnp.concatenate(sums, axis=0), hits_t[t])
             forces = forces + (pltpu.roll(share, body_total, 1) if q else share)
     wide_sub = iota((SUB, width), 0)
     gathered = jnp.zeros((SUB, LANES), F32)
@@ -506,24 +508,35 @@
     )
 
 
+def exact_dot(values, ones):
+    high = values.astype(jnp.bfloat16).astype(F32)
+    rest = values - high
+    middle = rest.astype(jnp.bfloat16).astype(F32)
+    parts = jnp.concatenate([high, middle, rest - middle, jnp.zeros_like(high)], axis=0)
+    shares = jnp.dot(
+        parts.astype(jnp.bfloat16), ones.astype(jnp.bfloat16), preferred_element_type=F32
+    )
+    return shares[0:SUB] + (shares[SUB : 2 * SUB] + shares[2 * SUB : 3 * SUB])
+
+
 def last_kernel(
     body_total,
     message,
     phi,
     direction,
     part,
-    modes,
-    bodies_t,
+    modes_t,
+    hits,
     potential,
     velocity_t,
     flux,
     phi_s,
     flux_s,
+    velocity_s,
     out_sems,
 ):
     levels, rows, cols = phi.shape
-    mode_count = modes.shape[0]
-    blocks = cols // LANES
+    blocks, mode_count = modes_t.shape[0:2]
     width = message.shape[1]
     owned = velocity_t.shape[0]
     main = pl.ds(2 * SUB, rows)
@@ -548,19 +561,22 @@
     second_step = next_top / next_bottom
     on_dir = first_step + second_step
     on_part = first_step * second_step
-
     outgoing = []
+
+    def send(src, dst):
+        copy = pltpu.make_async_copy(src, dst, out_sems.at[len(outgoing)])
+        copy.start()
+        outgoing.append(copy)
+
+
     for l in range(levels):
         for t in range(blocks):
             lanes = pl.ds(t * LANES, LANES)
             change = on_dir * direction[t, l, main, :] - on_part * part[t, l, main, :]
             phi_s[l, :, lanes] = phi[l, :, lanes] + change
-        copy = pltpu.make_async_copy(phi_s.at[l], potential.at[l], out_sems.at[l])
-        copy.start()
-        outgoing.append(copy)
-
-    wide_sub = lax.broadcasted_iota(jnp.int32, (SUB, width), 0)
-    wide_lane = lax.broadcasted_iota(jnp.int32, (SUB, width), 1)
+        send(phi_s.at[l], potential.at[l])
+
+    wide_sub, wide_lane = iota((SUB, width), 0), iota((SUB, width), 1)
     foot_scale = 1.0 / math.sqrt(FOOT)
     forces = foot_scale * (on_part * pltpu.roll(top, body_total, 1) - on_dir * top)
     forces = jnp.where(wide_sub == mode_count, 1.0, forces)
@@ -572,35 +588,18 @@
             table = pltpu.roll(table, body_total, 1)
         value = jnp.sum(table * forces, axis=0, keepdims=True)
         velocity = jnp.where(wide_sub == k, value, velocity)
+    per_row = [exact_dot(velocity, hits[t]) for t in range(blocks)]
 
     me = (lax.axis_index("gx") * lax.axis_size("gy") + lax.axis_index("gy")) * owned
     mine = ((wide_lane == me + wide_sub) & (wide_sub < owned)).astype(F32)
-    velocity_t[...] = dot_nt(mine, velocity)[0:owned, 0:mode_count]
-
-    per_row = []
+    velocity_s[...] = dot_nt(mine, velocity)[0:owned, 0:mode_count]
+    send(velocity_s, velocity_t)
     for t in range(blocks):
-        hits = body_hits(bodies_t, t, body_total, width)
-        per_row.append(
-            lax.dot_general(
-                velocity,
-                hits,
-                (((1,), (0,)), ((), ())),
-                precision=lax.Precision.HIGHEST,
-                preferred_element_type=F32,
-            )
-        )
-    per_row.append(jnp.zeros((LANES - blocks * SUB, rows), F32))
-    spread = jnp.concatenate(per_row, axis=0).T
-
-    for t in range(blocks):
-        lanes = pl.ds(t * LANES, LANES)
-        total = jnp.zeros((rows, LANES), F32)
-        for k in range(mode_count):
-            total = total + modes[k, :, lanes] * spread[:, t * SUB + k : t * SUB + k + 1]
-        flux_s[:, lanes] = total
-    flux_copy = pltpu.make_async_copy(flux_s, flux, out_sems.at[levels])
-    flux_copy.start()
-    outgoing.append(flux_copy)
+        total = modes_t[t, 0] * per_row[t][0:1, :]
+        for k in range(1, mode_count):
+            total = total + modes_t[t, k] * per_row[t][k : k + 1, :]
+        flux_s[:, t * LANES : (t + 1) * LANES] = total.T
+    send(flux_s, flux)
     for copy in outgoing:
         copy.wait()
 
@@ -712,10 +711,10 @@
         (res, start_potential, horiz_coef, vert_coef, row_near, row_far, packed),
     )
     col_near, col_far = swap_near(near, "gy"), swap_far(far, "gy")
-    modes_t, hits = call(
+    modes_t, hits, hits_t = call(
         functools.partial(ahead_kernel, body_total),
         "ahead_kernel",
-        [((blocks, mode_count, LANES, rows), VMEM), ((blocks, width, rows), VMEM)],
+        [((blocks, mode_count, LANES, rows), VMEM), ((blocks, width, rows), VMEM), ((blocks, rows, width), VMEM)],
         [VMEM] * 3,
         (edge_coef, mode_shapes, bodies_t),
     )
@@ -739,7 +738,7 @@
             table,
             vert_mix,
             modes_t,
-            hits,
+            hits_t,
         ),
         [
             pltpu.VMEM((blocks, levels, padded, LANES), F32),
@@ -755,13 +754,14 @@
     potential, velocity_t, flux = call(
         functools.partial(last_kernel, body_total),
         "last_kernel",
-        [((levels, rows, cols), HBM), ((owned, mode_count), VMEM), ((rows, cols), HBM)],
+        [((levels, rows, cols), HBM), ((owned, mode_count), HBM), ((rows, cols), HBM)],
         [VMEM] * 6,
-        (message, start_potential, direction, part, mode_shapes, bodies_t),
+        (message, start_potential, direction, part, modes_t, hits),
         [
             pltpu.VMEM((levels, rows, cols), F32),
             pltpu.VMEM((rows, cols), F32),
-            pltpu.SemaphoreType.DMA((levels + 1,)),
+            pltpu.VMEM((owned, mode_count), F32),
+            pltpu.SemaphoreType.DMA((levels + 2,)),
         ],
     )
     return (potential, velocity_t.T, flux)

time: 44.4 us -> 43.1 us (0.971)
  Pallas kernels: 16 us -> 14.8 us
    pallas_call x6, Pallas kernels: 16 us -> 14.8 us  [call(): pl.pallas_call(kernel, out_shape=tuple((jax.ShapeDtypeStruct(shape, F32)...]
where the time goes in v5:
time: 43.1 us; the launch traced here: 43 us
  starting transfers between devices  19.3 us (45%)
  Pallas kernels  14.8 us (34%)
  waiting for transfers between devices  8.01 us (19%)
  between operations  0.83 us (2%)
    ppermute x6, starting transfers between devices, sum_over(): total = total + lax.ppermute(value, axis, pairs)  14.9 us
    pallas_call x6, Pallas kernels, call(): pl.pallas_call(kernel, out_shape=tuple((jax.ShapeDtypeStruct(shape, F32)...  14.8 us
    ppermute x6, waiting for transfers between devices, sum_over(): total = total + lax.ppermute(value, axis, pairs)  7.02 us
    ppermute x2, starting transfers between devices, swap_near(): return lax.ppermute(value, axis, [(i, i ^ 1) for i in range(size)])  3.09 us
    ppermute x2, starting transfers between devices, swap_far(): return lax.ppermute(value, axis, pairs + [(j, i) for i, j in pairs])  1.31 us
    ppermute x2, waiting for transfers between devices, swap_near(): return lax.ppermute(value, axis, [(i, i ^ 1) for i in range(size)])  0.98 us
  transfers between devices with their start and end apart: 10, of which 6 were waited for; matrix products, arithmetic and copies ran while one was open for 0% of the time, Pallas kernels for 7%

profile of v5, /device:TPU:0, one launch (start us, length us, event | category | flops | bytes accessed | tf_op | source)
XLA Modules:
  0.0 43.0 jit_solution(4637848868496993408)
XLA Ops:
  0.7 1.4 %strip_kernel.1 = (f32[10,8,256]{2,1,0:T(8,128)S(1)}, f32[10,8,256]{2,1,0:T(8,128)S(1)}) custom-call(f32[9,128,256]{2,1,0:T(8,128)} %phi.7, f32[9,128,256]{2,1,0:T(8,128)} %forcing.3, f32[128,256]{1,0:T(8,128)} %horiz.5, f32[128,256]{1,0:T(8,128)} %vert.5), custom_call_target="tpu_custom_call" | custom-call | tf_op jit(solution)/shard_map/strip_kernel/pallas_call | solution.py:657
  2.1 0.5 %collective-permute-start = (f32[10,8,256]{2,1,0:T(8,128)S(1)}, f32[10,8,256]{2,1,0:T(8,128)S(1)}, u32[]{:S(2)}, u32[]{:S(2)}) collective-permute-start(f32[10,8,256]{2,1,0:T(8,128)S(1)} %get-tuple-element.23), channel_id=1, source_target_pairs={{0,4},{4,0},{8,12},{12,8},{16,20},{20,16},{24,28},{28,24},{1,5},{5... | collective-permute-start | bytes 245768 | tf_op jit(solution)/shard_map/ppermute | solution.py:609
  2.6 0.7 %collective-permute-start.1 = (f32[10,8,256]{2,1,0:T(8,128)S(1)}, f32[10,8,256]{2,1,0:T(8,128)S(1)}, u32[]{:S(2)}, u32[]{:S(2)}) collective-permute-start(f32[10,8,256]{2,1,0:T(8,128)S(1)} %get-tuple-element.24), channel_id=1, source_target_pairs={{4,8},{12,16},{20,24},{8,4},{16,12},{24,20},{5,9},{13,17},{21,25},... | collective-permute-start | bytes 245768 | tf_op jit(solution)/shard_map/ppermute | solution.py:615
  3.4 2.9 %inner_kernel.1 = (f32[2,9,128,128]{3,2,1,0:T(8,128)S(1)}, f32[144,128]{1,0:T(8,128)S(1)}, f32[24,128]{1,0:T(8,128)S(1)}) custom-call(f32[9,128,256]{2,1,0:T(8,128)S(1)} %copy-done, f32[9,128,256]{2,1,0:T(8,128)S(1)} %copy-done.1, f32[128,256]{1,0:T(8,128)S(1)} %copy-done.2, f32[128,256]{1,0:T(8,128)S(1)} %copy-done.3, f32[6,2,6]{2,1,0:T(2,128)S(1)} %bitcast.4, ...), custom_call_target="tpu_custom_call" | custom-call | tf_op jit(solution)/shard_map/inner_kernel/pallas_call | solution.py:657
  6.2 0.0 collective-permute-done.row_near
  6.3 0.0 copy-start.5
  6.3 0.4 edge_kernel.1
  6.7 2.6 %collective-permute-start.2 = (f32[72,128]{1,0:T(8,128)S(1)}, f32[72,128]{1,0:T(8,128)S(1)}, u32[]{:S(2)}, u32[]{:S(2)}) collective-permute-start(f32[72,128]{1,0:T(8,128)S(1)} %get-tuple-element.29), channel_id=1, source_target_pairs={{0,1},{1,0},{2,3},{3,2},{4,5},{5,4},{6,7},{7,6},{8,9},{9,8},{10,11... | collective-permute-start | bytes 110600 | tf_op jit(solution)/shard_map/ppermute | solution.py:609
  9.2 0.7 %collective-permute-start.3 = (f32[72,128]{1,0:T(8,128)S(1)}, f32[72,128]{1,0:T(8,128)S(1)}, u32[]{:S(2)}, u32[]{:S(2)}) collective-permute-start(f32[72,128]{1,0:T(8,128)S(1)} %get-tuple-element.30), channel_id=1, source_target_pairs={{1,2},{2,1},{5,6},{6,5},{9,10},{10,9},{13,14},{14,13},{17,18},{18,... | collective-permute-start | bytes 110600 | tf_op jit(solution)/shard_map/ppermute | solution.py:615
  9.9 0.3 ahead_kernel.1
  10.2 1.0 %collective-permute-done.2.col_near = f32[72,128]{1,0:T(8,128)S(1)} collective-permute-done((f32[72,128]{1,0:T(8,128)S(1)}, f32[72,128]{1,0:T(8,128)S(1)}, u32[]{:S(2)}, u32[]{:S(2)}) %collective-permute-start.2) | collective-permute-done | bytes 36896 | tf_op jit(solution)/shard_map/ppermute | solution.py:609
  11.2 8.4 %main_kernel.1 = (f32[3,9,160,128]{3,2,1,0:T(8,128)S(1)}, f32[3,9,160,128]{3,2,1,0:T(8,128)S(1)}, f32[32,128]{1,0:T(8,128)S(1)}) custom-call(f32[2,9,128,128]{3,2,1,0:T(8,128)S(1)} %get-tuple-element.22.res, f32[4,2,9,8,128]{4,3,2,1,0:T(8,128)S(1)} %get-tuple-element.26.edge, f32[128,256]{1,0:T(8,128)S(1)} %copy-done.2, f32[128,256]{1,0:T(8,128)S(1)} %copy-done.3, ...), custom_call_target="tpu_custom_call" | custom-call | tf_op jit(solution)/shard_map/main_kernel/pallas_call | solution.py:657
  19.6 2.4 %collective-permute-start.4 = (f32[32,128]{1,0:T(8,128)S(1)}, f32[32,128]{1,0:T(8,128)S(1)}, u32[]{:S(2)}, u32[]{:S(2)}) collective-permute-start(f32[32,128]{1,0:T(8,128)S(1)} %get-tuple-element.34), channel_id=1, source_target_pairs={{0,4},{4,0},{8,12},{12,8},{16,20},{20,16},{24,28},{28,24},{1,5},{5... | collective-permute-start | bytes 49160 | tf_op jit(solution)/shard_map/ppermute | solution.py:626
  22.0 0.8 %collective-permute-done.4 = f32[32,128]{1,0:T(8,128)S(1)} collective-permute-done((f32[32,128]{1,0:T(8,128)S(1)}, f32[32,128]{1,0:T(8,128)S(1)}, u32[]{:S(2)}, u32[]{:S(2)}) %collective-permute-start.4) | collective-permute-done | bytes 16416 | tf_op jit(solution)/shard_map/ppermute | solution.py:626
  22.8 2.5 %collective-permute-start.5 = (f32[32,128]{1,0:T(8,128)S(1)}, f32[32,128]{1,0:T(8,128)S(1)}, u32[]{:S(2)}, u32[]{:S(2)}) collective-permute-start(f32[32,128]{1,0:T(8,128)S(1)} %add.18), channel_id=1, source_target_pairs={{0,8},{4,12},{8,0},{12,4},{16,24},{20,28},{24,16},{28,20},{1,9},{5... | collective-permute-start | bytes 49160 | tf_op jit(solution)/shard_map/ppermute | solution.py:626
  25.3 1.7 %collective-permute-done.5 = f32[32,128]{1,0:T(8,128)S(1)} collective-permute-done((f32[32,128]{1,0:T(8,128)S(1)}, f32[32,128]{1,0:T(8,128)S(1)}, u32[]{:S(2)}, u32[]{:S(2)}) %collective-permute-start.5) | collective-permute-done | bytes 16416 | tf_op jit(solution)/shard_map/ppermute | solution.py:626
  27.0 3.0 %collective-permute-start.6 = (f32[32,128]{1,0:T(8,128)S(1)}, f32[32,128]{1,0:T(8,128)S(1)}, u32[]{:S(2)}, u32[]{:S(2)}) collective-permute-start(f32[32,128]{1,0:T(8,128)S(1)} %add.19), channel_id=1, source_target_pairs={{0,16},{4,20},{8,24},{12,28},{16,0},{20,4},{24,8},{28,12},{1,17},{... | collective-permute-start | bytes 49160 | tf_op jit(solution)/shard_map/ppermute | solution.py:626
  30.1 1.7 %collective-permute-done.6 = f32[32,128]{1,0:T(8,128)S(1)} collective-permute-done((f32[32,128]{1,0:T(8,128)S(1)}, f32[32,128]{1,0:T(8,128)S(1)}, u32[]{:S(2)}, u32[]{:S(2)}) %collective-permute-start.6) | collective-permute-done | bytes 16416 | tf_op jit(solution)/shard_map/ppermute | solution.py:626
  31.8 2.4 %collective-permute-start.9 = (f32[32,128]{1,0:T(8,128)S(1)}, f32[32,128]{1,0:T(8,128)S(1)}, u32[]{:S(2)}, u32[]{:S(2)}) collective-permute-start(f32[32,128]{1,0:T(8,128)S(1)} %add.20), channel_id=1, source_target_pairs={{0,3},{1,2},{2,1},{3,0},{4,7},{5,6},{6,5},{7,4},{8,11},{9,10},{10,... | collective-permute-start | bytes 49160 | tf_op jit(solution)/shard_map/ppermute | solution.py:626
  34.2 3.6 %collective-permute-start.8 = (f32[32,128]{1,0:T(8,128)S(1)}, f32[32,128]{1,0:T(8,128)S(1)}, u32[]{:S(2)}, u32[]{:S(2)}) collective-permute-start(f32[32,128]{1,0:T(8,128)S(1)} %add.20), channel_id=1, source_target_pairs={{0,2},{1,3},{2,0},{3,1},{4,6},{5,7},{6,4},{7,5},{8,10},{9,11},{10,... | collective-permute-start | bytes 49160 | tf_op jit(solution)/shard_map/ppermute | solution.py:626
  37.8 1.0 %collective-permute-start.7 = (f32[32,128]{1,0:T(8,128)S(1)}, f32[32,128]{1,0:T(8,128)S(1)}, u32[]{:S(2)}, u32[]{:S(2)}) collective-permute-start(f32[32,128]{1,0:T(8,128)S(1)} %add.20), channel_id=1, source_target_pairs={{0,1},{1,0},{2,3},{3,2},{4,5},{5,4},{6,7},{7,6},{8,9},{9,8},{10,11... | collective-permute-start | bytes 49160 | tf_op jit(solution)/shard_map/ppermute | solution.py:626
  38.8 0.7 %collective-permute-done.8 = f32[32,128]{1,0:T(8,128)S(1)} collective-permute-done((f32[32,128]{1,0:T(8,128)S(1)}, f32[32,128]{1,0:T(8,128)S(1)}, u32[]{:S(2)}, u32[]{:S(2)}) %collective-permute-start.8) | collective-permute-done | bytes 16416 | tf_op jit(solution)/shard_map/ppermute | solution.py:626
  39.5 2.0 %collective-permute-done.7 = f32[32,128]{1,0:T(8,128)S(1)} collective-permute-done((f32[32,128]{1,0:T(8,128)S(1)}, f32[32,128]{1,0:T(8,128)S(1)}, u32[]{:S(2)}, u32[]{:S(2)}) %collective-permute-start.7) | collective-permute-done | bytes 16416 | tf_op jit(solution)/shard_map/ppermute | solution.py:626
  41.5 1.4 %last_kernel.1 = (f32[9,128,256]{2,1,0:T(8,128)}, f32[2,6]{1,0:T(2,128)}, f32[128,256]{1,0:T(8,128)}) custom-call(f32[32,128]{1,0:T(8,128)S(1)} %add_add_fusion.message, f32[9,128,256]{2,1,0:T(8,128)S(1)} %copy-done, f32[3,9,160,128]{3,2,1,0:T(8,128)S(1)} %get-tuple-element.35.direction, f32[3,9,160,128]{3,2,1,0:T(8,128)S(1)} %get-tuple-element.36.part, ...), custom_call_target="tpu_custom_call" | custom-call | tf_op jit(solution)/shard_map/last_kernel/pallas_call | solution.py:657
  (24 shorter events, 0.1 us)
Async XLA Ops:
  0.6 2.7 %copy-start.3 = (f32[128,256]{1,0:T(8,128)S(1)}, f32[128,256]{1,0:T(8,128)}, u32[]{:S(2)}) copy-start(f32[128,256]{1,0:T(8,128)} %vert.5) | copy-start | bytes 393220
  0.6 2.7 %copy-start.2 = (f32[128,256]{1,0:T(8,128)S(1)}, f32[128,256]{1,0:T(8,128)}, u32[]{:S(2)}) copy-start(f32[128,256]{1,0:T(8,128)} %horiz.5) | copy-start | bytes 393220
  0.7 2.7 %copy-start = (f32[9,128,256]{2,1,0:T(8,128)S(1)}, f32[9,128,256]{2,1,0:T(8,128)}, u32[]{:S(2)}) copy-start(f32[9,128,256]{2,1,0:T(8,128)} %phi.7) | copy-start | bytes 3538948
  0.7 2.7 %copy-start.1 = (f32[9,128,256]{2,1,0:T(8,128)S(1)}, f32[9,128,256]{2,1,0:T(8,128)}, u32[]{:S(2)}) copy-start(f32[9,128,256]{2,1,0:T(8,128)} %forcing.3) | copy-start | bytes 3538948
  0.7 2.7 %copy-start.7 = (f32[6,2]{0,1:T(2,128)S(1)}, f32[6,2]{0,1:T(2,128)}, u32[]{:S(2)}) copy-start(f32[6,2]{0,1:T(2,128)} %param.17) | copy-start | bytes 148
  0.7 2.7 %copy-start.6 = (f32[6,6,2]{1,2,0:T(2,128)S(1)}, f32[6,6,2]{1,2,0:T(2,128)}, u32[]{:S(2)}) copy-start(f32[6,6,2]{1,2,0:T(2,128)} %param.16) | copy-start | bytes 868
  2.1 4.1 %collective-permute-start = (f32[10,8,256]{2,1,0:T(8,128)S(1)}, f32[10,8,256]{2,1,0:T(8,128)S(1)}, u32[]{:S(2)}, u32[]{:S(2)}) collective-permute-start(f32[10,8,256]{2,1,0:T(8,128)S(1)} %get-tuple-element.23), channel_id=1, source_target_pairs={{0,4},{4,0},{8,12},{12,8},{16,20},{20,16},{24,28},{28,24},{1,5},{5... | collective-permute-start | bytes 245768 | tf_op jit(solution)/shard_map/ppermute | solution.py:609
  2.6 3.6 %collective-permute-start.1 = (f32[10,8,256]{2,1,0:T(8,128)S(1)}, f32[10,8,256]{2,1,0:T(8,128)S(1)}, u32[]{:S(2)}, u32[]{:S(2)}) collective-permute-start(f32[10,8,256]{2,1,0:T(8,128)S(1)} %get-tuple-element.24), channel_id=1, source_target_pairs={{4,8},{12,16},{20,24},{8,4},{16,12},{24,20},{5,9},{13,17},{21,25},... | collective-permute-start | bytes 245768 | tf_op jit(solution)/shard_map/ppermute | solution.py:615
  6.2 3.7 %copy-start.4 = (f32[6,128,256]{2,1,0:T(8,128)S(1)}, f32[6,128,256]{2,1,0:T(8,128)}, u32[]{:S(2)}) copy-start(f32[6,128,256]{2,1,0:T(8,128)} %modes.1) | copy-start | bytes 2359300
  6.3 3.7 %copy-start.8 = (s32[128,2]{0,1:T(2,128)S(1)}, s32[128,2]{0,1:T(2,128)}, u32[]{:S(2)}) copy-start(s32[128,2]{0,1:T(2,128)} %param.15) | copy-start | bytes 3076
  6.3 4.9 %copy-start.5 = (f32[9,9]{1,0:T(8,128)S(1)}, f32[9,9]{1,0:T(8,128)}, u32[]{:S(2)}) copy-start(f32[9,9]{1,0:T(8,128)} %mix.1) | copy-start | bytes 976
  6.7 4.5 %collective-permute-start.2 = (f32[72,128]{1,0:T(8,128)S(1)}, f32[72,128]{1,0:T(8,128)S(1)}, u32[]{:S(2)}, u32[]{:S(2)}) collective-permute-start(f32[72,128]{1,0:T(8,128)S(1)} %get-tuple-element.29), channel_id=1, source_target_pairs={{0,1},{1,0},{2,3},{3,2},{4,5},{5,4},{6,7},{7,6},{8,9},{9,8},{10,11... | collective-permute-start | bytes 110600 | tf_op jit(solution)/shard_map/ppermute | solution.py:609
  9.2 1.9 %collective-permute-start.3 = (f32[72,128]{1,0:T(8,128)S(1)}, f32[72,128]{1,0:T(8,128)S(1)}, u32[]{:S(2)}, u32[]{:S(2)}) collective-permute-start(f32[72,128]{1,0:T(8,128)S(1)} %get-tuple-element.30), channel_id=1, source_target_pairs={{1,2},{2,1},{5,6},{6,5},{9,10},{10,9},{13,14},{14,13},{17,18},{18,... | collective-permute-start | bytes 110600 | tf_op jit(solution)/shard_map/ppermute | solution.py:615
  19.6 3.2 %collective-permute-start.4 = (f32[32,128]{1,0:T(8,128)S(1)}, f32[32,128]{1,0:T(8,128)S(1)}, u32[]{:S(2)}, u32[]{:S(2)}) collective-permute-start(f32[32,128]{1,0:T(8,128)S(1)} %get-tuple-element.34), channel_id=1, source_target_pairs={{0,4},{4,0},{8,12},{12,8},{16,20},{20,16},{24,28},{28,24},{1,5},{5... | collective-permute-start | bytes 49160 | tf_op jit(solution)/shard_map/ppermute | solution.py:626
  22.8 4.2 %collective-permute-start.5 = (f32[32,128]{1,0:T(8,128)S(1)}, f32[32,128]{1,0:T(8,128)S(1)}, u32[]{:S(2)}, u32[]{:S(2)}) collective-permute-start(f32[32,128]{1,0:T(8,128)S(1)} %add.18), channel_id=1, source_target_pairs={{0,8},{4,12},{8,0},{12,4},{16,24},{20,28},{24,16},{28,20},{1,9},{5... | collective-permute-start | bytes 49160 | tf_op jit(solution)/shard_map/ppermute | solution.py:626
  27.0 4.8 %collective-permute-start.6 = (f32[32,128]{1,0:T(8,128)S(1)}, f32[32,128]{1,0:T(8,128)S(1)}, u32[]{:S(2)}, u32[]{:S(2)}) collective-permute-start(f32[32,128]{1,0:T(8,128)S(1)} %add.19), channel_id=1, source_target_pairs={{0,16},{4,20},{8,24},{12,28},{16,0},{20,4},{24,8},{28,12},{1,17},{... | collective-permute-start | bytes 49160 | tf_op jit(solution)/shard_map/ppermute | solution.py:626
  31.8 7.0 %collective-permute-start.9 = (f32[32,128]{1,0:T(8,128)S(1)}, f32[32,128]{1,0:T(8,128)S(1)}, u32[]{:S(2)}, u32[]{:S(2)}) collective-permute-start(f32[32,128]{1,0:T(8,128)S(1)} %add.20), channel_id=1, source_target_pairs={{0,3},{1,2},{2,1},{3,0},{4,7},{5,6},{6,5},{7,4},{8,11},{9,10},{10,... | collective-permute-start | bytes 49160 | tf_op jit(solution)/shard_map/ppermute | solution.py:626
  34.2 5.3 %collective-permute-start.8 = (f32[32,128]{1,0:T(8,128)S(1)}, f32[32,128]{1,0:T(8,128)S(1)}, u32[]{:S(2)}, u32[]{:S(2)}) collective-permute-start(f32[32,128]{1,0:T(8,128)S(1)} %add.20), channel_id=1, source_target_pairs={{0,2},{1,3},{2,0},{3,1},{4,6},{5,7},{6,4},{7,5},{8,10},{9,11},{10,... | collective-permute-start | bytes 49160 | tf_op jit(solution)/shard_map/ppermute | solution.py:626
  37.8 3.7 %collective-permute-start.7 = (f32[32,128]{1,0:T(8,128)S(1)}, f32[32,128]{1,0:T(8,128)S(1)}, u32[]{:S(2)}, u32[]{:S(2)}) collective-permute-start(f32[32,128]{1,0:T(8,128)S(1)} %add.20), channel_id=1, source_target_pairs={{0,1},{1,0},{2,3},{3,2},{4,5},{5,4},{6,7},{7,6},{8,9},{9,8},{10,11... | collective-permute-start | bytes 49160 | tf_op jit(solution)/shard_map/ppermute | solution.py:626

commit v6 on v5

--- a/solution.py
+++ b/solution.py
@@ -26,40 +26,34 @@
     return pl.ds(pl.multiple_of(index * SUB, SUB), SUB)
 
 
-def stencil(ref, row, wanted, tiles, levels, coefs, lane, wrap):
-    for t in wanted:
-        center = {
-            u: [ref[u % tiles, l, pl.ds(row, SUB), :] for l in range(levels)]
-            for u in (t - 1, t, t + 1)
-        }
-        horiz, vert = coefs[t]
-        last_coef = 5.0 * horiz + vert
-        mid_coef = last_coef + vert
-        horiz12 = horiz * (1.0 / 12.0)
-        per_level = []
-        for l in range(levels):
-            x = center[t][l]
-            after = center[t + 1][l] if wrap or t + 1 < tiles else 0.0
-            before = center[t - 1][l] if wrap or t > 0 else 0.0
-
-            def rows_at(offset):
-                return ref[t, l, pl.ds(row + offset, SUB), :]
-
-            right1 = pltpu.roll(jnp.where(lane < 1, after, x), LANES - 1, 1)
-            right2 = pltpu.roll(jnp.where(lane < 2, after, x), LANES - 2, 1)
-            left1 = pltpu.roll(jnp.where(lane >= LANES - 1, before, x), 1, 1)
-            left2 = pltpu.roll(jnp.where(lane >= LANES - 2, before, x), 2, 1)
-            nearest = (rows_at(-1) + rows_at(1)) + (right1 + left1)
-            farther = (rows_at(-2) + rows_at(2)) + (right2 + left2)
-            if l == 0:
-                beside = center[t][1]
-            elif l == levels - 1:
-                beside = center[t][l - 1]
-            else:
-                beside = center[t][l - 1] + center[t][l + 1]
-            coef = last_coef if l == levels - 1 else mid_coef
-            per_level.append(coef * x + horiz12 * (farther - FAR * nearest) - vert * beside)
-        yield t, per_level
+def stencil(ref, row, t, tiles, levels, coefs, lane, wrap):
+    here = pl.ds(row, SUB)
+    horiz, vert = coefs
+    last_coef = 5.0 * horiz + vert
+    mid_coef = last_coef + vert
+    horiz12 = horiz * (1.0 / 12.0)
+    for l in range(levels):
+        x = ref[t, l, here, :]
+        after = ref[(t + 1) % tiles, l, here, :] if wrap or t + 1 < tiles else 0.0
+        before = ref[(t - 1) % tiles, l, here, :] if wrap or t > 0 else 0.0
+
+        def rows_at(offset):
+            return ref[t, l, pl.ds(row + offset, SUB), :]
+
+        right1 = pltpu.roll(jnp.where(lane < 1, after, x), LANES - 1, 1)
+        right2 = pltpu.roll(jnp.where(lane < 2, after, x), LANES - 2, 1)
+        left1 = pltpu.roll(jnp.where(lane >= LANES - 1, before, x), 1, 1)
+        left2 = pltpu.roll(jnp.where(lane >= LANES - 2, before, x), 2, 1)
+        nearest = (rows_at(-1) + rows_at(1)) + (right1 + left1)
+        farther = (rows_at(-2) + rows_at(2)) + (right2 + left2)
+        if l == 0:
+            beside = ref[t, 1, here, :]
+        elif l == levels - 1:
+            beside = ref[t, l - 1, here, :]
+        else:
+            beside = ref[t, l - 1, here, :] + ref[t, l + 1, here, :]
+        coef = last_coef if l == levels - 1 else mid_coef
+        yield coef * x + horiz12 * (farther - FAR * nearest) - vert * beside
 
 
 def strip_kernel(phi, forcing, horiz_in, vert_in, near_out, far_out, phi_s, res_s, horiz, vert, sems):
@@ -94,12 +88,12 @@
             (horiz[end, :, t * LANES : (t + 1) * LANES], vert[end, :, t * LANES : (t + 1) * LANES])
             for t in range(blocks)
         ]
-        image = stencil(phi_s.at[end], SUB, range(blocks), blocks, levels, coefs, lane, False)
         strips = {}
-        for t, image_t in image:
-            for l in range(levels):
+        for t in range(blocks):
+            image = stencil(phi_s.at[end], SUB, t, blocks, levels, coefs[t], lane, False)
+            for l, value in enumerate(image):
                 potential = phi_s[end, t, l, SUB : 2 * SUB, :]
-                strips[t, l] = (res_s[end, t, l] - image_t[l], potential)
+                strips[t, l] = (res_s[end, t, l] - value, potential)
             strips[t, levels] = coefs[t]
         kept.append(strips)
     for place, (a_top, b_top) in kept[0].items():
@@ -156,15 +150,12 @@
     def residual(i, carry):
         here = tile_at(i)
         row = pl.multiple_of(i * SUB + SUB, SUB)
-        coefs = []
         for t in range(blocks):
             lanes = pl.ds(t * LANES, LANES)
-            coefs.append((horiz[here, lanes], vert[here, lanes]))
-        image = stencil(phi_s, row, range(blocks), blocks, levels, coefs, lane, False)
-        for t, image_t in image:
-            for l in range(levels):
-                own = forcing[l, here, pl.ds(t * LANES, LANES)]
-                res[t, l, here, :] = own - image_t[l]
+            coefs = (horiz[here, lanes], vert[here, lanes])
+            image = stencil(phi_s, row, t, blocks, levels, coefs, lane, False)
+            for l, value in enumerate(image):
+                res[t, l, here, :] = forcing[l, here, lanes] - value
         return carry
 
     lax.fori_loop(0, rows // SUB, residual, 0, unroll=2)
@@ -290,23 +281,85 @@
         far_out[i * SUB : (i + 1) * SUB, :] = jnp.where(col_even, to_left, to_right)
 
 
-def ahead_kernel(body_total, after, modes, bodies_t, modes_t, hits, hits_t):
+def ahead_kernel(
+    body_total,
+    res,
+    edge,
+    horiz_in,
+    vert_in,
+    edge_coef,
+    mix,
+    modes,
+    bodies_t,
+    modes_t,
+    hits,
+    hits_t,
+    early,
+    res_own,
+    horiz,
+    vert,
+    scale,
+):
+    blocks, levels, rows, _ = res.shape
+    row_tiles = rows // SUB
     mode_count = modes.shape[0]
-    for t in range(hits.shape[0]):
+    for t in range(blocks):
         for k in range(mode_count):
             modes_t[t, k] = modes[k, :, t * LANES : (t + 1) * LANES].T
         found = body_hits(bodies_t, t, body_total, hits.shape[1])
         hits[t] = found
         hits_t[t] = found.T
 
+    def direction(i, own, residuals, coefs):
+        there = tile_at(i + 1)
+        for t in range(blocks):
+            h, v = coefs[t]
+            bottom = 5.0 * h + 2.0 * v
+            inside = bottom > 0.0
+            factor = jnp.where(inside, 1.0 / jnp.where(inside, bottom, 1.0), 0.0)
+            scale[t, there, :] = factor
+            horiz[t, there, :] = h
+            vert[t, there, :] = v
+            if own:
+                for l in range(levels):
+                    res_own[t, l, there, :] = residuals[t][l]
+            weighted = [value * factor for value in residuals[t]]
+            for l, value in enumerate(mix_levels(mix, weighted, levels)):
+                early[t, l, there, :] = value
+
+    def own_coefs(i):
+        here = tile_at(i)
+        result = []
+        for t in range(blocks):
+            lanes = pl.ds(t * LANES, LANES)
+            result.append((horiz_in[here, lanes], vert_in[here, lanes]))
+        return result
+
+    for n, i in enumerate((0, 1, row_tiles, row_tiles + 1)):
+        own = 1 <= i <= row_tiles
+        residuals = [[edge[n, t, l] for l in range(levels)] for t in range(blocks)]
+        if own:
+            coefs = own_coefs(i - 1)
+        else:
+            coefs = [(edge_coef[n // 2, 0, t], edge_coef[n // 2, 1, t]) for t in range(blocks)]
+        direction(i, own, residuals, coefs)
+
+    def body(i, carry):
+        here = tile_at(i - 1)
+        residuals = [[res[t, l, here, :] for l in range(levels)] for t in range(blocks)]
+        direction(i, True, residuals, own_coefs(i - 1))
+        return carry
+
+    lax.fori_loop(2, row_tiles, body, 0, unroll=2)
+
 
 def main_kernel(
     body_total,
-    res,
-    edge,
+    early,
+    res_own,
     horiz,
     vert,
-    edge_coef,
+    scale,
     own,
     col_near,
     col_far,
@@ -324,7 +377,8 @@
     scale_s,
     got_s,
 ):
-    blocks, levels, rows, _ = res.shape
+    blocks, levels, padded, _ = early.shape
+    rows = padded - 4 * SUB
     mode_count = modes_t.shape[1]
     tiles = blocks + 1
     side = blocks
@@ -346,120 +400,125 @@
         there = pl.ds((i + fold) * SUB, SUB)
         got_s[there, :] = jnp.where(from_left, left, right)
 
-    def first(i, inner, residuals, coefs):
-        here = tile_at(i)
-        there = tile_at(i + 1)
-        got, mine = got_s[here, :], own[here, :]
-        halo = (lane < 4) | (lane >= LANES - 4)
-        slot = coef_slot(levels)
-        side_coef = [
-            jnp.where(halo, pltpu.roll(got, (LANES - 4 - slot - 8 * n) % LANES, 1), 0.0) for n in range(2)
-        ]
-        coefs = list(coefs) + [tuple(side_coef)]
-        outer = (lane < 2, lane >= LANES - 2, (lane < 2) | (lane >= LANES - 2))
-        scales, edges = [], []
-        for t in everything:
-            h, v = coefs[t]
+    halo = (lane < 4) | (lane >= LANES - 4)
+    half = LANES // 2
+    slot = coef_slot(levels)
+
+    def first(group, inner):
+        starts, ends = lane < 2, lane >= LANES - 2
+        weighted = []
+        for i in group:
+            there, here = tile_at(i + 1), tile_at(i)
+            got, mine = got_s[here, :], own[here, :]
+            h, v = [
+                jnp.where(halo, pltpu.roll(got, (LANES - 4 - slot - 8 * n) % LANES, 1), 0.0)
+                for n in range(2)
+            ]
             bottom = 5.0 * h + 2.0 * v
             inside = bottom > 0.0
-            scale = jnp.where(inside, 1.0 / jnp.where(inside, bottom, 1.0), 0.0)
-            scales.append(scale)
-            scale_s[t, there, :] = scale
-            horiz_s[t, there, :] = h
-            vert_s[t, there, :] = v
-            if t == side:
-                mask = outer[2]
-            elif blocks == 1:
-                mask = outer[2]
-            elif t == 0:
-                mask = outer[0]
-            elif t == blocks - 1:
-                mask = outer[1]
-            else:
-                mask = None
-            edges.append(None if mask is None else jnp.where(mask, h * (1.0 / 12.0), 0.0))
-        weighted = [[] for _ in everything]
+            factor = jnp.where(inside, 1.0 / jnp.where(inside, bottom, 1.0), 0.0)
+            scale_s[there, :] = factor
+            horiz_s[there, :] = h
+            vert_s[there, :] = v
+            side_edge = jnp.where(starts | ends, h * (factor * (1.0 / 12.0)), 0.0)
+            first_edge = jnp.where(starts, horiz[0, there, :] * (1.0 / 12.0), 0.0)
+            last_edge = jnp.where(ends, horiz[side - 1, there, :] * (1.0 / 12.0), 0.0)
+            both = first_edge * scale[0, there, :] + last_edge * scale[side - 1, there, :]
+            both = pltpu.roll(both, half, 1)
+            values = []
+            for l in range(levels):
+                place = (LANES - 2 - 8 * levels - 4 * l) % LANES
+                ours = pltpu.roll(mine, place, 1)
+                beyond = pltpu.roll(got, (LANES - 4 - 8 * l) % LANES, 1)
+                across = pltpu.roll(got, (place + half) % LANES, 1)
+                values.append(beyond * factor - side_edge * ours - both * across)
+                if inner:
+                    theirs = pltpu.roll(got, place, 1)
+                    terms = [jnp.zeros_like(theirs)] * blocks
+                    terms[0] = terms[0] + first_edge * theirs
+                    terms[-1] = terms[-1] + last_edge * theirs
+                    for t in range(blocks):
+                        res_s[t, l, there, :] = res_own[t, l, there, :] - terms[t]
+            weighted.append(values)
+        mixed = [mix_levels(mix, values, levels) for values in weighted]
+        turned = [[pltpu.roll(value, half, 1) for value in values] for values in mixed]
+        for n, i in enumerate(group):
+            there = tile_at(i + 1)
+            for l in range(levels):
+                dir_s[side, l, there, :] = mixed[n][l]
+                changes = [jnp.zeros((SUB, LANES), F32)] * blocks
+                changes[0] = changes[0] + jnp.where(starts, turned[n][l], 0.0)
+                changes[-1] = changes[-1] + jnp.where(ends, turned[n][l], 0.0)
+                for t in range(blocks):
+                    dir_s[t, l, there, :] = early[t, l, there, :] + changes[t]
+
+    def first_body(i, carry):
+        first([8 * i + n + 1 for n in range(8)], True)
+        return carry
+
+    first([0, row_tiles + 1], False)
+    lax.fori_loop(0, row_tiles // 8, first_body, 0, unroll=1)
+
+    def coefs_at(t, row):
+        here = pl.ds(row, SUB)
+        if t == side:
+            return horiz_s[here, :], vert_s[here, :]
+        return horiz[t, here, :], vert[t, here, :]
+
+    def second(group):
+        rows_of = [pl.multiple_of(i * SUB + SUB, SUB) for i in group]
+        waiting = None
+        for row in rows_of:
+            for t in everything:
+                here = pl.ds(row, SUB)
+                factor = scale_s[here, :] if t == side else scale[t, here, :]
+                weighted = []
+                image = stencil(dir_s, row, t, tiles, levels, coefs_at(t, row), lane, True)
+                for l, value in enumerate(image):
+                    img_s[t, l, here, :] = value
+                    weighted.append(value * factor)
+                    if waiting:
+                        part_s[waiting[0], l, waiting[1], :] = mix_level(mix, waiting[2], l)
+                waiting = (t, here, weighted)
         for l in range(levels):
-            place = (LANES - 2 - 8 * levels - 4 * l) % LANES
-            theirs = pltpu.roll(got, place, 1)
-            ours = pltpu.roll(mine, place, 1)
-            for t in everything:
-                if t == side:
-                    value = pltpu.roll(got, (LANES - 4 - 8 * l) % LANES, 1) - edges[t] * ours
-                else:
-                    value = residuals[t][l]
-                    if edges[t] is not None:
-                        value = value - edges[t] * theirs
-                    if inner:
-                        res_s[t, l, there, :] = value
-                weighted[t].append(value * scales[t])
-        for t in everything:
-            for l, value in enumerate(mix_levels(mix, weighted[t], levels)):
-                dir_s[t, l, there, :] = value
-
-    def own_coefs(i):
-        here = tile_at(i)
-        result = []
-        for t in range(blocks):
-            lanes = pl.ds(t * LANES, LANES)
-            result.append((horiz[here, lanes], vert[here, lanes]))
-        return result
-
-    for n, i in enumerate((0, 1, row_tiles, row_tiles + 1)):
-        residuals = [[edge[n, t, l] for l in range(levels)] for t in range(blocks)]
-        if 1 <= i <= row_tiles:
-            coefs = own_coefs(i - 1)
-        else:
-            coefs = [(edge_coef[n // 2, 0, t], edge_coef[n // 2, 1, t]) for t in range(blocks)]
-        first(i, 1 <= i <= row_tiles, residuals, coefs)
-
-    def first_body(i, carry):
-        here = tile_at(i - 1)
-        residuals = [[res[t, l, here, :] for l in range(levels)] for t in range(blocks)]
-        first(i, True, residuals, own_coefs(i - 1))
+            part_s[waiting[0], l, waiting[1], :] = mix_level(mix, waiting[2], l)
+
+    def second_body(i, carry):
+        second([9 * i + n for n in range(9)])
         return carry
 
-    lax.fori_loop(2, row_tiles, first_body, 0, unroll=7)
-
-    def coefs_at(row, count):
-        here = pl.ds(row, SUB)
-        return [(horiz_s[t, here, :], vert_s[t, here, :]) for t in range(count)]
-
-    def second(i, carry):
-        row = pl.multiple_of(i * SUB + SUB, SUB)
-        here = pl.ds(row, SUB)
-        image = stencil(
-            dir_s, row, everything, tiles, levels, coefs_at(row, tiles), lane, True
-        )
-        for t, image_t in image:
-            scale = scale_s[t, here, :]
-            weighted = []
-            for l in range(levels):
-                img_s[t, l, here, :] = image_t[l]
-                weighted.append(image_t[l] * scale)
-            for l, value in enumerate(mix_levels(mix, weighted, levels)):
-                part_s[t, l, here, :] = value
-        return carry
+    lax.fori_loop(0, (row_tiles + 2) // 9, second_body, 0, unroll=1)
+    for i in range((row_tiles + 2) // 9 * 9, row_tiles + 2):
+        second([i])
 
     def third(i, totals):
-        row = pl.multiple_of(i * SUB + SUB, SUB)
-        here = pl.ds(row, SUB)
-        image = stencil(
-            part_s, row, range(blocks), tiles, levels, coefs_at(row, blocks), lane, True
-        )
         totals = list(totals)
-        for t, image_t in image:
-            for l in range(levels):
-                residual = res_s[t, l, here, :]
-                img1 = img_s[t, l, here, :]
-                img2 = image_t[l]
-                products = (residual * img1, img1 * img1, residual * img2, img1 * img2, img2 * img2)
-                totals = [total + product for total, product in zip(totals, products)]
+        waiting = None
+
+        def add(t, l, here, img2):
+            residual = res_s[t, l, here, :]
+            img1 = img_s[t, l, here, :]
+            products = (residual * img1, img1 * img1, residual * img2, img1 * img2, img2 * img2)
+            for n, product in enumerate(products):
+                totals[n] = totals[n] + product
+
+        for n in range(16):
+            row = pl.multiple_of((16 * i + n) * SUB + base, SUB)
+            here = pl.ds(row, SUB)
+            for t in range(blocks):
+                values = []
+                image = stencil(part_s, row, t, tiles, levels, coefs_at(t, row), lane, True)
+                for l, value in enumerate(image):
+                    values.append(value)
+                    if waiting:
+                        add(waiting[0], l, waiting[1], waiting[2][l])
+                waiting = (t, here, values)
+        for l in range(levels):
+            add(waiting[0], l, waiting[1], waiting[2][l])
         return tuple(totals)
 
     zero = jnp.zeros((SUB, LANES), F32)
-    lax.fori_loop(0, row_tiles + 2, second, 0, unroll=3)
-    totals = lax.fori_loop(1, row_tiles + 1, third, (zero,) * 5, unroll=4)
+    totals = lax.fori_loop(0, row_tiles // 16, third, (zero,) * 5, unroll=1)
 
     width = message.shape[1]
     surface_rows = pl.ds(base, rows)
@@ -484,15 +543,16 @@
     message[SUB:, :] = table[...]
 
 
+def mix_level(mix, weighted, l):
+    total = (mix[l, l] + 1.0) * weighted[l]
+    for m, value in enumerate(weighted):
+        if m != l:
+            total = total + mix[l, m] * value
+    return total
+
+
 def mix_levels(mix, weighted, levels):
-    out = []
-    for l in range(levels):
-        total = (mix[l, l] + 1.0) * weighted[l]
-        for m in range(levels):
-            if m != l:
-                total = total + mix[l, m] * weighted[m]
-        out.append(total)
-    return out
+    return [mix_level(mix, weighted, l) for l in range(levels)]
 
 
 def body_hits(bodies_t, block, count, width):
@@ -711,27 +771,31 @@
         (res, start_potential, horiz_coef, vert_coef, row_near, row_far, packed),
     )
     col_near, col_far = swap_near(near, "gy"), swap_far(far, "gy")
-    modes_t, hits, hits_t = call(
+    field = (tiles, levels, padded, LANES)
+    early_field = (blocks, levels, padded, LANES)
+    plane = (blocks, padded, LANES)
+    modes_t, hits, hits_t, early, res_own, horiz, vert, scale = call(
         functools.partial(ahead_kernel, body_total),
         "ahead_kernel",
-        [((blocks, mode_count, LANES, rows), VMEM), ((blocks, width, rows), VMEM), ((blocks, rows, width), VMEM)],
-        [VMEM] * 3,
-        (edge_coef, mode_shapes, bodies_t),
-    )
-
-    field = (tiles, levels, padded, LANES)
-    plane = pltpu.VMEM((tiles, padded, LANES), F32)
+        [((blocks, mode_count, LANES, rows), VMEM), ((blocks, width, rows), VMEM), ((blocks, rows, width), VMEM)]
+        + [(early_field, VMEM)] * 2
+        + [(plane, VMEM)] * 3,
+        [VMEM] * 5 + [SMEM] + [VMEM] * 2,
+        (res, edge, horiz_coef, vert_coef, edge_coef, vert_mix, mode_shapes, bodies_t),
+    )
+
+    side_plane = pltpu.VMEM((padded, LANES), F32)
     direction, part, message = call(
         functools.partial(main_kernel, body_total),
         "main_kernel",
         [(field, VMEM), (field, VMEM), ((4 * SUB, width), VMEM)],
         [VMEM] * 9 + [SMEM] + [VMEM] * 2,
         (
-            res,
-            edge,
-            horiz_coef,
-            vert_coef,
-            edge_coef,
+            early,
+            res_own,
+            horiz,
+            vert,
+            scale,
             own,
             col_near,
             col_far,
@@ -743,9 +807,9 @@
         [
             pltpu.VMEM((blocks, levels, padded, LANES), F32),
             pltpu.VMEM(field, F32),
-            plane,
-            plane,
-            plane,
+            side_plane,
+            side_plane,
+            side_plane,
             pltpu.VMEM(packed_shape, F32),
         ],
     )

time: 43.1 us -> 42 us (0.974)
  starting transfers between devices: 19.3 us -> 17.5 us
  Pallas kernels: 14.8 us -> 15.4 us
    ppermute x6, starting transfers between devices: 14.9 us -> 13.1 us  [sum_over(): total = total + lax.ppermute(value, axis, pairs)]
    ppermute x2, waiting for transfers between devices: 0.98 us -> 0.01 us  [swap_near(): return lax.ppermute(value, axis, [(i, i ^ 1) for i in range(size)])]
    ppermute x6, waiting for transfers between devices: 7.02 us -> 7.97 us  [sum_over(): total = total + lax.ppermute(value, axis, pairs)]
    pallas_call x6, Pallas kernels: 14.8 us -> 15.4 us  [call(): pl.pallas_call(kernel, out_shape=tuple((jax.ShapeDtypeStruct(shape, F32)...]
  transfers between devices with their start and end apart: 10 -> 10, of which waited for: 6 -> 5; matrix products, arithmetic and copies ran while one was open for 0% -> 0% of each run, Pallas kernels for 7% -> 12%
where the time goes in v6:
time: 42 us; the launch traced here: 41.8 us
  starting transfers between devices  17.5 us (42%)
  Pallas kernels  15.4 us (37%)
  waiting for transfers between devices  7.98 us (19%)
  between operations  0.86 us (2%)
    pallas_call x6, Pallas kernels, call(): pl.pallas_call(kernel, out_shape=tuple((jax.ShapeDtypeStruct(shape, F32)...  15.4 us
    ppermute x6, starting transfers between devices, sum_over(): total = total + lax.ppermute(value, axis, pairs)  13.1 us
    ppermute x6, waiting for transfers between devices, sum_over(): total = total + lax.ppermute(value, axis, pairs)  7.97 us
    ppermute x2, starting transfers between devices, swap_near(): return lax.ppermute(value, axis, [(i, i ^ 1) for i in range(size)])  3.09 us
    ppermute x2, starting transfers between devices, swap_far(): return lax.ppermute(value, axis, pairs + [(j, i) for i, j in pairs])  1.31 us
  transfers between devices with their start and end apart: 10, of which 5 were waited for; matrix products, arithmetic and copies ran while one was open for 0% of the time, Pallas kernels for 12%

profile of v6, /device:TPU:0, one launch (start us, length us, event | category | flops | bytes accessed | tf_op | source)
XLA Modules:
  0.0 41.8 jit_solution(4189989655180813632)
XLA Ops:
  0.7 1.4 %strip_kernel.1 = (f32[10,8,256]{2,1,0:T(8,128)S(1)}, f32[10,8,256]{2,1,0:T(8,128)S(1)}) custom-call(f32[9,128,256]{2,1,0:T(8,128)} %phi.7, f32[9,128,256]{2,1,0:T(8,128)} %forcing.3, f32[128,256]{1,0:T(8,128)} %horiz_in.3, f32[128,256]{1,0:T(8,128)} %vert_in.3), custom_call_target="tpu_custom_call" | custom-call | tf_op jit(solution)/shard_map/strip_kernel/pallas_call | solution.py:717
  2.1 0.5 %collective-permute-start = (f32[10,8,256]{2,1,0:T(8,128)S(1)}, f32[10,8,256]{2,1,0:T(8,128)S(1)}, u32[]{:S(2)}, u32[]{:S(2)}) collective-permute-start(f32[10,8,256]{2,1,0:T(8,128)S(1)} %get-tuple-element.28), channel_id=1, source_target_pairs={{0,4},{4,0},{8,12},{12,8},{16,20},{20,16},{24,28},{28,24},{1,5},{5... | collective-permute-start | bytes 245768 | tf_op jit(solution)/shard_map/ppermute | solution.py:669
  2.6 0.7 %collective-permute-start.1 = (f32[10,8,256]{2,1,0:T(8,128)S(1)}, f32[10,8,256]{2,1,0:T(8,128)S(1)}, u32[]{:S(2)}, u32[]{:S(2)}) collective-permute-start(f32[10,8,256]{2,1,0:T(8,128)S(1)} %get-tuple-element.29), channel_id=1, source_target_pairs={{4,8},{12,16},{20,24},{8,4},{16,12},{24,20},{5,9},{13,17},{21,25},... | collective-permute-start | bytes 245768 | tf_op jit(solution)/shard_map/ppermute | solution.py:675
  3.4 2.9 %inner_kernel.1 = (f32[2,9,128,128]{3,2,1,0:T(8,128)S(1)}, f32[144,128]{1,0:T(8,128)S(1)}, f32[24,128]{1,0:T(8,128)S(1)}) custom-call(f32[9,128,256]{2,1,0:T(8,128)S(1)} %copy-done, f32[9,128,256]{2,1,0:T(8,128)S(1)} %copy-done.1, f32[128,256]{1,0:T(8,128)S(1)} %copy-done.2, f32[128,256]{1,0:T(8,128)S(1)} %copy-done.3, f32[6,2,6]{2,1,0:T(2,128)S(1)} %bitcast.4, ...), custom_call_target="tpu_custom_call" | custom-call | tf_op jit(solution)/shard_map/inner_kernel/pallas_call | solution.py:717
  6.2 0.0 copy-start.4
  6.3 0.0 copy-start.5
  6.3 0.0 copy-start.8
  6.3 0.4 edge_kernel.1
  6.7 2.6 %collective-permute-start.2 = (f32[72,128]{1,0:T(8,128)S(1)}, f32[72,128]{1,0:T(8,128)S(1)}, u32[]{:S(2)}, u32[]{:S(2)}) collective-permute-start(f32[72,128]{1,0:T(8,128)S(1)} %get-tuple-element.39), channel_id=1, source_target_pairs={{0,1},{1,0},{2,3},{3,2},{4,5},{5,4},{6,7},{7,6},{8,9},{9,8},{10,11... | collective-permute-start | bytes 110600 | tf_op jit(solution)/shard_map/ppermute | solution.py:669
  9.3 0.7 %collective-permute-start.3 = (f32[72,128]{1,0:T(8,128)S(1)}, f32[72,128]{1,0:T(8,128)S(1)}, u32[]{:S(2)}, u32[]{:S(2)}) collective-permute-start(f32[72,128]{1,0:T(8,128)S(1)} %get-tuple-element.40), channel_id=1, source_target_pairs={{1,2},{2,1},{5,6},{6,5},{9,10},{10,9},{13,14},{14,13},{17,18},{18,... | collective-permute-start | bytes 110600 | tf_op jit(solution)/shard_map/ppermute | solution.py:675
  9.9 2.2 %ahead_kernel.1 = (f32[2,6,128,128]{3,2,1,0:T(8,128)S(1)}, f32[2,128,128]{2,1,0:T(8,128)S(1)}, f32[2,128,128]{2,1,0:T(8,128)S(1)}, f32[2,9,160,128]{3,2,1,0:T(8,...) custom-call(f32[2,9,128,128]{3,2,1,0:T(8,128)S(1)} %get-tuple-elemen, ...), custom_call_target="tpu_custom_call" | custom-call | tf_op jit(solution)/shard_map/ahead_kernel/pallas_call | solution.py:717
  12.2 7.1 %main_kernel.1 = (f32[3,9,160,128]{3,2,1,0:T(8,128)S(1)}, f32[3,9,160,128]{3,2,1,0:T(8,128)S(1)}, f32[32,128]{1,0:T(8,128)S(1)}) custom-call(f32[2,9,160,128]{3,2,1,0:T(8,128)S(1)} %get-tuple-element.33.early, f32[2,9,160,128]{3,2,1,0:T(8,128)S(1)} %get-tuple-element.34.res_own, f32[2,160,128]{2,1,0:T(8,128)S(1)} %get-tuple-element.35.horiz, ...), custom_call_target="tpu_custom_call" | custom-call | tf_op jit(solution)/shard_map/main_kernel/pallas_call | solution.py:717
  19.3 2.7 %collective-permute-start.4 = (f32[32,128]{1,0:T(8,128)S(1)}, f32[32,128]{1,0:T(8,128)S(1)}, u32[]{:S(2)}, u32[]{:S(2)}) collective-permute-start(f32[32,128]{1,0:T(8,128)S(1)} %get-tuple-element.44), channel_id=1, source_target_pairs={{0,4},{4,0},{8,12},{12,8},{16,20},{20,16},{24,28},{28,24},{1,5},{5... | collective-permute-start | bytes 49160 | tf_op jit(solution)/shard_map/ppermute | solution.py:686
  22.0 0.8 %collective-permute-done.4 = f32[32,128]{1,0:T(8,128)S(1)} collective-permute-done((f32[32,128]{1,0:T(8,128)S(1)}, f32[32,128]{1,0:T(8,128)S(1)}, u32[]{:S(2)}, u32[]{:S(2)}) %collective-permute-start.4) | collective-permute-done | bytes 16416 | tf_op jit(solution)/shard_map/ppermute | solution.py:686
  22.8 1.6 %collective-permute-start.5 = (f32[32,128]{1,0:T(8,128)S(1)}, f32[32,128]{1,0:T(8,128)S(1)}, u32[]{:S(2)}, u32[]{:S(2)}) collective-permute-start(f32[32,128]{1,0:T(8,128)S(1)} %add.18), channel_id=1, source_target_pairs={{0,8},{4,12},{8,0},{12,4},{16,24},{20,28},{24,16},{28,20},{1,9},{5... | collective-permute-start | bytes 49160 | tf_op jit(solution)/shard_map/ppermute | solution.py:686
  24.4 2.2 %collective-permute-done.5 = f32[32,128]{1,0:T(8,128)S(1)} collective-permute-done((f32[32,128]{1,0:T(8,128)S(1)}, f32[32,128]{1,0:T(8,128)S(1)}, u32[]{:S(2)}, u32[]{:S(2)}) %collective-permute-start.5) | collective-permute-done | bytes 16416 | tf_op jit(solution)/shard_map/ppermute | solution.py:686
  26.6 2.6 %collective-permute-start.6 = (f32[32,128]{1,0:T(8,128)S(1)}, f32[32,128]{1,0:T(8,128)S(1)}, u32[]{:S(2)}, u32[]{:S(2)}) collective-permute-start(f32[32,128]{1,0:T(8,128)S(1)} %add.19), channel_id=1, source_target_pairs={{0,16},{4,20},{8,24},{12,28},{16,0},{20,4},{24,8},{28,12},{1,17},{... | collective-permute-start | bytes 49160 | tf_op jit(solution)/shard_map/ppermute | solution.py:686
  29.1 2.0 %collective-permute-done.6 = f32[32,128]{1,0:T(8,128)S(1)} collective-permute-done((f32[32,128]{1,0:T(8,128)S(1)}, f32[32,128]{1,0:T(8,128)S(1)}, u32[]{:S(2)}, u32[]{:S(2)}) %collective-permute-start.6) | collective-permute-done | bytes 16416 | tf_op jit(solution)/shard_map/ppermute | solution.py:686
  31.2 1.7 %collective-permute-start.9 = (f32[32,128]{1,0:T(8,128)S(1)}, f32[32,128]{1,0:T(8,128)S(1)}, u32[]{:S(2)}, u32[]{:S(2)}) collective-permute-start(f32[32,128]{1,0:T(8,128)S(1)} %add.20), channel_id=1, source_target_pairs={{0,3},{1,2},{2,1},{3,0},{4,7},{5,6},{6,5},{7,4},{8,11},{9,10},{10,... | collective-permute-start | bytes 49160 | tf_op jit(solution)/shard_map/ppermute | solution.py:686
  32.9 3.7 %collective-permute-start.8 = (f32[32,128]{1,0:T(8,128)S(1)}, f32[32,128]{1,0:T(8,128)S(1)}, u32[]{:S(2)}, u32[]{:S(2)}) collective-permute-start(f32[32,128]{1,0:T(8,128)S(1)} %add.20), channel_id=1, source_target_pairs={{0,2},{1,3},{2,0},{3,1},{4,6},{5,7},{6,4},{7,5},{8,10},{9,11},{10,... | collective-permute-start | bytes 49160 | tf_op jit(solution)/shard_map/ppermute | solution.py:686
  36.6 0.8 %collective-permute-start.7 = (f32[32,128]{1,0:T(8,128)S(1)}, f32[32,128]{1,0:T(8,128)S(1)}, u32[]{:S(2)}, u32[]{:S(2)}) collective-permute-start(f32[32,128]{1,0:T(8,128)S(1)} %add.20), channel_id=1, source_target_pairs={{0,1},{1,0},{2,3},{3,2},{4,5},{5,4},{6,7},{7,6},{8,9},{9,8},{10,11... | collective-permute-start | bytes 49160 | tf_op jit(solution)/shard_map/ppermute | solution.py:686
  37.4 0.9 %collective-permute-done.8 = f32[32,128]{1,0:T(8,128)S(1)} collective-permute-done((f32[32,128]{1,0:T(8,128)S(1)}, f32[32,128]{1,0:T(8,128)S(1)}, u32[]{:S(2)}, u32[]{:S(2)}) %collective-permute-start.8) | collective-permute-done | bytes 16416 | tf_op jit(solution)/shard_map/ppermute | solution.py:686
  38.3 2.0 %collective-permute-done.7 = f32[32,128]{1,0:T(8,128)S(1)} collective-permute-done((f32[32,128]{1,0:T(8,128)S(1)}, f32[32,128]{1,0:T(8,128)S(1)}, u32[]{:S(2)}, u32[]{:S(2)}) %collective-permute-start.7) | collective-permute-done | bytes 16416 | tf_op jit(solution)/shard_map/ppermute | solution.py:686
  40.4 1.5 %last_kernel.1 = (f32[9,128,256]{2,1,0:T(8,128)}, f32[2,6]{1,0:T(2,128)}, f32[128,256]{1,0:T(8,128)}) custom-call(f32[32,128]{1,0:T(8,128)S(1)} %add_add_fusion.message, f32[9,128,256]{2,1,0:T(8,128)S(1)} %copy-done, f32[3,9,160,128]{3,2,1,0:T(8,128)S(1)} %get-tuple-element.45.direction, f32[3,9,160,128]{3,2,1,0:T(8,128)S(1)} %get-tuple-element.46.part, ...), custom_call_target="tpu_custom_call" | custom-call | tf_op jit(solution)/shard_map/last_kernel/pallas_call | solution.py:717
  (24 shorter events, 0.1 us)
Async XLA Ops:
  0.6 2.7 %copy-start.3 = (f32[128,256]{1,0:T(8,128)S(1)}, f32[128,256]{1,0:T(8,128)}, u32[]{:S(2)}) copy-start(f32[128,256]{1,0:T(8,128)} %vert_in.3) | copy-start | bytes 393220
  0.6 2.7 %copy-start.2 = (f32[128,256]{1,0:T(8,128)S(1)}, f32[128,256]{1,0:T(8,128)}, u32[]{:S(2)}) copy-start(f32[128,256]{1,0:T(8,128)} %horiz_in.3) | copy-start | bytes 393220
  0.7 2.7 %copy-start = (f32[9,128,256]{2,1,0:T(8,128)S(1)}, f32[9,128,256]{2,1,0:T(8,128)}, u32[]{:S(2)}) copy-start(f32[9,128,256]{2,1,0:T(8,128)} %phi.7) | copy-start | bytes 3538948
  0.7 2.7 %copy-start.1 = (f32[9,128,256]{2,1,0:T(8,128)S(1)}, f32[9,128,256]{2,1,0:T(8,128)}, u32[]{:S(2)}) copy-start(f32[9,128,256]{2,1,0:T(8,128)} %forcing.3) | copy-start | bytes 3538948
  0.7 2.7 %copy-start.7 = (f32[6,2]{0,1:T(2,128)S(1)}, f32[6,2]{0,1:T(2,128)}, u32[]{:S(2)}) copy-start(f32[6,2]{0,1:T(2,128)} %param.17) | copy-start | bytes 148
  0.7 2.7 %copy-start.6 = (f32[6,6,2]{1,2,0:T(2,128)S(1)}, f32[6,6,2]{1,2,0:T(2,128)}, u32[]{:S(2)}) copy-start(f32[6,6,2]{1,2,0:T(2,128)} %param.16) | copy-start | bytes 868
  2.1 4.2 %collective-permute-start = (f32[10,8,256]{2,1,0:T(8,128)S(1)}, f32[10,8,256]{2,1,0:T(8,128)S(1)}, u32[]{:S(2)}, u32[]{:S(2)}) collective-permute-start(f32[10,8,256]{2,1,0:T(8,128)S(1)} %get-tuple-element.28), channel_id=1, source_target_pairs={{0,4},{4,0},{8,12},{12,8},{16,20},{20,16},{24,28},{28,24},{1,5},{5... | collective-permute-start | bytes 245768 | tf_op jit(solution)/shard_map/ppermute | solution.py:669
  2.6 3.7 %collective-permute-start.1 = (f32[10,8,256]{2,1,0:T(8,128)S(1)}, f32[10,8,256]{2,1,0:T(8,128)S(1)}, u32[]{:S(2)}, u32[]{:S(2)}) collective-permute-start(f32[10,8,256]{2,1,0:T(8,128)S(1)} %get-tuple-element.29), channel_id=1, source_target_pairs={{4,8},{12,16},{20,24},{8,4},{16,12},{24,20},{5,9},{13,17},{21,25},... | collective-permute-start | bytes 245768 | tf_op jit(solution)/shard_map/ppermute | solution.py:675
  6.2 3.7 %copy-start.4 = (f32[6,128,256]{2,1,0:T(8,128)S(1)}, f32[6,128,256]{2,1,0:T(8,128)}, u32[]{:S(2)}) copy-start(f32[6,128,256]{2,1,0:T(8,128)} %modes.1) | copy-start | bytes 2359300
  6.3 3.7 %copy-start.5 = (f32[9,9]{1,0:T(8,128)S(1)}, f32[9,9]{1,0:T(8,128)}, u32[]{:S(2)}) copy-start(f32[9,9]{1,0:T(8,128)} %mix.3) | copy-start | bytes 976
  6.3 3.7 %copy-start.8 = (s32[128,2]{0,1:T(2,128)S(1)}, s32[128,2]{0,1:T(2,128)}, u32[]{:S(2)}) copy-start(s32[128,2]{0,1:T(2,128)} %param.15) | copy-start | bytes 3076
  6.7 5.5 %collective-permute-start.2 = (f32[72,128]{1,0:T(8,128)S(1)}, f32[72,128]{1,0:T(8,128)S(1)}, u32[]{:S(2)}, u32[]{:S(2)}) collective-permute-start(f32[72,128]{1,0:T(8,128)S(1)} %get-tuple-element.39), channel_id=1, source_target_pairs={{0,1},{1,0},{2,3},{3,2},{4,5},{5,4},{6,7},{7,6},{8,9},{9,8},{10,11... | collective-permute-start | bytes 110600 | tf_op jit(solution)/shard_map/ppermute | solution.py:669
  9.3 2.9 %collective-permute-start.3 = (f32[72,128]{1,0:T(8,128)S(1)}, f32[72,128]{1,0:T(8,128)S(1)}, u32[]{:S(2)}, u32[]{:S(2)}) collective-permute-start(f32[72,128]{1,0:T(8,128)S(1)} %get-tuple-element.40), channel_id=1, source_target_pairs={{1,2},{2,1},{5,6},{6,5},{9,10},{10,9},{13,14},{14,13},{17,18},{18,... | collective-permute-start | bytes 110600 | tf_op jit(solution)/shard_map/ppermute | solution.py:675
  19.3 3.5 %collective-permute-start.4 = (f32[32,128]{1,0:T(8,128)S(1)}, f32[32,128]{1,0:T(8,128)S(1)}, u32[]{:S(2)}, u32[]{:S(2)}) collective-permute-start(f32[32,128]{1,0:T(8,128)S(1)} %get-tuple-element.44), channel_id=1, source_target_pairs={{0,4},{4,0},{8,12},{12,8},{16,20},{20,16},{24,28},{28,24},{1,5},{5... | collective-permute-start | bytes 49160 | tf_op jit(solution)/shard_map/ppermute | solution.py:686
  22.8 3.7 %collective-permute-start.5 = (f32[32,128]{1,0:T(8,128)S(1)}, f32[32,128]{1,0:T(8,128)S(1)}, u32[]{:S(2)}, u32[]{:S(2)}) collective-permute-start(f32[32,128]{1,0:T(8,128)S(1)} %add.18), channel_id=1, source_target_pairs={{0,8},{4,12},{8,0},{12,4},{16,24},{20,28},{24,16},{28,20},{1,9},{5... | collective-permute-start | bytes 49160 | tf_op jit(solution)/shard_map/ppermute | solution.py:686
  26.6 4.6 %collective-permute-start.6 = (f32[32,128]{1,0:T(8,128)S(1)}, f32[32,128]{1,0:T(8,128)S(1)}, u32[]{:S(2)}, u32[]{:S(2)}) collective-permute-start(f32[32,128]{1,0:T(8,128)S(1)} %add.19), channel_id=1, source_target_pairs={{0,16},{4,20},{8,24},{12,28},{16,0},{20,4},{24,8},{28,12},{1,17},{... | collective-permute-start | bytes 49160 | tf_op jit(solution)/shard_map/ppermute | solution.py:686
  31.2 6.2 %collective-permute-start.9 = (f32[32,128]{1,0:T(8,128)S(1)}, f32[32,128]{1,0:T(8,128)S(1)}, u32[]{:S(2)}, u32[]{:S(2)}) collective-permute-start(f32[32,128]{1,0:T(8,128)S(1)} %add.20), channel_id=1, source_target_pairs={{0,3},{1,2},{2,1},{3,0},{4,7},{5,6},{6,5},{7,4},{8,11},{9,10},{10,... | collective-permute-start | bytes 49160 | tf_op jit(solution)/shard_map/ppermute | solution.py:686
  32.9 5.4 %collective-permute-start.8 = (f32[32,128]{1,0:T(8,128)S(1)}, f32[32,128]{1,0:T(8,128)S(1)}, u32[]{:S(2)}, u32[]{:S(2)}) collective-permute-start(f32[32,128]{1,0:T(8,128)S(1)} %add.20), channel_id=1, source_target_pairs={{0,2},{1,3},{2,0},{3,1},{4,6},{5,7},{6,4},{7,5},{8,10},{9,11},{10,... | collective-permute-start | bytes 49160 | tf_op jit(solution)/shard_map/ppermute | solution.py:686
  36.6 3.7 %collective-permute-start.7 = (f32[32,128]{1,0:T(8,128)S(1)}, f32[32,128]{1,0:T(8,128)S(1)}, u32[]{:S(2)}, u32[]{:S(2)}) collective-permute-start(f32[32,128]{1,0:T(8,128)S(1)} %add.20), channel_id=1, source_target_pairs={{0,1},{1,0},{2,3},{3,2},{4,5},{5,4},{6,7},{7,6},{8,9},{9,8},{10,11... | collective-permute-start | bytes 49160 | tf_op jit(solution)/shard_map/ppermute | solution.py:686

commit v7 on v6

--- a/solution.py
+++ b/solution.py
@@ -158,7 +158,7 @@
                 res[t, l, here, :] = forcing[l, here, lanes] - value
         return carry
 
-    lax.fori_loop(0, rows // SUB, residual, 0, unroll=2)
+    lax.fori_loop(0, rows // SUB, residual, 0, unroll=8)
 
     def body(i, carry):
         here = tile_at(i)
@@ -452,12 +452,8 @@
                 for t in range(blocks):
                     dir_s[t, l, there, :] = early[t, l, there, :] + changes[t]
 
-    def first_body(i, carry):
-        first([8 * i + n + 1 for n in range(8)], True)
-        return carry
-
     first([0, row_tiles + 1], False)
-    lax.fori_loop(0, row_tiles // 8, first_body, 0, unroll=1)
+    first(range(1, row_tiles + 1), True)
 
     def coefs_at(t, row):
         here = pl.ds(row, SUB)
@@ -491,7 +487,7 @@
     for i in range((row_tiles + 2) // 9 * 9, row_tiles + 2):
         second([i])
 
-    def third(i, totals):
+    def third(totals):
         totals = list(totals)
         waiting = None
 
@@ -502,8 +498,8 @@
             for n, product in enumerate(products):
                 totals[n] = totals[n] + product
 
-        for n in range(16):
-            row = pl.multiple_of((16 * i + n) * SUB + base, SUB)
+        for i in range(row_tiles):
+            row = i * SUB + base
             here = pl.ds(row, SUB)
             for t in range(blocks):
                 values = []
@@ -518,7 +514,7 @@
         return tuple(totals)
 
     zero = jnp.zeros((SUB, LANES), F32)
-    totals = lax.fori_loop(0, row_tiles // 16, third, (zero,) * 5, unroll=1)
+    totals = third((zero,) * 5)
 
     width = message.shape[1]
     surface_rows = pl.ds(base, rows)

time: 42 us -> 41.6 us (level)
  Pallas kernels: 15.4 us -> 14.7 us
  starting transfers between devices: 17.5 us -> 18.2 us
  waiting for transfers between devices: 7.98 us -> 7.53 us
    ppermute x6, starting transfers between devices: 13.1 us -> 13.8 us  [sum_over(): total = total + lax.ppermute(value, axis, pairs)]
    pallas_call x6, Pallas kernels: 15.4 us -> 14.7 us  [call(): pl.pallas_call(kernel, out_shape=tuple((jax.ShapeDtypeStruct(shape, F32)...]
    ppermute x6, waiting for transfers between devices: 7.97 us -> 7.52 us  [sum_over(): total = total + lax.ppermute(value, axis, pairs)]
  transfers between devices with their start and end apart: 10 -> 10, of which waited for: 5 -> 5; matrix products, arithmetic and copies ran while one was open for 0% -> 0% of each run, Pallas kernels for 12% -> 11%
where the time goes in v7:
time: 41.6 us; the launch traced here: 41.4 us
  starting transfers between devices  18.2 us (44%)
  Pallas kernels  14.7 us (35%)
  waiting for transfers between devices  7.53 us (18%)
  between operations  0.86 us (2%)
    pallas_call x6, Pallas kernels, call(): pl.pallas_call(kernel, out_shape=tuple((jax.ShapeDtypeStruct(shape, F32)...  14.7 us
    ppermute x6, starting transfers between devices, sum_over(): total = total + lax.ppermute(value, axis, pairs)  13.8 us
    ppermute x6, waiting for transfers between devices, sum_over(): total = total + lax.ppermute(value, axis, pairs)  7.52 us
    ppermute x2, starting transfers between devices, swap_near(): return lax.ppermute(value, axis, [(i, i ^ 1) for i in range(size)])  3.09 us
    ppermute x2, starting transfers between devices, swap_far(): return lax.ppermute(value, axis, pairs + [(j, i) for i, j in pairs])  1.31 us
  transfers between devices with their start and end apart: 10, of which 5 were waited for; matrix products, arithmetic and copies ran while one was open for 0% of the time, Pallas kernels for 11%

profile of v7, /device:TPU:0, one launch (start us, length us, event | category | flops | bytes accessed | tf_op | source)
XLA Modules:
  0.0 41.4 jit_solution(8558814084627994126)
XLA Ops:
  0.7 1.4 %strip_kernel.1 = (f32[10,8,256]{2,1,0:T(8,128)S(1)}, f32[10,8,256]{2,1,0:T(8,128)S(1)}) custom-call(f32[9,128,256]{2,1,0:T(8,128)} %phi.7, f32[9,128,256]{2,1,0:T(8,128)} %forcing.3, f32[128,256]{1,0:T(8,128)} %horiz_in.3, f32[128,256]{1,0:T(8,128)} %vert_in.3), custom_call_target="tpu_custom_call" | custom-call | tf_op jit(solution)/shard_map/strip_kernel/pallas_call | solution.py:713
  2.1 0.5 %collective-permute-start = (f32[10,8,256]{2,1,0:T(8,128)S(1)}, f32[10,8,256]{2,1,0:T(8,128)S(1)}, u32[]{:S(2)}, u32[]{:S(2)}) collective-permute-start(f32[10,8,256]{2,1,0:T(8,128)S(1)} %get-tuple-element.28), channel_id=1, source_target_pairs={{0,4},{4,0},{8,12},{12,8},{16,20},{20,16},{24,28},{28,24},{1,5},{5... | collective-permute-start | bytes 245768 | tf_op jit(solution)/shard_map/ppermute | solution.py:665
  2.6 0.7 %collective-permute-start.1 = (f32[10,8,256]{2,1,0:T(8,128)S(1)}, f32[10,8,256]{2,1,0:T(8,128)S(1)}, u32[]{:S(2)}, u32[]{:S(2)}) collective-permute-start(f32[10,8,256]{2,1,0:T(8,128)S(1)} %get-tuple-element.29), channel_id=1, source_target_pairs={{4,8},{12,16},{20,24},{8,4},{16,12},{24,20},{5,9},{13,17},{21,25},... | collective-permute-start | bytes 245768 | tf_op jit(solution)/shard_map/ppermute | solution.py:671
  3.4 2.4 %inner_kernel.1 = (f32[2,9,128,128]{3,2,1,0:T(8,128)S(1)}, f32[144,128]{1,0:T(8,128)S(1)}, f32[24,128]{1,0:T(8,128)S(1)}) custom-call(f32[9,128,256]{2,1,0:T(8,128)S(1)} %copy-done, f32[9,128,256]{2,1,0:T(8,128)S(1)} %copy-done.1, f32[128,256]{1,0:T(8,128)S(1)} %copy-done.2, f32[128,256]{1,0:T(8,128)S(1)} %copy-done.3, f32[6,2,6]{2,1,0:T(2,128)S(1)} %bitcast.4, ...), custom_call_target="tpu_custom_call" | custom-call | tf_op jit(solution)/shard_map/inner_kernel/pallas_call | solution.py:713
  5.8 0.0 copy-start.4
  5.8 0.0 copy-start.5
  5.8 0.0 copy-start.8
  5.8 0.4 edge_kernel.1
  6.2 2.6 %collective-permute-start.2 = (f32[72,128]{1,0:T(8,128)S(1)}, f32[72,128]{1,0:T(8,128)S(1)}, u32[]{:S(2)}, u32[]{:S(2)}) collective-permute-start(f32[72,128]{1,0:T(8,128)S(1)} %get-tuple-element.39), channel_id=1, source_target_pairs={{0,1},{1,0},{2,3},{3,2},{4,5},{5,4},{6,7},{7,6},{8,9},{9,8},{10,11... | collective-permute-start | bytes 110600 | tf_op jit(solution)/shard_map/ppermute | solution.py:665
  8.8 0.7 %collective-permute-start.3 = (f32[72,128]{1,0:T(8,128)S(1)}, f32[72,128]{1,0:T(8,128)S(1)}, u32[]{:S(2)}, u32[]{:S(2)}) collective-permute-start(f32[72,128]{1,0:T(8,128)S(1)} %get-tuple-element.40), channel_id=1, source_target_pairs={{1,2},{2,1},{5,6},{6,5},{9,10},{10,9},{13,14},{14,13},{17,18},{18,... | collective-permute-start | bytes 110600 | tf_op jit(solution)/shard_map/ppermute | solution.py:671
  9.5 2.2 %ahead_kernel.1 = (f32[2,6,128,128]{3,2,1,0:T(8,128)S(1)}, f32[2,128,128]{2,1,0:T(8,128)S(1)}, f32[2,128,128]{2,1,0:T(8,128)S(1)}, f32[2,9,160,128]{3,2,1,0:T(8,...) custom-call(f32[2,9,128,128]{3,2,1,0:T(8,128)S(1)} %get-tuple-elemen, ...), custom_call_target="tpu_custom_call" | custom-call | tf_op jit(solution)/shard_map/ahead_kernel/pallas_call | solution.py:713
  11.7 6.9 %main_kernel.1 = (f32[3,9,160,128]{3,2,1,0:T(8,128)S(1)}, f32[3,9,160,128]{3,2,1,0:T(8,128)S(1)}, f32[32,128]{1,0:T(8,128)S(1)}) custom-call(f32[2,9,160,128]{3,2,1,0:T(8,128)S(1)} %get-tuple-element.33.early, f32[2,9,160,128]{3,2,1,0:T(8,128)S(1)} %get-tuple-element.34.res_own, f32[2,160,128]{2,1,0:T(8,128)S(1)} %get-tuple-element.35.horiz, ...), custom_call_target="tpu_custom_call" | custom-call | tf_op jit(solution)/shard_map/main_kernel/pallas_call | solution.py:713
  18.6 2.8 %collective-permute-start.4 = (f32[32,128]{1,0:T(8,128)S(1)}, f32[32,128]{1,0:T(8,128)S(1)}, u32[]{:S(2)}, u32[]{:S(2)}) collective-permute-start(f32[32,128]{1,0:T(8,128)S(1)} %get-tuple-element.44), channel_id=1, source_target_pairs={{0,4},{4,0},{8,12},{12,8},{16,20},{20,16},{24,28},{28,24},{1,5},{5... | collective-permute-start | bytes 49160 | tf_op jit(solution)/shard_map/ppermute | solution.py:682
  21.4 0.8 %collective-permute-done.4 = f32[32,128]{1,0:T(8,128)S(1)} collective-permute-done((f32[32,128]{1,0:T(8,128)S(1)}, f32[32,128]{1,0:T(8,128)S(1)}, u32[]{:S(2)}, u32[]{:S(2)}) %collective-permute-start.4) | collective-permute-done | bytes 16416 | tf_op jit(solution)/shard_map/ppermute | solution.py:682
  22.2 1.7 %collective-permute-start.5 = (f32[32,128]{1,0:T(8,128)S(1)}, f32[32,128]{1,0:T(8,128)S(1)}, u32[]{:S(2)}, u32[]{:S(2)}) collective-permute-start(f32[32,128]{1,0:T(8,128)S(1)} %add.18), channel_id=1, source_target_pairs={{0,8},{4,12},{8,0},{12,4},{16,24},{20,28},{24,16},{28,20},{1,9},{5... | collective-permute-start | bytes 49160 | tf_op jit(solution)/shard_map/ppermute | solution.py:682
  23.9 2.0 %collective-permute-done.5 = f32[32,128]{1,0:T(8,128)S(1)} collective-permute-done((f32[32,128]{1,0:T(8,128)S(1)}, f32[32,128]{1,0:T(8,128)S(1)}, u32[]{:S(2)}, u32[]{:S(2)}) %collective-permute-start.5) | collective-permute-done | bytes 16416 | tf_op jit(solution)/shard_map/ppermute | solution.py:682
  26.0 2.7 %collective-permute-start.6 = (f32[32,128]{1,0:T(8,128)S(1)}, f32[32,128]{1,0:T(8,128)S(1)}, u32[]{:S(2)}, u32[]{:S(2)}) collective-permute-start(f32[32,128]{1,0:T(8,128)S(1)} %add.19), channel_id=1, source_target_pairs={{0,16},{4,20},{8,24},{12,28},{16,0},{20,4},{24,8},{28,12},{1,17},{... | collective-permute-start | bytes 49160 | tf_op jit(solution)/shard_map/ppermute | solution.py:682
  28.7 1.9 %collective-permute-done.6 = f32[32,128]{1,0:T(8,128)S(1)} collective-permute-done((f32[32,128]{1,0:T(8,128)S(1)}, f32[32,128]{1,0:T(8,128)S(1)}, u32[]{:S(2)}, u32[]{:S(2)}) %collective-permute-start.6) | collective-permute-done | bytes 16416 | tf_op jit(solution)/shard_map/ppermute | solution.py:682
  30.6 1.8 %collective-permute-start.9 = (f32[32,128]{1,0:T(8,128)S(1)}, f32[32,128]{1,0:T(8,128)S(1)}, u32[]{:S(2)}, u32[]{:S(2)}) collective-permute-start(f32[32,128]{1,0:T(8,128)S(1)} %add.20), channel_id=1, source_target_pairs={{0,3},{1,2},{2,1},{3,0},{4,7},{5,6},{6,5},{7,4},{8,11},{9,10},{10,... | collective-permute-start | bytes 49160 | tf_op jit(solution)/shard_map/ppermute | solution.py:682
  32.4 3.8 %collective-permute-start.8 = (f32[32,128]{1,0:T(8,128)S(1)}, f32[32,128]{1,0:T(8,128)S(1)}, u32[]{:S(2)}, u32[]{:S(2)}) collective-permute-start(f32[32,128]{1,0:T(8,128)S(1)} %add.20), channel_id=1, source_target_pairs={{0,2},{1,3},{2,0},{3,1},{4,6},{5,7},{6,4},{7,5},{8,10},{9,11},{10,... | collective-permute-start | bytes 49160 | tf_op jit(solution)/shard_map/ppermute | solution.py:682
  36.2 1.0 %collective-permute-start.7 = (f32[32,128]{1,0:T(8,128)S(1)}, f32[32,128]{1,0:T(8,128)S(1)}, u32[]{:S(2)}, u32[]{:S(2)}) collective-permute-start(f32[32,128]{1,0:T(8,128)S(1)} %add.20), channel_id=1, source_target_pairs={{0,1},{1,0},{2,3},{3,2},{4,5},{5,4},{6,7},{7,6},{8,9},{9,8},{10,11... | collective-permute-start | bytes 49160 | tf_op jit(solution)/shard_map/ppermute | solution.py:682
  37.2 0.7 %collective-permute-done.8 = f32[32,128]{1,0:T(8,128)S(1)} collective-permute-done((f32[32,128]{1,0:T(8,128)S(1)}, f32[32,128]{1,0:T(8,128)S(1)}, u32[]{:S(2)}, u32[]{:S(2)}) %collective-permute-start.8) | collective-permute-done | bytes 16416 | tf_op jit(solution)/shard_map/ppermute | solution.py:682
  37.9 2.0 %collective-permute-done.7 = f32[32,128]{1,0:T(8,128)S(1)} collective-permute-done((f32[32,128]{1,0:T(8,128)S(1)}, f32[32,128]{1,0:T(8,128)S(1)}, u32[]{:S(2)}, u32[]{:S(2)}) %collective-permute-start.7) | collective-permute-done | bytes 16416 | tf_op jit(solution)/shard_map/ppermute | solution.py:682
  40.0 1.5 %last_kernel.1 = (f32[9,128,256]{2,1,0:T(8,128)}, f32[2,6]{1,0:T(2,128)}, f32[128,256]{1,0:T(8,128)}) custom-call(f32[32,128]{1,0:T(8,128)S(1)} %add_add_fusion.message, f32[9,128,256]{2,1,0:T(8,128)S(1)} %copy-done, f32[3,9,160,128]{3,2,1,0:T(8,128)S(1)} %get-tuple-element.45.direction, f32[3,9,160,128]{3,2,1,0:T(8,128)S(1)} %get-tuple-element.46.part, ...), custom_call_target="tpu_custom_call" | custom-call | tf_op jit(solution)/shard_map/last_kernel/pallas_call | solution.py:713
  (24 shorter events, 0.1 us)
Async XLA Ops:
  0.6 2.7 %copy-start.3 = (f32[128,256]{1,0:T(8,128)S(1)}, f32[128,256]{1,0:T(8,128)}, u32[]{:S(2)}) copy-start(f32[128,256]{1,0:T(8,128)} %vert_in.3) | copy-start | bytes 393220
  0.6 2.7 %copy-start.2 = (f32[128,256]{1,0:T(8,128)S(1)}, f32[128,256]{1,0:T(8,128)}, u32[]{:S(2)}) copy-start(f32[128,256]{1,0:T(8,128)} %horiz_in.3) | copy-start | bytes 393220
  0.7 2.7 %copy-start = (f32[9,128,256]{2,1,0:T(8,128)S(1)}, f32[9,128,256]{2,1,0:T(8,128)}, u32[]{:S(2)}) copy-start(f32[9,128,256]{2,1,0:T(8,128)} %phi.7) | copy-start | bytes 3538948
  0.7 2.7 %copy-start.1 = (f32[9,128,256]{2,1,0:T(8,128)S(1)}, f32[9,128,256]{2,1,0:T(8,128)}, u32[]{:S(2)}) copy-start(f32[9,128,256]{2,1,0:T(8,128)} %forcing.3) | copy-start | bytes 3538948
  0.7 2.7 %copy-start.7 = (f32[6,2]{0,1:T(2,128)S(1)}, f32[6,2]{0,1:T(2,128)}, u32[]{:S(2)}) copy-start(f32[6,2]{0,1:T(2,128)} %param.17) | copy-start | bytes 148
  0.7 2.7 %copy-start.6 = (f32[6,6,2]{1,2,0:T(2,128)S(1)}, f32[6,6,2]{1,2,0:T(2,128)}, u32[]{:S(2)}) copy-start(f32[6,6,2]{1,2,0:T(2,128)} %param.16) | copy-start | bytes 868
  2.1 3.7 %collective-permute-start = (f32[10,8,256]{2,1,0:T(8,128)S(1)}, f32[10,8,256]{2,1,0:T(8,128)S(1)}, u32[]{:S(2)}, u32[]{:S(2)}) collective-permute-start(f32[10,8,256]{2,1,0:T(8,128)S(1)} %get-tuple-element.28), channel_id=1, source_target_pairs={{0,4},{4,0},{8,12},{12,8},{16,20},{20,16},{24,28},{28,24},{1,5},{5... | collective-permute-start | bytes 245768 | tf_op jit(solution)/shard_map/ppermute | solution.py:665
  2.6 3.2 %collective-permute-start.1 = (f32[10,8,256]{2,1,0:T(8,128)S(1)}, f32[10,8,256]{2,1,0:T(8,128)S(1)}, u32[]{:S(2)}, u32[]{:S(2)}) collective-permute-start(f32[10,8,256]{2,1,0:T(8,128)S(1)} %get-tuple-element.29), channel_id=1, source_target_pairs={{4,8},{12,16},{20,24},{8,4},{16,12},{24,20},{5,9},{13,17},{21,25},... | collective-permute-start | bytes 245768 | tf_op jit(solution)/shard_map/ppermute | solution.py:671
  5.8 3.7 %copy-start.4 = (f32[6,128,256]{2,1,0:T(8,128)S(1)}, f32[6,128,256]{2,1,0:T(8,128)}, u32[]{:S(2)}) copy-start(f32[6,128,256]{2,1,0:T(8,128)} %modes.1) | copy-start | bytes 2359300
  5.8 3.7 %copy-start.5 = (f32[9,9]{1,0:T(8,128)S(1)}, f32[9,9]{1,0:T(8,128)}, u32[]{:S(2)}) copy-start(f32[9,9]{1,0:T(8,128)} %mix.3) | copy-start | bytes 976
  5.8 3.7 %copy-start.8 = (s32[128,2]{0,1:T(2,128)S(1)}, s32[128,2]{0,1:T(2,128)}, u32[]{:S(2)}) copy-start(s32[128,2]{0,1:T(2,128)} %param.15) | copy-start | bytes 3076
  6.2 5.5 %collective-permute-start.2 = (f32[72,128]{1,0:T(8,128)S(1)}, f32[72,128]{1,0:T(8,128)S(1)}, u32[]{:S(2)}, u32[]{:S(2)}) collective-permute-start(f32[72,128]{1,0:T(8,128)S(1)} %get-tuple-element.39), channel_id=1, source_target_pairs={{0,1},{1,0},{2,3},{3,2},{4,5},{5,4},{6,7},{7,6},{8,9},{9,8},{10,11... | collective-permute-start | bytes 110600 | tf_op jit(solution)/shard_map/ppermute | solution.py:665
  8.8 2.9 %collective-permute-start.3 = (f32[72,128]{1,0:T(8,128)S(1)}, f32[72,128]{1,0:T(8,128)S(1)}, u32[]{:S(2)}, u32[]{:S(2)}) collective-permute-start(f32[72,128]{1,0:T(8,128)S(1)} %get-tuple-element.40), channel_id=1, source_target_pairs={{1,2},{2,1},{5,6},{6,5},{9,10},{10,9},{13,14},{14,13},{17,18},{18,... | collective-permute-start | bytes 110600 | tf_op jit(solution)/shard_map/ppermute | solution.py:671
  18.6 3.6 %collective-permute-start.4 = (f32[32,128]{1,0:T(8,128)S(1)}, f32[32,128]{1,0:T(8,128)S(1)}, u32[]{:S(2)}, u32[]{:S(2)}) collective-permute-start(f32[32,128]{1,0:T(8,128)S(1)} %get-tuple-element.44), channel_id=1, source_target_pairs={{0,4},{4,0},{8,12},{12,8},{16,20},{20,16},{24,28},{28,24},{1,5},{5... | collective-permute-start | bytes 49160 | tf_op jit(solution)/shard_map/ppermute | solution.py:682
  22.2 3.7 %collective-permute-start.5 = (f32[32,128]{1,0:T(8,128)S(1)}, f32[32,128]{1,0:T(8,128)S(1)}, u32[]{:S(2)}, u32[]{:S(2)}) collective-permute-start(f32[32,128]{1,0:T(8,128)S(1)} %add.18), channel_id=1, source_target_pairs={{0,8},{4,12},{8,0},{12,4},{16,24},{20,28},{24,16},{28,20},{1,9},{5... | collective-permute-start | bytes 49160 | tf_op jit(solution)/shard_map/ppermute | solution.py:682
  26.0 4.6 %collective-permute-start.6 = (f32[32,128]{1,0:T(8,128)S(1)}, f32[32,128]{1,0:T(8,128)S(1)}, u32[]{:S(2)}, u32[]{:S(2)}) collective-permute-start(f32[32,128]{1,0:T(8,128)S(1)} %add.19), channel_id=1, source_target_pairs={{0,16},{4,20},{8,24},{12,28},{16,0},{20,4},{24,8},{28,12},{1,17},{... | collective-permute-start | bytes 49160 | tf_op jit(solution)/shard_map/ppermute | solution.py:682
  30.6 6.6 %collective-permute-start.9 = (f32[32,128]{1,0:T(8,128)S(1)}, f32[32,128]{1,0:T(8,128)S(1)}, u32[]{:S(2)}, u32[]{:S(2)}) collective-permute-start(f32[32,128]{1,0:T(8,128)S(1)} %add.20), channel_id=1, source_target_pairs={{0,3},{1,2},{2,1},{3,0},{4,7},{5,6},{6,5},{7,4},{8,11},{9,10},{10,... | collective-permute-start | bytes 49160 | tf_op jit(solution)/shard_map/ppermute | solution.py:682
  32.4 5.5 %collective-permute-start.8 = (f32[32,128]{1,0:T(8,128)S(1)}, f32[32,128]{1,0:T(8,128)S(1)}, u32[]{:S(2)}, u32[]{:S(2)}) collective-permute-start(f32[32,128]{1,0:T(8,128)S(1)} %add.20), channel_id=1, source_target_pairs={{0,2},{1,3},{2,0},{3,1},{4,6},{5,7},{6,4},{7,5},{8,10},{9,11},{10,... | collective-permute-start | bytes 49160 | tf_op jit(solution)/shard_map/ppermute | solution.py:682
  36.2 3.7 %collective-permute-start.7 = (f32[32,128]{1,0:T(8,128)S(1)}, f32[32,128]{1,0:T(8,128)S(1)}, u32[]{:S(2)}, u32[]{:S(2)}) collective-permute-start(f32[32,128]{1,0:T(8,128)S(1)} %add.20), channel_id=1, source_target_pairs={{0,1},{1,0},{2,3},{3,2},{4,5},{5,4},{6,7},{7,6},{8,9},{9,8},{10,11... | collective-permute-start | bytes 49160 | tf_op jit(solution)/shard_map/ppermute | solution.py:682

commit v8 on v7

--- a/solution.py
+++ b/solution.py
@@ -461,11 +461,11 @@
             return horiz_s[here, :], vert_s[here, :]
         return horiz[t, here, :], vert[t, here, :]
 
-    def second(group):
+    def second(group, wanted):
         rows_of = [pl.multiple_of(i * SUB + SUB, SUB) for i in group]
         waiting = None
         for row in rows_of:
-            for t in everything:
+            for t in wanted:
                 here = pl.ds(row, SUB)
                 factor = scale_s[here, :] if t == side else scale[t, here, :]
                 weighted = []
@@ -479,13 +479,15 @@
         for l in range(levels):
             part_s[waiting[0], l, waiting[1], :] = mix_level(mix, waiting[2], l)
 
+    second([0, row_tiles + 1], range(blocks))
+
     def second_body(i, carry):
-        second([9 * i + n for n in range(9)])
+        second([8 * i + n + 1 for n in range(8)], everything)
         return carry
 
-    lax.fori_loop(0, (row_tiles + 2) // 9, second_body, 0, unroll=1)
-    for i in range((row_tiles + 2) // 9 * 9, row_tiles + 2):
-        second([i])
+    lax.fori_loop(0, row_tiles // 8, second_body, 0)
+    for i in range(row_tiles // 8 * 8 + 1, row_tiles + 1):
+        second([i], everything)
 
     def third(totals):
         totals = list(totals)

time: 41.6 us -> 41.5 us (level)
  no operation moved by 1% of the time
where the time goes in v8:
time: 41.5 us; the launch traced here: 41.3 us
  starting transfers between devices  18.2 us (44%)
  Pallas kernels  14.6 us (35%)
  waiting for transfers between devices  7.53 us (18%)
  between operations  0.86 us (2%)
    pallas_call x6, Pallas kernels, call(): pl.pallas_call(kernel, out_shape=tuple((jax.ShapeDtypeStruct(shape, F32)...  14.6 us
    ppermute x6, starting transfers between devices, sum_over(): total = total + lax.ppermute(value, axis, pairs)  13.8 us
    ppermute x6, waiting for transfers between devices, sum_over(): total = total + lax.ppermute(value, axis, pairs)  7.52 us
    ppermute x2, starting transfers between devices, swap_near(): return lax.ppermute(value, axis, [(i, i ^ 1) for i in range(size)])  3.09 us
    ppermute x2, starting transfers between devices, swap_far(): return lax.ppermute(value, axis, pairs + [(j, i) for i, j in pairs])  1.31 us
  transfers between devices with their start and end apart: 10, of which 5 were waited for; matrix products, arithmetic and copies ran while one was open for 0% of the time, Pallas kernels for 11%

profile of v8, /device:TPU:0, one launch (start us, length us, event | category | flops | bytes accessed | tf_op | source)
XLA Modules:
  0.0 41.3 jit_solution(12783256914564254937)
XLA Ops:
  0.7 1.4 %strip_kernel.1 = (f32[10,8,256]{2,1,0:T(8,128)S(1)}, f32[10,8,256]{2,1,0:T(8,128)S(1)}) custom-call(f32[9,128,256]{2,1,0:T(8,128)} %phi.7, f32[9,128,256]{2,1,0:T(8,128)} %forcing.3, f32[128,256]{1,0:T(8,128)} %horiz_in.3, f32[128,256]{1,0:T(8,128)} %vert_in.3), custom_call_target="tpu_custom_call" | custom-call | tf_op jit(solution)/shard_map/strip_kernel/pallas_call | solution.py:715
  2.1 0.5 %collective-permute-start = (f32[10,8,256]{2,1,0:T(8,128)S(1)}, f32[10,8,256]{2,1,0:T(8,128)S(1)}, u32[]{:S(2)}, u32[]{:S(2)}) collective-permute-start(f32[10,8,256]{2,1,0:T(8,128)S(1)} %get-tuple-element.28), channel_id=1, source_target_pairs={{0,4},{4,0},{8,12},{12,8},{16,20},{20,16},{24,28},{28,24},{1,5},{5... | collective-permute-start | bytes 245768 | tf_op jit(solution)/shard_map/ppermute | solution.py:667
  2.6 0.7 %collective-permute-start.1 = (f32[10,8,256]{2,1,0:T(8,128)S(1)}, f32[10,8,256]{2,1,0:T(8,128)S(1)}, u32[]{:S(2)}, u32[]{:S(2)}) collective-permute-start(f32[10,8,256]{2,1,0:T(8,128)S(1)} %get-tuple-element.29), channel_id=1, source_target_pairs={{4,8},{12,16},{20,24},{8,4},{16,12},{24,20},{5,9},{13,17},{21,25},... | collective-permute-start | bytes 245768 | tf_op jit(solution)/shard_map/ppermute | solution.py:673
  3.4 2.4 %inner_kernel.1 = (f32[2,9,128,128]{3,2,1,0:T(8,128)S(1)}, f32[144,128]{1,0:T(8,128)S(1)}, f32[24,128]{1,0:T(8,128)S(1)}) custom-call(f32[9,128,256]{2,1,0:T(8,128)S(1)} %copy-done, f32[9,128,256]{2,1,0:T(8,128)S(1)} %copy-done.1, f32[128,256]{1,0:T(8,128)S(1)} %copy-done.2, f32[128,256]{1,0:T(8,128)S(1)} %copy-done.3, f32[6,2,6]{2,1,0:T(2,128)S(1)} %bitcast.4, ...), custom_call_target="tpu_custom_call" | custom-call | tf_op jit(solution)/shard_map/inner_kernel/pallas_call | solution.py:715
  5.8 0.0 copy-start.4
  5.8 0.0 copy-start.5
  5.8 0.0 copy-start.8
  5.8 0.4 edge_kernel.1
  6.2 2.6 %collective-permute-start.2 = (f32[72,128]{1,0:T(8,128)S(1)}, f32[72,128]{1,0:T(8,128)S(1)}, u32[]{:S(2)}, u32[]{:S(2)}) collective-permute-start(f32[72,128]{1,0:T(8,128)S(1)} %get-tuple-element.39), channel_id=1, source_target_pairs={{0,1},{1,0},{2,3},{3,2},{4,5},{5,4},{6,7},{7,6},{8,9},{9,8},{10,11... | collective-permute-start | bytes 110600 | tf_op jit(solution)/shard_map/ppermute | solution.py:667
  8.8 0.7 %collective-permute-start.3 = (f32[72,128]{1,0:T(8,128)S(1)}, f32[72,128]{1,0:T(8,128)S(1)}, u32[]{:S(2)}, u32[]{:S(2)}) collective-permute-start(f32[72,128]{1,0:T(8,128)S(1)} %get-tuple-element.40), channel_id=1, source_target_pairs={{1,2},{2,1},{5,6},{6,5},{9,10},{10,9},{13,14},{14,13},{17,18},{18,... | collective-permute-start | bytes 110600 | tf_op jit(solution)/shard_map/ppermute | solution.py:673
  9.5 2.2 %ahead_kernel.1 = (f32[2,6,128,128]{3,2,1,0:T(8,128)S(1)}, f32[2,128,128]{2,1,0:T(8,128)S(1)}, f32[2,128,128]{2,1,0:T(8,128)S(1)}, f32[2,9,160,128]{3,2,1,0:T(8,...) custom-call(f32[2,9,128,128]{3,2,1,0:T(8,128)S(1)} %get-tuple-elemen, ...), custom_call_target="tpu_custom_call" | custom-call | tf_op jit(solution)/shard_map/ahead_kernel/pallas_call | solution.py:715
  11.7 6.8 %main_kernel.1 = (f32[3,9,160,128]{3,2,1,0:T(8,128)S(1)}, f32[3,9,160,128]{3,2,1,0:T(8,128)S(1)}, f32[32,128]{1,0:T(8,128)S(1)}) custom-call(f32[2,9,160,128]{3,2,1,0:T(8,128)S(1)} %get-tuple-element.33.early, f32[2,9,160,128]{3,2,1,0:T(8,128)S(1)} %get-tuple-element.34.res_own, f32[2,160,128]{2,1,0:T(8,128)S(1)} %get-tuple-element.35.horiz, ...), custom_call_target="tpu_custom_call" | custom-call | tf_op jit(solution)/shard_map/main_kernel/pallas_call | solution.py:715
  18.5 2.8 %collective-permute-start.4 = (f32[32,128]{1,0:T(8,128)S(1)}, f32[32,128]{1,0:T(8,128)S(1)}, u32[]{:S(2)}, u32[]{:S(2)}) collective-permute-start(f32[32,128]{1,0:T(8,128)S(1)} %get-tuple-element.44), channel_id=1, source_target_pairs={{0,4},{4,0},{8,12},{12,8},{16,20},{20,16},{24,28},{28,24},{1,5},{5... | collective-permute-start | bytes 49160 | tf_op jit(solution)/shard_map/ppermute | solution.py:684
  21.3 0.8 %collective-permute-done.4 = f32[32,128]{1,0:T(8,128)S(1)} collective-permute-done((f32[32,128]{1,0:T(8,128)S(1)}, f32[32,128]{1,0:T(8,128)S(1)}, u32[]{:S(2)}, u32[]{:S(2)}) %collective-permute-start.4) | collective-permute-done | bytes 16416 | tf_op jit(solution)/shard_map/ppermute | solution.py:684
  22.1 1.7 %collective-permute-start.5 = (f32[32,128]{1,0:T(8,128)S(1)}, f32[32,128]{1,0:T(8,128)S(1)}, u32[]{:S(2)}, u32[]{:S(2)}) collective-permute-start(f32[32,128]{1,0:T(8,128)S(1)} %add.18), channel_id=1, source_target_pairs={{0,8},{4,12},{8,0},{12,4},{16,24},{20,28},{24,16},{28,20},{1,9},{5... | collective-permute-start | bytes 49160 | tf_op jit(solution)/shard_map/ppermute | solution.py:684
  23.8 2.0 %collective-permute-done.5 = f32[32,128]{1,0:T(8,128)S(1)} collective-permute-done((f32[32,128]{1,0:T(8,128)S(1)}, f32[32,128]{1,0:T(8,128)S(1)}, u32[]{:S(2)}, u32[]{:S(2)}) %collective-permute-start.5) | collective-permute-done | bytes 16416 | tf_op jit(solution)/shard_map/ppermute | solution.py:684
  25.9 2.7 %collective-permute-start.6 = (f32[32,128]{1,0:T(8,128)S(1)}, f32[32,128]{1,0:T(8,128)S(1)}, u32[]{:S(2)}, u32[]{:S(2)}) collective-permute-start(f32[32,128]{1,0:T(8,128)S(1)} %add.19), channel_id=1, source_target_pairs={{0,16},{4,20},{8,24},{12,28},{16,0},{20,4},{24,8},{28,12},{1,17},{... | collective-permute-start | bytes 49160 | tf_op jit(solution)/shard_map/ppermute | solution.py:684
  28.6 1.9 %collective-permute-done.6 = f32[32,128]{1,0:T(8,128)S(1)} collective-permute-done((f32[32,128]{1,0:T(8,128)S(1)}, f32[32,128]{1,0:T(8,128)S(1)}, u32[]{:S(2)}, u32[]{:S(2)}) %collective-permute-start.6) | collective-permute-done | bytes 16416 | tf_op jit(solution)/shard_map/ppermute | solution.py:684
  30.5 1.8 %collective-permute-start.9 = (f32[32,128]{1,0:T(8,128)S(1)}, f32[32,128]{1,0:T(8,128)S(1)}, u32[]{:S(2)}, u32[]{:S(2)}) collective-permute-start(f32[32,128]{1,0:T(8,128)S(1)} %add.20), channel_id=1, source_target_pairs={{0,3},{1,2},{2,1},{3,0},{4,7},{5,6},{6,5},{7,4},{8,11},{9,10},{10,... | collective-permute-start | bytes 49160 | tf_op jit(solution)/shard_map/ppermute | solution.py:684
  32.3 3.8 %collective-permute-start.8 = (f32[32,128]{1,0:T(8,128)S(1)}, f32[32,128]{1,0:T(8,128)S(1)}, u32[]{:S(2)}, u32[]{:S(2)}) collective-permute-start(f32[32,128]{1,0:T(8,128)S(1)} %add.20), channel_id=1, source_target_pairs={{0,2},{1,3},{2,0},{3,1},{4,6},{5,7},{6,4},{7,5},{8,10},{9,11},{10,... | collective-permute-start | bytes 49160 | tf_op jit(solution)/shard_map/ppermute | solution.py:684
  36.1 1.0 %collective-permute-start.7 = (f32[32,128]{1,0:T(8,128)S(1)}, f32[32,128]{1,0:T(8,128)S(1)}, u32[]{:S(2)}, u32[]{:S(2)}) collective-permute-start(f32[32,128]{1,0:T(8,128)S(1)} %add.20), channel_id=1, source_target_pairs={{0,1},{1,0},{2,3},{3,2},{4,5},{5,4},{6,7},{7,6},{8,9},{9,8},{10,11... | collective-permute-start | bytes 49160 | tf_op jit(solution)/shard_map/ppermute | solution.py:684
  37.1 0.7 %collective-permute-done.8 = f32[32,128]{1,0:T(8,128)S(1)} collective-permute-done((f32[32,128]{1,0:T(8,128)S(1)}, f32[32,128]{1,0:T(8,128)S(1)}, u32[]{:S(2)}, u32[]{:S(2)}) %collective-permute-start.8) | collective-permute-done | bytes 16416 | tf_op jit(solution)/shard_map/ppermute | solution.py:684
  37.8 2.0 %collective-permute-done.7 = f32[32,128]{1,0:T(8,128)S(1)} collective-permute-done((f32[32,128]{1,0:T(8,128)S(1)}, f32[32,128]{1,0:T(8,128)S(1)}, u32[]{:S(2)}, u32[]{:S(2)}) %collective-permute-start.7) | collective-permute-done | bytes 16416 | tf_op jit(solution)/shard_map/ppermute | solution.py:684
  39.9 1.5 %last_kernel.1 = (f32[9,128,256]{2,1,0:T(8,128)}, f32[2,6]{1,0:T(2,128)}, f32[128,256]{1,0:T(8,128)}) custom-call(f32[32,128]{1,0:T(8,128)S(1)} %add_add_fusion.message, f32[9,128,256]{2,1,0:T(8,128)S(1)} %copy-done, f32[3,9,160,128]{3,2,1,0:T(8,128)S(1)} %get-tuple-element.45.direction, f32[3,9,160,128]{3,2,1,0:T(8,128)S(1)} %get-tuple-element.46.part, ...), custom_call_target="tpu_custom_call" | custom-call | tf_op jit(solution)/shard_map/last_kernel/pallas_call | solution.py:715
  (24 shorter events, 0.1 us)
Async XLA Ops:
  0.6 2.7 %copy-start.3 = (f32[128,256]{1,0:T(8,128)S(1)}, f32[128,256]{1,0:T(8,128)}, u32[]{:S(2)}) copy-start(f32[128,256]{1,0:T(8,128)} %vert_in.3) | copy-start | bytes 393220
  0.6 2.7 %copy-start.2 = (f32[128,256]{1,0:T(8,128)S(1)}, f32[128,256]{1,0:T(8,128)}, u32[]{:S(2)}) copy-start(f32[128,256]{1,0:T(8,128)} %horiz_in.3) | copy-start | bytes 393220
  0.7 2.7 %copy-start = (f32[9,128,256]{2,1,0:T(8,128)S(1)}, f32[9,128,256]{2,1,0:T(8,128)}, u32[]{:S(2)}) copy-start(f32[9,128,256]{2,1,0:T(8,128)} %phi.7) | copy-start | bytes 3538948
  0.7 2.7 %copy-start.1 = (f32[9,128,256]{2,1,0:T(8,128)S(1)}, f32[9,128,256]{2,1,0:T(8,128)}, u32[]{:S(2)}) copy-start(f32[9,128,256]{2,1,0:T(8,128)} %forcing.3) | copy-start | bytes 3538948
  0.7 2.7 %copy-start.7 = (f32[6,2]{0,1:T(2,128)S(1)}, f32[6,2]{0,1:T(2,128)}, u32[]{:S(2)}) copy-start(f32[6,2]{0,1:T(2,128)} %param.17) | copy-start | bytes 148
  0.7 2.7 %copy-start.6 = (f32[6,6,2]{1,2,0:T(2,128)S(1)}, f32[6,6,2]{1,2,0:T(2,128)}, u32[]{:S(2)}) copy-start(f32[6,6,2]{1,2,0:T(2,128)} %param.16) | copy-start | bytes 868
  2.1 3.7 %collective-permute-start = (f32[10,8,256]{2,1,0:T(8,128)S(1)}, f32[10,8,256]{2,1,0:T(8,128)S(1)}, u32[]{:S(2)}, u32[]{:S(2)}) collective-permute-start(f32[10,8,256]{2,1,0:T(8,128)S(1)} %get-tuple-element.28), channel_id=1, source_target_pairs={{0,4},{4,0},{8,12},{12,8},{16,20},{20,16},{24,28},{28,24},{1,5},{5... | collective-permute-start | bytes 245768 | tf_op jit(solution)/shard_map/ppermute | solution.py:667
  2.6 3.2 %collective-permute-start.1 = (f32[10,8,256]{2,1,0:T(8,128)S(1)}, f32[10,8,256]{2,1,0:T(8,128)S(1)}, u32[]{:S(2)}, u32[]{:S(2)}) collective-permute-start(f32[10,8,256]{2,1,0:T(8,128)S(1)} %get-tuple-element.29), channel_id=1, source_target_pairs={{4,8},{12,16},{20,24},{8,4},{16,12},{24,20},{5,9},{13,17},{21,25},... | collective-permute-start | bytes 245768 | tf_op jit(solution)/shard_map/ppermute | solution.py:673
  5.8 3.7 %copy-start.4 = (f32[6,128,256]{2,1,0:T(8,128)S(1)}, f32[6,128,256]{2,1,0:T(8,128)}, u32[]{:S(2)}) copy-start(f32[6,128,256]{2,1,0:T(8,128)} %modes.1) | copy-start | bytes 2359300
  5.8 3.7 %copy-start.5 = (f32[9,9]{1,0:T(8,128)S(1)}, f32[9,9]{1,0:T(8,128)}, u32[]{:S(2)}) copy-start(f32[9,9]{1,0:T(8,128)} %mix.3) | copy-start | bytes 976
  5.8 3.7 %copy-start.8 = (s32[128,2]{0,1:T(2,128)S(1)}, s32[128,2]{0,1:T(2,128)}, u32[]{:S(2)}) copy-start(s32[128,2]{0,1:T(2,128)} %param.15) | copy-start | bytes 3076
  6.2 5.5 %collective-permute-start.2 = (f32[72,128]{1,0:T(8,128)S(1)}, f32[72,128]{1,0:T(8,128)S(1)}, u32[]{:S(2)}, u32[]{:S(2)}) collective-permute-start(f32[72,128]{1,0:T(8,128)S(1)} %get-tuple-element.39), channel_id=1, source_target_pairs={{0,1},{1,0},{2,3},{3,2},{4,5},{5,4},{6,7},{7,6},{8,9},{9,8},{10,11... | collective-permute-start | bytes 110600 | tf_op jit(solution)/shard_map/ppermute | solution.py:667
  8.8 2.9 %collective-permute-start.3 = (f32[72,128]{1,0:T(8,128)S(1)}, f32[72,128]{1,0:T(8,128)S(1)}, u32[]{:S(2)}, u32[]{:S(2)}) collective-permute-start(f32[72,128]{1,0:T(8,128)S(1)} %get-tuple-element.40), channel_id=1, source_target_pairs={{1,2},{2,1},{5,6},{6,5},{9,10},{10,9},{13,14},{14,13},{17,18},{18,... | collective-permute-start | bytes 110600 | tf_op jit(solution)/shard_map/ppermute | solution.py:673
  18.5 3.6 %collective-permute-start.4 = (f32[32,128]{1,0:T(8,128)S(1)}, f32[32,128]{1,0:T(8,128)S(1)}, u32[]{:S(2)}, u32[]{:S(2)}) collective-permute-start(f32[32,128]{1,0:T(8,128)S(1)} %get-tuple-element.44), channel_id=1, source_target_pairs={{0,4},{4,0},{8,12},{12,8},{16,20},{20,16},{24,28},{28,24},{1,5},{5... | collective-permute-start | bytes 49160 | tf_op jit(solution)/shard_map/ppermute | solution.py:684
  22.1 3.7 %collective-permute-start.5 = (f32[32,128]{1,0:T(8,128)S(1)}, f32[32,128]{1,0:T(8,128)S(1)}, u32[]{:S(2)}, u32[]{:S(2)}) collective-permute-start(f32[32,128]{1,0:T(8,128)S(1)} %add.18), channel_id=1, source_target_pairs={{0,8},{4,12},{8,0},{12,4},{16,24},{20,28},{24,16},{28,20},{1,9},{5... | collective-permute-start | bytes 49160 | tf_op jit(solution)/shard_map/ppermute | solution.py:684
  25.9 4.6 %collective-permute-start.6 = (f32[32,128]{1,0:T(8,128)S(1)}, f32[32,128]{1,0:T(8,128)S(1)}, u32[]{:S(2)}, u32[]{:S(2)}) collective-permute-start(f32[32,128]{1,0:T(8,128)S(1)} %add.19), channel_id=1, source_target_pairs={{0,16},{4,20},{8,24},{12,28},{16,0},{20,4},{24,8},{28,12},{1,17},{... | collective-permute-start | bytes 49160 | tf_op jit(solution)/shard_map/ppermute | solution.py:684
  30.5 6.6 %collective-permute-start.9 = (f32[32,128]{1,0:T(8,128)S(1)}, f32[32,128]{1,0:T(8,128)S(1)}, u32[]{:S(2)}, u32[]{:S(2)}) collective-permute-start(f32[32,128]{1,0:T(8,128)S(1)} %add.20), channel_id=1, source_target_pairs={{0,3},{1,2},{2,1},{3,0},{4,7},{5,6},{6,5},{7,4},{8,11},{9,10},{10,... | collective-permute-start | bytes 49160 | tf_op jit(solution)/shard_map/ppermute | solution.py:684
  32.3 5.5 %collective-permute-start.8 = (f32[32,128]{1,0:T(8,128)S(1)}, f32[32,128]{1,0:T(8,128)S(1)}, u32[]{:S(2)}, u32[]{:S(2)}) collective-permute-start(f32[32,128]{1,0:T(8,128)S(1)} %add.20), channel_id=1, source_target_pairs={{0,2},{1,3},{2,0},{3,1},{4,6},{5,7},{6,4},{7,5},{8,10},{9,11},{10,... | collective-permute-start | bytes 49160 | tf_op jit(solution)/shard_map/ppermute | solution.py:684
  36.1 3.7 %collective-permute-start.7 = (f32[32,128]{1,0:T(8,128)S(1)}, f32[32,128]{1,0:T(8,128)S(1)}, u32[]{:S(2)}, u32[]{:S(2)}) collective-permute-start(f32[32,128]{1,0:T(8,128)S(1)} %add.20), channel_id=1, source_target_pairs={{0,1},{1,0},{2,3},{3,2},{4,5},{5,4},{6,7},{7,6},{8,9},{9,8},{10,11... | collective-permute-start | bytes 49160 | tf_op jit(solution)/shard_map/ppermute | solution.py:684
